TPU v7x, 32 devices: a whole 2x2x4 slice. The times are simulated.
32 devices in a mesh: dp: 16 (over z, y, x), seq: 2 (over core).
Axes of the slice: x: 2, y: 2, z: 4, core: 2. Of those that a mesh axis runs over, the one named last changes fastest.
Arguments:
- patches: bfloat16 [48, 1024, 512], P('dp', 'seq'), may hold values from -6 to 6
- text_rows: bfloat16 [48, 77, 512], P('dp'), may hold values from -6 to 6
- lengths: int32 [48], P('dp'), may hold values from 5 to 77, as said below
- first_gain: bfloat16 [512], P(('dp', 'seq')), may hold values from 0.099609375 to 1.8984375
- first_shift: bfloat16 [512], P(('dp', 'seq')), may hold values from -3 to 3
- in_weight: bfloat16 [512, 1536], P(('dp', 'seq')), may hold values from -0.25 to 0.25
- query_bias: bfloat16 [512], P(('dp', 'seq')), may hold values from -3 to 3
- value_bias: bfloat16 [512], P(('dp', 'seq')), may hold values from -0.1796875 to 0.1796875
- out_weight: bfloat16 [512, 512], P(('dp', 'seq')), may hold values from -0.5 to 0.5
- branch_bias: bfloat16 [512], P(('dp', 'seq')), may hold values from -3 to 3
- second_gain: bfloat16 [512], P(('dp', 'seq')), may hold values from 0.099609375 to 1.8984375
- second_shift: bfloat16 [512], P(('dp', 'seq')), may hold values from -3 to 3
- up_weight: bfloat16 [512, 2048], P(('dp', 'seq')), may hold values from -0.25 to 0.25
- up_bias: bfloat16 [2048], P(('dp', 'seq')), may hold values from -3 to 3
- down_weight: bfloat16 [2048, 512], P(('dp', 'seq')), may hold values from -0.125 to 0.125
- down_bias: bfloat16 [512], P(('dp', 'seq')), may hold values from -3 to 3
- patch_cotangent: bfloat16 [48, 1024, 512], P('dp', 'seq'), may hold values from -6 to 6
- text_cotangent: bfloat16 [48, 77, 512], P('dp'), may hold values from -6 to 6
Outputs:
- out_patches: bfloat16 [48, 1024, 512], P('dp', 'seq')
- out_text: bfloat16 [48, 77, 512], P('dp')
- grad_patches: bfloat16 [48, 1024, 512], P('dp', 'seq')
- grad_text: bfloat16 [48, 77, 512], P('dp')
- first_gain_grad: float32 [512], P(('dp', 'seq'))
- first_shift_grad: float32 [512], P(('dp', 'seq'))
- in_weight_grad: float32 [512, 1536], P(('dp', 'seq'))
- query_bias_grad: float32 [512], P(('dp', 'seq'))
- value_bias_grad: float32 [512], P(('dp', 'seq'))
- out_weight_grad: float32 [512, 512], P(('dp', 'seq'))
- branch_bias_grad: float32 [512], P(('dp', 'seq'))
- second_gain_grad: float32 [512], P(('dp', 'seq'))
- second_shift_grad: float32 [512], P(('dp', 'seq'))
- up_weight_grad: float32 [512, 2048], P(('dp', 'seq'))
- up_bias_grad: float32 [2048], P(('dp', 'seq'))
- down_weight_grad: float32 [2048, 512], P(('dp', 'seq'))
- down_bias_grad: float32 [512], P(('dp', 'seq'))
Inputs may be any that keep to these rules, and one draw needn't show every extreme that they name: `lengths`: in every draw one item uses all 77 language slots and another uses 5.
All inputs are finite; a program needn't handle non-finite values.
Results may differ from a plain program's by a relative error of at most 0.014.
Values may be sent and summed in bfloat16 or wider, within the bound.
A program may use at most 192 MiB of HBM per device.

v0:
```python
from functools import partial
import math

import jax
import jax.numpy as jnp
from jax import lax
from jax.sharding import PartitionSpec as P

HEADS = 8


EPSILON = 1e-05
NEG_FILL = -1e30


def project(left_side, right_side):
    return jnp.einsum("ird,df->irf", left_side, right_side, preferred_element_type=jnp.float32)


def project_back(grad_rows, right_side):
    return jnp.einsum("irf,df->ird", grad_rows, right_side, preferred_element_type=jnp.float32)


def outer_sum(left_side, grad_rows):
    return jnp.einsum("ird,irf->df", left_side, grad_rows, preferred_element_type=jnp.float32)


def column_sum(grad_rows):
    return jnp.sum(grad_rows.astype(jnp.float32), axis=(0, 1))


def norm_rows(token_rows, gain_vec, shift_vec):
    row_mean = jnp.mean(token_rows, axis=-1, keepdims=True)
    centred = token_rows - row_mean
    inverse = lax.rsqrt(jnp.mean(centred * centred, axis=-1, keepdims=True) + EPSILON)
    scaled = centred * inverse
    return (scaled * gain_vec + shift_vec, scaled, inverse)


def norm_back(grad_rows, scaled, inverse, gain_vec, row_weight):
    gain_grad = jnp.sum(grad_rows * scaled * row_weight, axis=(0, 1))
    shift_grad = jnp.sum(grad_rows * row_weight, axis=(0, 1))
    row_inner = grad_rows * gain_vec
    rows_grad = inverse * (
        row_inner
        - jnp.mean(row_inner, axis=-1, keepdims=True)
        - scaled * jnp.mean(row_inner * scaled, axis=-1, keepdims=True)
    )
    return (rows_grad, gain_grad, shift_grad)


def head_slice(block, head_index, head_size):
    return lax.dynamic_slice_in_dim(block, head_index * head_size, head_size, 2)


def head_scores(queries, key_rows, key_valid, head_index, head_size):
    score_scale = 1.0 / math.sqrt(head_size)
    scores = (
        jnp.einsum(
            "iqe,ike->iqk",
            head_slice(queries, head_index, head_size),
            head_slice(key_rows, head_index, head_size),
            preferred_element_type=jnp.float32,
        )
        * score_scale
    )
    return jnp.where(key_valid[:, None, :], scores, NEG_FILL)


def merge_heads(stacked):
    head_count, item_count, row_count, head_size = stacked.shape
    return jnp.transpose(stacked, (1, 2, 0, 3)).reshape(
        item_count, row_count, head_count * head_size
    )


def attend(queries, key_rows, values, key_valid, head_count):
    head_size = queries.shape[-1] // head_count

    def one_head(head_index):
        scores = head_scores(queries, key_rows, key_valid, head_index, head_size)
        row_max = jnp.max(scores, axis=-1, keepdims=True)
        powers = jnp.exp(scores - row_max)
        row_total = jnp.sum(powers, axis=-1, keepdims=True)
        probs = (powers / row_total).astype(jnp.bfloat16)
        head_out = jnp.einsum(
            "iqk,ike->iqe",
            probs,
            head_slice(values, head_index, head_size),
            preferred_element_type=jnp.float32,
        )
        return (head_out, row_max[..., 0] + jnp.log(row_total[..., 0]))

    head_outs, log_totals = lax.map(one_head, jnp.arange(head_count))
    return (merge_heads(head_outs).astype(jnp.bfloat16), log_totals)


def attend_back(
    queries, key_rows, values, key_valid, log_totals, grad_att, query_weight, head_count
):
    head_size = queries.shape[-1] // head_count
    score_scale = 1.0 / math.sqrt(head_size)

    def one_head(head_index):
        scores = head_scores(queries, key_rows, key_valid, head_index, head_size)
        probs = jnp.exp(scores - log_totals[head_index][..., None])
        grad_out = head_slice(grad_att, head_index, head_size)
        grad_probs = jnp.einsum(
            "iqe,ike->iqk",
            grad_out,
            head_slice(values, head_index, head_size),
            preferred_element_type=jnp.float32,
        )
        row_inner = jnp.sum(probs * grad_probs, axis=-1, keepdims=True)
        grad_scores = (probs * (grad_probs - row_inner)).astype(jnp.bfloat16)
        grad_query = (
            jnp.einsum(
                "iqk,ike->iqe",
                grad_scores,
                head_slice(key_rows, head_index, head_size),
                preferred_element_type=jnp.float32,
            )
            * score_scale
        )
        kept_scores = grad_scores * query_weight
        kept_probs = probs.astype(jnp.bfloat16) * query_weight
        grad_key = (
            jnp.einsum(
                "iqk,iqe->ike",
                kept_scores,
                head_slice(queries, head_index, head_size),
                preferred_element_type=jnp.float32,
            )
            * score_scale
        )
        grad_value = jnp.einsum(
            "iqk,iqe->ike", kept_probs, grad_out, preferred_element_type=jnp.float32
        )
        return (grad_query, grad_key, grad_value, row_inner[..., 0])

    grad_query, grad_key, grad_value, inner_rows = lax.map(one_head, jnp.arange(head_count))
    return (merge_heads(grad_query), merge_heads(grad_key), merge_heads(grad_value), inner_rows)


def forward(gathered, token_rows, text_valid, head_count, text_count, pair_gather):
    (
        gain_one,
        shift_one,
        in_full,
        query_full,
        value_full,
        out_full,
        branch_full,
        gain_two,
        shift_two,
        up_full,
        up_bias_full,
        down_full,
        down_bias_full,
    ) = gathered
    model_width = token_rows.shape[-1]
    local_rows = token_rows.shape[1] - text_count
    item_count = token_rows.shape[0]
    normed_one, scaled_one, inverse_one = norm_rows(
        token_rows, gain_one.astype(jnp.float32), shift_one.astype(jnp.float32)
    )
    first_in = normed_one.astype(jnp.bfloat16)
    projected = project(first_in, in_full)
    queries = (projected[..., :model_width] + query_full.astype(jnp.float32)).astype(jnp.bfloat16)
    key_rows = projected[..., model_width : 2 * model_width].astype(jnp.bfloat16)
    values = (projected[..., 2 * model_width :] + value_full.astype(jnp.float32)).astype(
        jnp.bfloat16
    )
    patch_keys, patch_values = pair_gather(key_rows[:, :local_rows], values[:, :local_rows])
    all_keys = jnp.concatenate([patch_keys, key_rows[:, local_rows:]], axis=1)
    all_values = jnp.concatenate([patch_values, values[:, local_rows:]], axis=1)
    key_valid = jnp.concatenate(
        [jnp.ones((item_count, patch_keys.shape[1]), jnp.bool_), text_valid], axis=1
    )
    attended, log_totals = attend(queries, all_keys, all_values, key_valid, head_count)
    middle = token_rows + (project(attended, out_full) + branch_full.astype(jnp.float32))
    normed_two, scaled_two, inverse_two = norm_rows(
        middle, gain_two.astype(jnp.float32), shift_two.astype(jnp.float32)
    )
    second_in = normed_two.astype(jnp.bfloat16)
    hidden_pre = project(second_in, up_full) + up_bias_full.astype(jnp.float32)
    hidden = jax.nn.gelu(hidden_pre, approximate=False).astype(jnp.bfloat16)
    result = middle + project(hidden, down_full) + down_bias_full.astype(jnp.float32)
    stored = (
        first_in,
        scaled_one,
        inverse_one,
        queries,
        all_keys,
        all_values,
        key_valid,
        log_totals,
        attended,
        scaled_two,
        inverse_two,
        second_in,
        hidden_pre,
        hidden,
    )
    return (result, stored)


def per_device(
    patches,
    text_rows,
    lengths,
    first_gain,
    first_shift,
    in_weight,
    query_bias,
    value_bias,
    out_weight,
    branch_bias,
    second_gain,
    second_shift,
    up_weight,
    up_bias,
    down_weight,
    down_bias,
    patch_cotangent,
    text_cotangent,
):
    local_rows = patches.shape[1]
    item_count = patches.shape[0]
    text_count = text_rows.shape[1]
    gathered = (
        lax.all_gather(first_gain, ("dp", "seq"), axis=0, tiled=True),
        lax.all_gather(first_shift, ("dp", "seq"), axis=0, tiled=True),
        lax.all_gather(in_weight, ("dp", "seq"), axis=0, tiled=True),
        lax.all_gather(query_bias, ("dp", "seq"), axis=0, tiled=True),
        lax.all_gather(value_bias, ("dp", "seq"), axis=0, tiled=True),
        lax.all_gather(out_weight, ("dp", "seq"), axis=0, tiled=True),
        lax.all_gather(branch_bias, ("dp", "seq"), axis=0, tiled=True),
        lax.all_gather(second_gain, ("dp", "seq"), axis=0, tiled=True),
        lax.all_gather(second_shift, ("dp", "seq"), axis=0, tiled=True),
        lax.all_gather(up_weight, ("dp", "seq"), axis=0, tiled=True),
        lax.all_gather(up_bias, ("dp", "seq"), axis=0, tiled=True),
        lax.all_gather(down_weight, ("dp", "seq"), axis=0, tiled=True),
        lax.all_gather(down_bias, ("dp", "seq"), axis=0, tiled=True),
    )
    token_rows = jnp.concatenate([patches, text_rows], axis=1).astype(jnp.float32)
    text_valid = jnp.arange(text_count)[None, :] < lengths[:, None]
    lead_device = jnp.where(lax.axis_index("seq") == 0, 1.0, 0.0).astype(jnp.float32)
    row_weight = jnp.concatenate(
        [
            jnp.ones((item_count, local_rows, 1), jnp.float32),
            jnp.broadcast_to(lead_device, (item_count, text_count, 1)),
        ],
        axis=1,
    )
    weight_low = row_weight.astype(jnp.bfloat16)
    result, stored = forward(
        gathered,
        token_rows,
        text_valid,
        HEADS,
        text_count,
        lambda key_part, value_part: (
            lax.all_gather(key_part, "seq", axis=1, tiled=True),
            lax.all_gather(value_part, "seq", axis=1, tiled=True),
        ),
    )
    (
        first_in,
        scaled_one,
        inverse_one,
        queries,
        all_keys,
        all_values,
        key_valid,
        log_totals,
        attended,
        scaled_two,
        inverse_two,
        second_in,
        hidden_pre,
        hidden,
    ) = stored
    (
        gain_one,
        shift_one,
        in_full,
        query_full,
        value_full,
        out_full,
        branch_full,
        gain_two,
        shift_two,
        up_full,
        up_bias_full,
        down_full,
        down_bias_full,
    ) = gathered
    grad_result = jnp.concatenate([patch_cotangent, text_cotangent], axis=1)
    result_kept = grad_result * weight_low
    down_grad = outer_sum(hidden, result_kept)
    down_bias_grad = column_sum(result_kept)
    grad_hidden = project_back(grad_result, down_full)
    unused_value, gelu_back = jax.vjp(partial(jax.nn.gelu, approximate=False), hidden_pre)
    grad_pre = gelu_back(grad_hidden)[0].astype(jnp.bfloat16)
    pre_kept = grad_pre * weight_low
    up_grad = outer_sum(second_in, pre_kept)
    up_bias_grad = column_sum(pre_kept)
    grad_second = project_back(grad_pre, up_full)
    grad_middle, second_gain_grad, second_shift_grad = norm_back(
        grad_second, scaled_two, inverse_two, gain_two.astype(jnp.float32), row_weight
    )
    grad_middle = grad_middle + grad_result.astype(jnp.float32)
    grad_branch = grad_middle.astype(jnp.bfloat16)
    branch_kept = grad_branch * weight_low
    out_grad = outer_sum(attended, branch_kept)
    branch_bias_grad = column_sum(branch_kept)
    grad_att = project_back(grad_branch, out_full).astype(jnp.bfloat16)
    patch_span = all_keys.shape[1] - text_count
    grad_queries, grad_keys, grad_values, inner_rows = attend_back(
        queries, all_keys, all_values, key_valid, log_totals, grad_att, weight_low, HEADS
    )
    key_sum, value_sum = (
        lax.psum_scatter(grad_keys[:, :patch_span], "seq", scatter_dimension=1, tiled=True),
        lax.psum_scatter(grad_values[:, :patch_span], "seq", scatter_dimension=1, tiled=True),
    )
    text_key_part = grad_keys[:, patch_span:]
    text_value_part = grad_values[:, patch_span:]
    key_text, value_text = lax.psum((text_key_part, text_value_part), "seq")
    grad_mixed = jnp.concatenate(
        [
            grad_queries.astype(jnp.bfloat16),
            jnp.concatenate([key_sum, key_text], axis=1).astype(jnp.bfloat16),
            jnp.concatenate([value_sum, value_text], axis=1).astype(jnp.bfloat16),
        ],
        axis=-1,
    )
    mixed_kept = grad_mixed * weight_low
    model_width = patches.shape[-1]
    in_grad = outer_sum(first_in, mixed_kept)
    query_bias_grad = column_sum(mixed_kept[..., :model_width])
    value_bias_grad = column_sum(mixed_kept[..., 2 * model_width :])
    grad_first = project_back(grad_mixed, in_full)
    grad_inputs, first_gain_grad, first_shift_grad = norm_back(
        grad_first, scaled_one, inverse_one, gain_one.astype(jnp.float32), row_weight
    )
    grad_inputs = (grad_inputs + grad_middle).astype(jnp.bfloat16)
    summed = (
        lax.psum_scatter(first_gain_grad, ("dp", "seq"), scatter_dimension=0, tiled=True),
        lax.psum_scatter(first_shift_grad, ("dp", "seq"), scatter_dimension=0, tiled=True),
        lax.psum_scatter(in_grad, ("dp", "seq"), scatter_dimension=0, tiled=True),
        lax.psum_scatter(query_bias_grad, ("dp", "seq"), scatter_dimension=0, tiled=True),
        lax.psum_scatter(value_bias_grad, ("dp", "seq"), scatter_dimension=0, tiled=True),
        lax.psum_scatter(out_grad, ("dp", "seq"), scatter_dimension=0, tiled=True),
        lax.psum_scatter(branch_bias_grad, ("dp", "seq"), scatter_dimension=0, tiled=True),
        lax.psum_scatter(second_gain_grad, ("dp", "seq"), scatter_dimension=0, tiled=True),
        lax.psum_scatter(second_shift_grad, ("dp", "seq"), scatter_dimension=0, tiled=True),
        lax.psum_scatter(up_grad, ("dp", "seq"), scatter_dimension=0, tiled=True),
        lax.psum_scatter(up_bias_grad, ("dp", "seq"), scatter_dimension=0, tiled=True),
        lax.psum_scatter(down_grad, ("dp", "seq"), scatter_dimension=0, tiled=True),
        lax.psum_scatter(down_bias_grad, ("dp", "seq"), scatter_dimension=0, tiled=True),
    )
    out_rows = result.astype(jnp.bfloat16)
    return (
        out_rows[:, :local_rows],
        out_rows[:, local_rows:],
        grad_inputs[:, :local_rows],
        grad_inputs[:, local_rows:],
        summed[0],
        summed[1],
        summed[2],
        summed[3],
        summed[4],
        summed[5],
        summed[6],
        summed[7],
        summed[8],
        summed[9],
        summed[10],
        summed[11],
        summed[12],
    )


def solution(mesh):
    placed = (
        P("dp", "seq", None),
        P("dp", None, None),
        P("dp"),
        P(("dp", "seq")),
        P(("dp", "seq")),
        P(("dp", "seq"), None),
        P(("dp", "seq")),
        P(("dp", "seq")),
        P(("dp", "seq"), None),
        P(("dp", "seq")),
        P(("dp", "seq")),
        P(("dp", "seq")),
        P(("dp", "seq"), None),
        P(("dp", "seq")),
        P(("dp", "seq"), None),
        P(("dp", "seq")),
        P("dp", "seq", None),
        P("dp", None, None),
    )
    return jax.shard_map(
        per_device,
        mesh=mesh,
        in_specs=placed,
        out_specs=(
            P("dp", "seq", None),
            P("dp", None, None),
            P("dp", "seq", None),
            P("dp", None, None),
            P(("dp", "seq")),
            P(("dp", "seq")),
            P(("dp", "seq"), None),
            P(("dp", "seq")),
            P(("dp", "seq")),
            P(("dp", "seq"), None),
            P(("dp", "seq")),
            P(("dp", "seq")),
            P(("dp", "seq")),
            P(("dp", "seq"), None),
            P(("dp", "seq")),
            P(("dp", "seq"), None),
            P(("dp", "seq")),
        ),
        check_vma=False,
    )
```

profile of v0, /device:TPU:0, one launch (start us, length us, event | category | flops | bytes accessed | tf_op | source)
XLA Modules:
  0.0 1120.7 jit_solution(443346942526769553)
XLA Ops:
  15.7 42.3 %all-reduce.22 = (bf16[512]{0:T(512)(128)(2,1)S(1)}, bf16[512]{0:T(512)(128)(2,1)S(1)}, bf16[512]{0:T(512)(128)(2,1)S(1)}, bf16[512]{0:T(512)(128)(2,1)S(1)}, bf...) all-reduce(bf16[512]{0:T(512)(128)(2,1)S(1)} %dynamic-update-slice., ...), channel_id=1, replica_groups=mesh['dp'=16,'seq'=2] {'dp','seq'}, use_global_device_ids=true, to_apply=%add.3 | all-reduce | flops 6144 | bytes 24576
  68.6 7.3 fusion.112
  85.0 44.0 %all_gather.52 = bf16[512,512]{1,0:T(8,128)(2,1)} all-gather(bf16[16,512]{1,0:T(8,128)(2,1)S(1)} %copy-done.48), channel_id=1, replica_groups=mesh['dp'=16,'seq'=2] {'dp','seq'}, dimensions={0}, use_global_device_ids=true | all-gather | bytes 540672 | tf_op jit(solution)/shard_map/all_gather | solution.py:237
  153.9 85.0 %while.27 = (s32[]{:T(128)}, bf16[8,3,589,64]{2,3,1,0:T(8,128)(2,1)}, f32[8,3,589]{2,1,0:T(4,128)}, pred[3,1101]{1,0:T(4,128)(4,1)S(1)}, s32[8]{0:T(128)}, /*ind...) while((s32[]{:T(128)}, ...), condition=%wide.region_5.6_spmd, body=%wide.region_2.5_spmd.sunk | while | flops 521383392 | bytes 25040776 | solution.py:94
  245.7 13.0 %fusion.80 = (u8[589,2048]{1,0:T(8,128)(4,1)S(1)}, u8[589,2048]{1,0:T(8,128)(4,1)}, f32[3,589,2048]{2,1,0:T(8,128)S(1)}) fusion(f32[2048]{0:T(1024)} %convert_element_type.131, bf16[512,2048]{1,0:T(8,128)(2,1)} %all-gather.12.cloned.1.call-done, f32[3,589,512]{2,1,0:T(8,128)} %copy-done.8, f32[512]{0:T(512)} %convert_element_type.129, ...), kind=kOutput, calls=%fused_computation.112 | convolution fusion | flops 3758441984 | bytes 22630200 | tf_op jit(solution)/shard_map/ird,df->irf/dot_general | solution.py:17
  263.8 35.7 %multiply_convert_fusion.1 = (bf16[3,589,2048]{2,1,0:T(8,128)(2,1)}, f32[3,589,2048]{2,1,0:T(8,128)}) fusion(f32[3,589,2048]{2,1,0:T(8,128)S(1)} %get-tuple-element.303, f32[2048]{0:T(1024)S(1)} %copy-done.45, u8[589,2048]{1,0:T(8,128)(4,1)} %get-tuple-element.217, u8[589,2048]{1,0:T(8,128)(4,1)S(1)} %get-tuple-element.216), kind=kLoop, calls=%fused_computation.59 | loop fusion | flops 256935936 | bytes 38608896 | tf_op jit(solution)/shard_map/convert_element_type | solution.py:187
  299.5 17.8 %convert_reduce_fusion = (f32[2048]{0:T(1024)}, bf16[3,589,2048]{2,1,0:T(8,128)(2,1)}) fusion(bf16[589]{0:T(1024)(128)(2,1)S(1)} %concatenate.46, f32[3,589,2048]{2,1,0:T(8,128)} %get-tuple-element.292, bf16[3,589,512]{2,1,0:T(8,128)(2,1)} %copy-done.12, bf16[2048,512]{1,0:T(8,128)(2,1)} %all-gather.14.cloned.1.call-done, f32[3,589,2048]{2,1,0:T(8,128)} %copy-done.10, ...), kind=kOutput, calls=%fused_computation.57 | convolution fusion | flops 3770804224 | bytes 40112280 | tf_op jit(solution)/shard_map/irf,df->ird/dot_general | solution.py:21
  317.4 11.1 multiply_reduce_fusion.2
  341.3 204.0 %while.28 = (s32[]{:T(128)}, bf16[8,3,589,64]{2,3,1,0:T(8,128)(2,1)}, f32[8,3,1101,64]{2,3,1,0:T(8,128)}, f32[8,3,1101,64]{2,3,1,0:T(8,128)}, pred[3,1101]{1,0:T...) while((s32[]{:T(128)}, ...), condition=%wide.region_12.13_spmd.clone, body=%wide.region_10.12_spmd.clone.sunk | while | flops 1266821760 | bytes 88138840 | solution.py:141
  377.2 6.4 multiply_reduce_fusion.9
  402.7 6.4 multiply_reduce_fusion.9
  453.7 6.4 multiply_reduce_fusion.9
  555.1 6.7 copy.83
  573.6 6.5 copy.85
  587.0 11.2 %fusion.81 = f32[512,2048]{1,0:T(8,128)} fusion(bf16[3,589,2048]{2,1,0:T(8,128)(2,1)} %get-tuple-element.307, bf16[589]{0:T(1024)(128)(2,1)S(1)} %get-tuple-element.563, f32[3,589,512]{2,1,0:T(8,128)} %copy-done.8, f32[512]{0:T(512)S(1)} %copy-done.56, f32[512]{0:T(512)S(1)} %convert_element_type.128, f32[3,589]{1,0:T(4,128)S(1)} %copy-done.42, ...), kind=kOutput, calls=%fused_computation.116 | convolution fusion | flops 3713809920 | bytes 15070162 | tf_op jit(solution)/shard_map/ird,irf->df/dot_general | solution.py:25
  599.7 9.0 convolution_bitcast_fusion
  615.8 6.6 all-reduce.24
  628.3 8.0 broadcast_multiply_fusion
  643.9 8.8 add_convert_fusion.1
  663.4 37.3 %all-reduce.20 = (f32[512]{0:T(512)S(1)}, f32[512]{0:T(512)S(1)}, f32[512]{0:T(512)S(1)}, f32[512]{0:T(512)S(1)}, f32[512]{0:T(512)S(1)}, /*index=5*/f32[512]{0:...) all-reduce(f32[512]{0:T(512)S(1)} %get-tuple-element.220, ...), channel_id=4, replica_groups=mesh['dp'=16,'seq'=2] {'dp','seq'}, use_global_device_ids=true, to_apply=%region_20.21.clone | all-reduce | flops 6144 | bytes 49152
  706.0 23.8 %reduce-scatter.13.cloned.1.call-done = f32[16,512]{1,0:T(8,128)} async-done(((f32[512,512]{1,0:T(8,128)}), f32[16,512]{1,0:T(8,128)}) %reduce-scatter.13.cloned.1.call-update) | async-done | bytes 32784 | tf_op jit(solution)/shard_map/reduce_scatter | solution.py:354
  729.8 139.8 %reduce-scatter.15.cloned.1.call-done = f32[16,2048]{1,0:T(8,128)} async-done(((f32[512,2048]{1,0:T(8,128)}), f32[16,2048]{1,0:T(8,128)}) %reduce-scatter.15.cloned.1.call-update) | async-done | bytes 131088 | tf_op jit(solution)/shard_map/reduce_scatter | solution.py:358
  869.6 139.6 %reduce-scatter.17.cloned.1.call-done = f32[64,512]{1,0:T(8,128)} async-done(((f32[2048,512]{1,0:T(8,128)}), f32[64,512]{1,0:T(8,128)}) %reduce-scatter.17.cloned.1.call-update) | async-done | bytes 131088 | tf_op jit(solution)/shard_map/reduce_scatter | solution.py:360
  1009.2 104.5 %reduce-scatter.11.cloned.1.call-done = f32[16,1536]{1,0:T(8,128)} async-done(((f32[512,1536]{1,0:T(8,128)}), f32[16,1536]{1,0:T(8,128)}) %reduce-scatter.11.cloned.1.call-update) | async-done | bytes 98320 | tf_op jit(solution)/shard_map/reduce_scatter | solution.py:351
  (391 shorter events, 386.9 us)
Async XLA Ops:
  7.2 61.4 %copy-start.4 = (bf16[3,512,512]{2,1,0:T(8,128)(2,1)S(1)}, bf16[3,512,512]{2,1,0:T(8,128)(2,1)}, u32[]{:S(2)}) copy-start(bf16[3,512,512]{2,1,0:T(8,128)(2,1)} %param.22) | copy-start | bytes 4718596
  7.2 61.4 %copy-start.19 = (bf16[3,77,512]{2,1,0:T(8,128)(2,1)S(1)}, bf16[3,77,512]{2,1,0:T(8,128)(2,1)}, u32[]{:S(2)}) copy-start(bf16[3,77,512]{2,1,0:T(8,128)(2,1)} %param.23) | copy-start | bytes 709636
  7.2 61.4 %all-gather.6.cloned.1.call-start = ((), (), s32[]{:S(2)}) async-start(), calls=%async_computation.6 | async-start | bytes 1622016 | tf_op jit(solution)/shard_map/all_gather | solution.py:234
  7.9 129.3 %all-gather.10.cloned.1.call-start = ((), (), s32[]{:S(2)}) async-start(), calls=%async_computation.8 | async-start | bytes 4718592 | tf_op jit(solution)/shard_map/all_gather | solution.py:265
  58.0 18.0 %copy-start.43 = (f32[512]{0:T(512)}, f32[512]{0:T(512)S(1)}, u32[]{:S(2)}) copy-start(f32[512]{0:T(512)S(1)} %convert_element_type.117) | copy-start | bytes 6148
  58.0 17.9 %copy-start.46 = (f32[512]{0:T(512)}, f32[512]{0:T(512)S(1)}, u32[]{:S(2)}) copy-start(f32[512]{0:T(512)S(1)} %convert_element_type.118) | copy-start | bytes 6148
  59.9 16.0 %copy-start.29 = (f32[3,589]{1,0:T(4,128)}, f32[3,589]{1,0:T(4,128)S(1)}, u32[]{:S(2)}) copy-start(f32[3,589]{1,0:T(4,128)S(1)} %broadcast_multiply_fusion.6) | copy-start | bytes 21208
  62.3 13.6 %copy-start.31 = (f32[3,589]{1,0:T(4,128)}, f32[3,589]{1,0:T(4,128)S(1)}, u32[]{:S(2)}) copy-start(f32[3,589]{1,0:T(4,128)S(1)} %add_rsqrt_fusion.1) | copy-start | bytes 21208
  79.6 50.6 %copy-start.28 = (bf16[3,512,512]{2,1,0:T(8,128)(2,1)S(1)}, bf16[3,512,512]{2,1,0:T(8,128)(2,1)}, u32[]{:S(2)}) copy-start(bf16[3,512,512]{2,1,0:T(8,128)(2,1)} %param.38) | copy-start | bytes 4718596
  79.6 63.8 %all-gather.8.cloned.1.call-start = ((), (), s32[]{:S(2)}) async-start(), calls=%async_computation.7 | async-start | bytes 4718592 | tf_op jit(solution)/shard_map/all_gather | solution.py:264
  82.5 163.2 %all-gather.12.cloned.1.call-start = ((), (), s32[]{:S(2)}) async-start(), calls=%async_computation.9 | async-start | bytes 2162688 | tf_op jit(solution)/shard_map/all_gather | solution.py:241
  83.1 216.4 %all-gather.14.cloned.1.call-start = ((), (), s32[]{:S(2)}) async-start(), calls=%async_computation.10 | async-start | bytes 2162688 | tf_op jit(solution)/shard_map/all_gather | solution.py:243
  83.6 538.7 %reduce-scatter.7.cloned.1.call-start = ((), (), s32[]{:S(2)}) async-start(), calls=%async_computation.11 | async-start | bytes 9437184 | tf_op jit(solution)/shard_map/reduce_scatter | solution.py:324
  84.3 46.0 %copy-start.33 = (bf16[3,77,512]{2,1,0:T(8,128)(2,1)S(1)}, bf16[3,77,512]{2,1,0:T(8,128)(2,1)}, u32[]{:S(2)}) copy-start(bf16[3,77,512]{2,1,0:T(8,128)(2,1)} %param.39) | copy-start | bytes 709636
  245.7 18.1 %copy-start.45 = (f32[2048]{0:T(1024)S(1)}, f32[2048]{0:T(1024)}, u32[]{:S(2)}) copy-start(f32[2048]{0:T(1024)} %convert_element_type.131) | copy-start | bytes 24580
  299.5 17.9 %copy-start.39 = (f32[3,589]{1,0:T(4,128)S(1)}, f32[3,589]{1,0:T(4,128)}, u32[]{:S(2)}) copy-start(f32[3,589]{1,0:T(4,128)} %copy-done.38) | copy-start | bytes 21208
  299.5 17.9 %copy-start.41 = (f32[3,589]{1,0:T(4,128)S(1)}, f32[3,589]{1,0:T(4,128)}, u32[]{:S(2)}) copy-start(f32[3,589]{1,0:T(4,128)} %add_rsqrt_fusion) | copy-start | bytes 21208
  299.5 17.9 %copy-start.52 = (f32[589]{0:T(1024)S(1)}, f32[589]{0:T(1024)}, u32[]{:S(2)}) copy-start(f32[589]{0:T(1024)} %concatenate.36) | copy-start | bytes 7072
  317.4 11.1 copy-start.9
  561.8 64.0 %reduce-scatter.9.cloned.1.call-start = ((), (), s32[]{:S(2)}) async-start(), calls=%async_computation.12 | async-start | bytes 9437184 | tf_op jit(solution)/shard_map/reduce_scatter | solution.py:325
  580.2 149.6 %reduce-scatter.13.cloned.1.call-start = ((), (), s32[]{:S(2)}) async-start(), calls=%async_computation.14 | async-start | bytes 1081344 | tf_op jit(solution)/shard_map/reduce_scatter | solution.py:354
  586.7 282.9 %reduce-scatter.15.cloned.1.call-start = ((), (), s32[]{:S(2)}) async-start(), calls=%async_computation.15 | async-start | bytes 4325376 | tf_op jit(solution)/shard_map/reduce_scatter | solution.py:358
  598.2 411.0 %reduce-scatter.17.cloned.1.call-start = ((), (), s32[]{:S(2)}) async-start(), calls=%async_computation.16 | async-start | bytes 4325376 | tf_op jit(solution)/shard_map/reduce_scatter | solution.py:360
  608.7 505.0 %reduce-scatter.11.cloned.1.call-start = ((), (), s32[]{:S(2)}) async-start(), calls=%async_computation.13 | async-start | bytes 3244032 | tf_op jit(solution)/shard_map/reduce_scatter | solution.py:351
  (65 other events, 382.9 us)
Sparse Core Ops, SparseCore 0:
  10.9 57.6 all-gather.5
  79.7 11.2 all-gather.9
  93.1 13.2 all-gather.7
  109.2 57.5 all-gather.11
  169.4 55.2 all-gather.13
  561.9 10.6 reduce-scatter.6
  580.3 10.5 reduce-scatter.8
  593.7 136.0 reduce-scatter.12
  732.7 136.8 reduce-scatter.14
  872.4 136.7 reduce-scatter.16
  1016.1 97.5 reduce-scatter.10
where the time goes:
time: 1130 us; the launch traced here: 1120 us
  waiting for transfers between devices  416 us (37%)
  matrix products  306 us (27%)
  blocking collectives  130 us (12%)
  local copies, waits for them, and re-layouts  128 us (11%)
  other arithmetic  98.4 us (9%)
  loops' own time  26.5 us (2%)
  between operations  15.1 us (1%)
    reduce_scatter x1, waiting for transfers between devices, per_device(): lax.psum_scatter(up_grad, ('dp', 'seq'), scatter_dimension=0, tiled=True)  140 us
    reduce_scatter x1, waiting for transfers between devices, per_device(): lax.psum_scatter(down_grad, ('dp', 'seq'), scatter_dimension=0, tiled=True)  140 us
    reduce_scatter x1, waiting for transfers between devices, per_device(): lax.psum_scatter(in_grad, ('dp', 'seq'), scatter_dimension=0, tiled=True)  105 us
    unnamed x2, blocking collectives  79.7 us
    dot_general x16, matrix products, head_scores(): jnp.einsum('iqe,ike->iqk', head_slice(queries, head_index, head_size), he...  70.5 us
    unnamed x157, local copies, waits for them, and re-layouts  52.6 us
    dot_general x8, matrix products, one_head(): jnp.einsum('iqe,ike->iqk', grad_out, head_slice(values, head_index, head_...  45.5 us
    all_gather x1, blocking collectives, per_device(): lax.all_gather(out_weight, ('dp', 'seq'), axis=0, tiled=True)  44 us
  transfers between devices with their start and end apart: 11, of which 5 were waited for; matrix products, arithmetic and copies ran while one was open for 23% of the time, Pallas kernels for 0%

commit v1 on v0

v1 whole, which is shorter than its diff:
```python
import functools
import math

import jax
import jax.numpy as jnp
from jax import lax
from jax.experimental import pallas as pl
from jax.experimental.pallas import tpu as pltpu
from jax.sharding import PartitionSpec as P

HEADS = 8
EPSILON = 1e-05
NEG_FILL = -1e30
LOG2E = math.log2(math.e)
LN2 = math.log(2.0)
ROW_TILE = 16
LANES = 128
MESH = pl.DeviceIdType.MESH
f32, bf16 = jnp.float32, jnp.bfloat16

GAIN1, SHIFT1, QBIAS, VBIAS, BRANCH, GAIN2, SHIFT2, DOWNB = range(8)


def round_up(value, unit):
    return -(-value // unit) * unit


def mm(a, b):
    return lax.dot_general(a, b, (((1,), (0,)), ((), ())), preferred_element_type=f32)


def mm_t(a, b):
    return lax.dot_general(a, b, (((1,), (1,)), ((), ())), preferred_element_type=f32)


def t_mm(a, b):
    return lax.dot_general(a, b, (((0,), (0,)), ((), ())), preferred_element_type=f32)


def compiler_params(**more):
    return pltpu.CompilerParams(vmem_limit_bytes=60 * 2**20, **more)


WHOLE = pl.BlockSpec(memory_space=pltpu.VMEM)


class Place:
    def __init__(self, depth, seq_size):
        self.depth, self.seq_size = depth, seq_size
        index = lax.axis_index("dp") * seq_size + lax.axis_index("seq")
        self.core = lax.rem(index, 2)
        self.x = lax.rem(index // 2, 2)
        self.y = lax.rem(index // 4, 2)
        self.z = index // 8
        core = self.core
        flip_x, flip_y = 1 - self.x, 1 - self.y
        x_first = self.x * core + flip_x * (1 - core)
        y_first = self.y * (1 - core) + flip_y * core
        x_second = self.x * (1 - core) + flip_x * core
        y_second = self.y * core + flip_y * (1 - core)
        self.columns = (
            (self.y, self.x),
            (y_first, x_first),
            (y_second, x_second),
            (flip_y, flip_x),
        )

    def device(self, z, y, x, core):
        index = ((z * 2 + y) * 2 + x) * 2 + core
        return (index // self.seq_size, lax.rem(index, self.seq_size))

    def layer(self, k):
        return lax.rem(self.z + self.depth - k, self.depth)

    def ahead(self, k):
        return lax.rem(self.z + k, self.depth)

    def first(self):
        return self.device(self.z, *self.columns[1], self.core)

    def second(self):
        return self.device(self.z, *self.columns[2], self.core)

    def other_core(self):
        return self.device(self.z, self.y, self.x, 1 - self.core)

    def above(self, k):
        return self.device(self.ahead(k), self.y, self.x, self.core)

    def greet(self):
        barrier = pltpu.get_barrier_semaphore()
        friends = [self.above(k) for k in range(1, self.depth)]
        friends += [self.first(), self.second(), self.other_core()]
        for friend in friends:
            pl.semaphore_signal(barrier, inc=1, device_id=friend, device_id_type=MESH)
        pl.semaphore_wait(barrier, len(friends))


def remote(src, dst, send, recv, device):
    return pltpu.make_async_remote_copy(
        src_ref=src, dst_ref=dst, send_sem=send, recv_sem=recv, device_id=device, device_id_type=MESH
    )


class Gather:
    def __init__(self, place, shard, full, out, into, local):
        self.place, self.shard, self.full, self.out, self.into, self.local = place, shard, full, out, into, local
        self.sends = []

    def block(self, k, column, core):
        y, x = self.place.columns[column]
        return self.full.at[self.place.layer(k), y, x, core]

    def copy(self, src, dst, lane, k, device):
        return remote(src, dst, self.out.at[lane, k], self.into.at[lane, k], device)

    def send(self, src, dst, lane, k, device):
        copy = self.copy(src, dst, lane, k, device)
        copy.start()
        self.sends.append(copy)

    def arrived(self, lane, k, column, core):
        here = self.block(k, column, core)
        self.copy(here, here, lane, k, self.place.other_core()).wait_recv()
        return here

    def start(self):
        place = self.place
        mine = self.block(0, 0, place.core)
        self.own = pltpu.make_async_copy(self.shard, mine, self.local)
        self.own.start()
        for k in range(1, place.depth):
            self.send(self.shard, mine, 0, k, place.above(k))
        self.forward_line(0)

    def forward_line(self, k):
        place = self.place
        here = self.arrived(0, k, 0, place.core) if k else self.block(0, 0, place.core)
        src = here if k else self.shard
        self.send(src, here, 1, k, place.first())
        self.send(src, here, 2, k, place.second())
        self.send(src, here, 4, k, place.other_core())

    def forward_first(self, k):
        here = self.arrived(1, k, 1, self.place.core)
        self.send(here, here, 3, k, self.place.second())
        self.send(here, here, 5, k, self.place.other_core())

    def forward_second(self, half, k):
        here = self.arrived(2 + half, k, 2 + half, self.place.core)
        self.send(here, here, 6 + half, k, self.place.other_core())

    def finish(self):
        for column in range(4):
            for k in range(self.place.depth):
                self.arrived(4 + column, k, column, 1 - self.place.core)
        self.own.wait()
        for copy in self.sends:
            copy.wait_send()


def gather_sems(depth):
    sems = pltpu.SemaphoreType.DMA
    return [sems((8, depth)), sems((8, depth)), sems]


def gather_kernel(seq_size, arrays, *refs):
    shards, fulls, sems = refs[:arrays], refs[arrays : 2 * arrays], refs[2 * arrays :]
    place = Place(fulls[0].shape[0], seq_size)
    place.greet()
    moves = [Gather(place, shards[n], fulls[n], *sems[3 * n : 3 * n + 3]) for n in range(arrays)]
    for move in moves:
        move.start()
    for k in range(1, place.depth):
        for move in moves:
            move.forward_line(k)
    for k in range(place.depth):
        for move in moves:
            move.forward_first(k)
    for half in range(2):
        for k in range(place.depth):
            for move in moves:
                move.forward_second(half, k)
    for move in moves:
        move.finish()


def gather(shards, devices, seq_size, number):
    depth = devices // 8
    fulls = pl.pallas_call(
        functools.partial(gather_kernel, seq_size, len(shards)),
        out_shape=[jax.ShapeDtypeStruct((depth, 2, 2, 2) + shard.shape, shard.dtype) for shard in shards],
        in_specs=[WHOLE] * len(shards),
        out_specs=[WHOLE] * len(shards),
        scratch_shapes=gather_sems(depth) * len(shards),
        compiler_params=compiler_params(collective_id=number, has_side_effects=True),
        name="gather",
    )(*shards)
    return [full.reshape(-1, full.shape[-1]) for full in fulls]


class Reduce:
    def __init__(self, place, part, total, from_core, held, from_second, pair, from_first, line, from_line, out, into):
        self.place, self.part, self.total = place, part, total
        self.from_core, self.held, self.from_second, self.pair = from_core, held, from_second, pair
        self.from_first, self.line, self.from_line = from_first, line, from_line
        self.out, self.into = out, into

    def copy(self, src, dst, lane, device):
        return remote(src, dst, self.out.at[lane], self.into.at[lane], device)

    def core_copies(self):
        core = self.place.core
        return [self.copy(self.part.at[:, :, :, 1 - core], self.from_core, 0, self.place.other_core())]

    def second_copies(self):
        columns = self.place.columns
        return [
            self.copy(self.held.at[:, columns[2 + k][0], columns[2 + k][1]], self.from_second.at[k], 1 + k,
                      self.place.second())
            for k in range(2)
        ]

    def first_copies(self):
        return [self.copy(self.pair.at[1], self.from_first, 3, self.place.first())]

    def line_copies(self):
        place = self.place
        return [
            self.copy(self.line.at[place.ahead(k)], self.from_line.at[k - 1], 3 + k, place.above(k))
            for k in range(1, place.depth)
        ]

    def start(self, copies):
        for copy in copies:
            copy.start()

    def wait(self, copies):
        for copy in copies:
            copy.wait()

    def add_core(self):
        self.wait(self.core_copies())
        own = self.part[:, :, :, self.place.core]
        self.held[...] = (own.astype(f32) + self.from_core[...].astype(f32)).astype(bf16)

    def add_second(self):
        self.wait(self.second_copies())
        for k in range(2):
            y, x = self.place.columns[k]
            self.pair[k] = (self.held[:, y, x].astype(f32) + self.from_second[k].astype(f32)).astype(bf16)

    def add_first(self):
        self.wait(self.first_copies())
        self.line[...] = (self.pair[0].astype(f32) + self.from_first[...].astype(f32)).astype(bf16)

    def add_line(self):
        self.wait(self.line_copies())
        result = self.line[self.place.z].astype(f32)
        for k in range(self.place.depth - 1):
            result = result + self.from_line[k].astype(f32)
        self.total[...] = result


REDUCE_SCRATCH = 9


def reduce_scratch(depth, rows, cols):
    shapes = [(depth, 2, 2), (depth, 2, 2), (2, depth), (2, depth), (depth,), (depth,), (depth - 1,)]
    sems = pltpu.SemaphoreType.DMA
    return [pltpu.VMEM(shape + (rows, cols), bf16) for shape in shapes] + [sems((3 + depth,))] * 2


def reduce_kernel(seq_size, arrays, *refs):
    parts, totals, scratch = refs[:arrays], refs[arrays : 2 * arrays], refs[2 * arrays :]
    place = Place(parts[0].shape[0], seq_size)
    place.greet()
    sums = [
        Reduce(place, parts[n], totals[n], *scratch[REDUCE_SCRATCH * n : REDUCE_SCRATCH * (n + 1)])
        for n in range(arrays)
    ]
    for one in sums:
        one.start(one.core_copies())
    for one in sums:
        one.add_core()
        one.start(one.second_copies())
    for one in sums:
        one.add_second()
        one.start(one.first_copies())
    for one in sums:
        one.add_first()
        one.start(one.line_copies())
    for one in sums:
        one.add_line()


def reduce(parts, devices, seq_size, number):
    depth = devices // 8
    sizes = [(part.shape[0] // devices, part.shape[1]) for part in parts]
    return pl.pallas_call(
        functools.partial(reduce_kernel, seq_size, len(parts)),
        out_shape=[jax.ShapeDtypeStruct(size, f32) for size in sizes],
        in_specs=[WHOLE] * len(parts),
        out_specs=[WHOLE] * len(parts),
        scratch_shapes=sum([reduce_scratch(depth, *size) for size in sizes], []),
        compiler_params=compiler_params(collective_id=number, has_side_effects=True),
        name="reduce",
    )(*[part.reshape((depth, 2, 2, 2) + size) for part, size in zip(parts, sizes)])


def norm_rows(rows):
    centred = rows - jnp.mean(rows, axis=1, keepdims=True)
    inverse = lax.rsqrt(jnp.mean(centred * centred, axis=1, keepdims=True) + EPSILON)
    return centred * inverse, inverse


def norm_back(grad, scaled, inverse, gain):
    inner = grad * gain
    return inverse * (
        inner
        - jnp.mean(inner, axis=1, keepdims=True)
        - scaled * jnp.mean(inner * scaled, axis=1, keepdims=True)
    )


def gelu_both(v):
    power = jnp.exp2(v * v * (-0.5 * LOG2E))
    base = 1.0 + (0.3275911 / math.sqrt(2.0)) * jnp.abs(v)
    t = pl.reciprocal(base, approx=True)
    t = t * (2.0 - base * t)
    series = 0.5 * 1.061405429
    for factor in (-1.453152027, 1.421413741, -0.284496736, 0.254829592):
        series = series * t + 0.5 * factor
    tail = series * t * power
    cdf = jnp.where(v >= 0, 1.0 - tail, tail)
    return v * cdf, cdf + v * power * (1.0 / math.sqrt(2.0 * math.pi))


def column_sum(rows):
    return jnp.sum(rows.astype(f32), axis=0, keepdims=True)


def to_columns(rows):
    count, width = rows.shape
    return jnp.transpose(jnp.concatenate([rows, jnp.zeros((LANES - count, width), f32)], axis=0)).astype(bf16)


def qkv_kernel(x_ref, w_ref, vec_ref, q_ref, k_ref, v_ref):
    width = x_ref.shape[2]
    scaled, _ = norm_rows(x_ref[0].astype(f32))
    first_in = (scaled * vec_ref[GAIN1 : GAIN1 + 1] + vec_ref[SHIFT1 : SHIFT1 + 1]).astype(bf16)
    scale = LOG2E / math.sqrt(width // HEADS)
    q = mm(first_in, w_ref[:, :width]) + vec_ref[QBIAS : QBIAS + 1]
    q_ref[0] = (q * scale).astype(bf16)
    k_ref[0] = mm(first_in, w_ref[:, width : 2 * width]).astype(bf16)
    v = mm(first_in, w_ref[:, 2 * width : 3 * width]) + vec_ref[VBIAS : VBIAS + 1]
    v_ref[0] = v.astype(bf16)


def qkv(x, weight, vecs):
    block = pl.BlockSpec((1,) + x.shape[1:], lambda i: (i, 0, 0))
    return pl.pallas_call(
        qkv_kernel,
        grid=(x.shape[0],),
        in_specs=[block, WHOLE, WHOLE],
        out_specs=[block] * 3,
        out_shape=[jax.ShapeDtypeStruct(x.shape, bf16)] * 3,
        compiler_params=compiler_params(),
        name="qkv",
    )(x, weight, vecs)


def collect(dst, refs, patch, text):
    count, width = len(refs), refs[0].shape[2]
    for r, ref in enumerate(refs):
        dst[r * patch : (r + 1) * patch, :width] = ref[0, :patch, :]
        at = count * patch + r * text
        dst[at : at + text, :width] = ref[0, patch:, :]
    filled = count * (patch + text)
    if dst.shape[0] > filled:
        dst[filled:, :width] = jnp.zeros((dst.shape[0] - filled, width), dst.dtype)


def attend_kernel(count, patch, head, *refs):
    q_ref, k_refs, v_refs = refs[0], refs[1 : 1 + count], refs[1 + count : 1 + 2 * count]
    bias_ref, out_ref, log_ref, keys, values = refs[1 + 2 * count :]
    width = q_ref.shape[2]
    text = q_ref.shape[1] - patch
    collect(keys, k_refs, patch, text)
    collect(values, v_refs, patch, text)
    values[:, width:] = jnp.ones((values.shape[0], values.shape[1] - width), bf16)
    q = q_ref[0]
    lane = lax.broadcasted_iota(jnp.int32, (1, width), 1) // head
    out = logs = None
    for h in range(width // head):
        q_head = jnp.where(lane == h, q, jnp.zeros_like(q))
        scores = mm_t(q_head, keys[...]) + bias_ref[0]
        top = jnp.max(scores, axis=1, keepdims=True)
        powers = jnp.exp2(scores - top).astype(bf16)
        mixed = mm(powers, values[...])
        total = mixed[:, width:]
        head_out = mixed[:, :width] * (1.0 / total)
        head_log = top + jnp.log2(total)
        out = head_out if out is None else jnp.where(lane == h, head_out, out)
        logs = head_log if logs is None else jnp.where(lane == h, head_log, logs)
    out_ref[0] = out.astype(bf16)
    log_ref[0] = logs


def attend(q, keys, values, bias, patch, head, width):
    items, _, model = q.shape
    count, span = len(keys), bias.shape[-1]
    block = pl.BlockSpec((1, q.shape[1], width), lambda i, p: (i, 0, p))
    return pl.pallas_call(
        functools.partial(attend_kernel, count, patch, head),
        grid=(items, model // width),
        in_specs=[block] * (1 + 2 * count) + [pl.BlockSpec((1, 1, span), lambda i, p: (i, 0, 0))],
        out_specs=[block, block],
        out_shape=[jax.ShapeDtypeStruct(q.shape, bf16), jax.ShapeDtypeStruct(q.shape, f32)],
        scratch_shapes=[pltpu.VMEM((span, width), bf16), pltpu.VMEM((span, 2 * width), bf16)],
        compiler_params=compiler_params(),
        name="attend",
    )(q, *keys, *values, bias)


def attend_back_kernel(count, patch, head, *refs):
    q_ref, k_refs, v_refs = refs[0], refs[1 : 1 + count], refs[1 + count : 1 + 2 * count]
    bias_ref, out_ref, log_ref, grad_ref, dq_ref = refs[1 + 2 * count : 6 + 2 * count]
    dk_refs, dv_refs = refs[6 + 2 * count : 6 + 3 * count], refs[6 + 3 * count : 6 + 4 * count]
    keys, values = refs[6 + 4 * count :]
    width = q_ref.shape[2]
    text = q_ref.shape[1] - patch
    collect(keys, k_refs, patch, text)
    collect(values, v_refs, patch, text)
    q, grad = q_ref[0], grad_ref[0]
    lane = lax.broadcasted_iota(jnp.int32, (1, width), 1) // head
    row = lax.broadcasted_iota(jnp.int32, (width, 1), 0) // head
    inner = grad.astype(f32) * out_ref[0].astype(f32)
    dq = dk = dv = None
    for h in range(width // head):
        mine = lane == h
        q_head = jnp.where(mine, q, jnp.zeros_like(q))
        grad_head = jnp.where(mine, grad, jnp.zeros_like(grad))
        delta = jnp.sum(jnp.where(mine, inner, 0.0), axis=1, keepdims=True)
        scores = mm_t(q_head, keys[...]) + bias_ref[0]
        probs = jnp.exp2(scores - log_ref[0, :, h * head : h * head + 1])
        grad_probs = mm_t(grad_head, values[...])
        grad_scores = (probs * (grad_probs - delta)).astype(bf16)
        dv_head = t_mm(grad, probs.astype(bf16))
        dk_head = t_mm(q, grad_scores)
        dq_head = mm(grad_scores, keys[...])
        dq = dq_head if dq is None else jnp.where(mine, dq_head, dq)
        dk = dk_head if dk is None else jnp.where(row == h, dk_head, dk)
        dv = dv_head if dv is None else jnp.where(row == h, dv_head, dv)
    dq_ref[0] = (dq * (1.0 / math.sqrt(head))).astype(bf16)
    for grads, parts in ((dk * LN2, dk_refs), (dv, dv_refs)):
        grads = jnp.transpose(grads).astype(bf16)
        for r in range(count):
            parts[r][0, :patch, :] = grads[r * patch : (r + 1) * patch]
            at = count * patch + r * text
            parts[r][0, patch:, :] = grads[at : at + text]


def attend_back(q, keys, values, bias, attended, logs, grad_att, patch, head, width):
    items, _, model = q.shape
    count, span = len(keys), bias.shape[-1]
    block = pl.BlockSpec((1, q.shape[1], width), lambda i, p: (i, 0, p))
    grads = pl.pallas_call(
        functools.partial(attend_back_kernel, count, patch, head),
        grid=(items, model // width),
        in_specs=[block] * (1 + 2 * count) + [pl.BlockSpec((1, 1, span), lambda i, p: (i, 0, 0))] + [block] * 3,
        out_specs=[block] * (1 + 2 * count),
        out_shape=[jax.ShapeDtypeStruct(q.shape, bf16)] * (1 + 2 * count),
        scratch_shapes=[pltpu.VMEM((span, width), bf16), pltpu.VMEM((span, width), bf16)],
        compiler_params=compiler_params(),
        name="attend_back",
    )(q, *keys, *values, bias, attended, logs, grad_att)
    return grads[0], grads[1 : 1 + count], grads[1 + count :]


def ffn_kernel(steps, chunk, x_ref, at_ref, dy_ref, w_ref, wd_ref, vec_ref,
               res_ref, gb_ref, ga_ref, part_ref, down_ref, second_s, hidden_s, pre_s, sums_s):
    step = pl.program_id(0)
    block = x_ref.shape[0] // steps
    rows = pl.ds(pl.multiple_of(step * block, ROW_TILE), block)
    model, units = x_ref.shape[1], wd_ref.shape[0]
    gain = vec_ref[GAIN2 : GAIN2 + 1]
    w_out = w_ref[:, units:]
    up_bias = jnp.transpose(wd_ref[:, model:].astype(f32))[:1]
    middle = x_ref[rows, :].astype(f32) + (mm(at_ref[rows, :], w_out) + vec_ref[BRANCH : BRANCH + 1])
    scaled, inverse = norm_rows(middle)
    second_in = (scaled * gain + vec_ref[SHIFT2 : SHIFT2 + 1]).astype(bf16)
    second_s[rows, :] = second_in
    dy = dy_ref[rows, :]
    result = middle + vec_ref[DOWNB : DOWNB + 1]
    grad_second = jnp.zeros_like(middle)
    for c in range(units // chunk):
        cols = slice(c * chunk, (c + 1) * chunk)
        value, slope = gelu_both(mm(second_in, w_ref[:, cols]) + up_bias[:, cols])
        hidden = value.astype(bf16)
        hidden_s[rows, cols] = hidden
        grad_pre = (mm_t(dy, wd_ref[cols, :model]) * slope).astype(bf16)
        pre_s[rows, cols] = grad_pre
        result = result + mm(hidden, wd_ref[cols, :model])
        grad_second = grad_second + mm_t(grad_pre, w_ref[:, cols])
    res_ref[rows, :] = result.astype(bf16)
    grad_branch = (dy.astype(f32) + norm_back(grad_second, scaled, inverse, gain)).astype(bf16)
    gb_ref[rows, :] = grad_branch
    ga_ref[rows, :] = mm_t(grad_branch, w_out).astype(bf16)

    @pl.when(step == 0)
    def _():
        sums_s[...] = jnp.zeros_like(sums_s)

    for at, grad in ((BRANCH, grad_branch), (GAIN2, grad_second * scaled), (SHIFT2, grad_second), (DOWNB, dy)):
        sums_s[at : at + 1, :] += column_sum(grad)

    @pl.when(step == steps - 1)
    def _():
        for c in range(units // model):
            cols = slice(c * model, (c + 1) * model)
            grad_pre = pre_s[:, cols]
            part_ref[:, cols] = t_mm(second_s[...], grad_pre).astype(bf16)
            down_ref[cols, :model] = jnp.transpose(t_mm(dy_ref[...], hidden_s[:, cols])).astype(bf16)
            down_ref[cols, model:] = to_columns(column_sum(grad_pre))
        part_ref[:, units : units + model] = t_mm(at_ref[...], gb_ref[...]).astype(bf16)
        part_ref[:, units + model :] = to_columns(sums_s[...])


def ffn(x, attended, dy, weights, w_down, vecs):
    rows, model = x.shape
    units = w_down.shape[0]
    steps = 3
    return pl.pallas_call(
        functools.partial(ffn_kernel, steps, 512),
        grid=(steps,),
        in_specs=[WHOLE] * 6,
        out_specs=[WHOLE] * 5,
        out_shape=[jax.ShapeDtypeStruct((rows, model), bf16)] * 3
        + [
            jax.ShapeDtypeStruct((model, units + model + LANES), bf16),
            jax.ShapeDtypeStruct((units, model + LANES), bf16),
        ],
        scratch_shapes=[
            pltpu.VMEM((rows, model), bf16),
            pltpu.VMEM((rows, units), bf16),
            pltpu.VMEM((rows, units), bf16),
            pltpu.VMEM((8, model), f32),
        ],
        compiler_params=compiler_params(),
        name="ffn",
    )(x, attended, dy, weights, w_down, vecs)


def in_back_kernel(steps, count, *refs):
    x_ref, gb_ref, w_ref, vec_ref, dq_ref = refs[:5]
    dk_refs, dv_refs = refs[5 : 5 + count], refs[5 + count : 5 + 2 * count]
    grad_ref, part_ref, first_s, mixed_s, sums_s = refs[5 + 2 * count :]
    step = pl.program_id(0)
    block = x_ref.shape[0] // steps
    rows = pl.ds(pl.multiple_of(step * block, ROW_TILE), block)
    model = x_ref.shape[1]
    gain = vec_ref[GAIN1 : GAIN1 + 1]
    scaled, inverse = norm_rows(x_ref[rows, :].astype(f32))
    first_s[rows, :] = (scaled * gain + vec_ref[SHIFT1 : SHIFT1 + 1]).astype(bf16)
    dq = dq_ref[rows, :]
    dk = sum(ref[rows, :].astype(f32) for ref in dk_refs).astype(bf16)
    dv = sum(ref[rows, :].astype(f32) for ref in dv_refs).astype(bf16)
    mixed_s[rows, :model] = dq
    mixed_s[rows, model : 2 * model] = dk
    mixed_s[rows, 2 * model :] = dv
    grad_first = mm_t(mixed_s[rows, :], w_ref[...])
    grad = gb_ref[rows, :].astype(f32) + norm_back(grad_first, scaled, inverse, gain)
    grad_ref[rows, :] = grad.astype(bf16)

    @pl.when(step == 0)
    def _():
        sums_s[...] = jnp.zeros_like(sums_s)

    for at, value in ((GAIN1, grad_first * scaled), (SHIFT1, grad_first), (QBIAS, dq), (VBIAS, dv)):
        sums_s[at : at + 1, :] += column_sum(value)

    @pl.when(step == steps - 1)
    def _():
        for c in range(3):
            cols = slice(c * model, (c + 1) * model)
            part_ref[:, cols] = t_mm(first_s[...], mixed_s[:, cols]).astype(bf16)
        part_ref[:, 3 * model :] = to_columns(sums_s[...])


def in_back(x, grad_branch, weight, vecs, dq, dks, dvs):
    rows, model = x.shape
    count, steps = len(dks), 3
    return pl.pallas_call(
        functools.partial(in_back_kernel, steps, count),
        grid=(steps,),
        in_specs=[WHOLE] * (5 + 2 * count),
        out_specs=[WHOLE] * 2,
        out_shape=[
            jax.ShapeDtypeStruct((rows, model), bf16),
            jax.ShapeDtypeStruct((model, 3 * model + LANES), bf16),
        ],
        scratch_shapes=[
            pltpu.VMEM((rows, model), bf16),
            pltpu.VMEM((rows, 3 * model), bf16),
            pltpu.VMEM((8, model), f32),
        ],
        compiler_params=compiler_params(),
        name="in_back",
    )(x, grad_branch, weight, vecs, dq, *dks, *dvs)


def per_device(
    seq_size,
    devices,
    patches,
    text_rows,
    lengths,
    first_gain,
    first_shift,
    in_weight,
    query_bias,
    value_bias,
    out_weight,
    branch_bias,
    second_gain,
    second_shift,
    up_weight,
    up_bias,
    down_weight,
    down_bias,
    patch_cotangent,
    text_cotangent,
):
    items, patch, model = patches.shape
    slots = text_rows.shape[1]
    units = up_weight.shape[1]
    head = model // HEADS
    width = min(LANES, model)
    share = -(-slots // seq_size)
    text = round_up(share, ROW_TILE)
    seq = lax.axis_index("seq")

    def rows_of(patch_rows, slot_rows):
        padded = jnp.pad(slot_rows, ((0, 0), (0, share * seq_size - slots), (0, 0)))
        mine = lax.dynamic_slice_in_dim(padded, seq * share, share, 1)
        mine = jnp.pad(mine, ((0, 0), (0, text - share), (0, 0)))
        return jnp.concatenate([patch_rows, mine], axis=1)

    def rotate(array, step):
        if step == 0:
            return array
        return lax.ppermute(array, "seq", [((i + step) % seq_size, i) for i in range(seq_size)])

    def rotate_back(array, step):
        if step == 0:
            return array
        return lax.ppermute(array, "seq", [(i, (i + step) % seq_size) for i in range(seq_size)])

    vec_shard = jnp.stack(
        [first_gain, first_shift, query_bias, value_bias, branch_bias, second_gain, second_shift, down_bias], axis=1
    )
    vec_shard = jnp.pad(vec_shard, ((0, 0), (0, LANES - vec_shard.shape[1])))
    (first,) = gather([jnp.concatenate([in_weight, vec_shard], axis=1)], devices, seq_size, 0)
    up_column = jnp.pad(up_bias[:, None], ((0, 0), (0, LANES - 1)))
    weights, w_down = gather(
        [jnp.concatenate([up_weight, out_weight], axis=1), jnp.concatenate([down_weight, up_column], axis=1)],
        devices,
        seq_size,
        1,
    )
    vecs = first[:, 3 * model :].astype(f32).T

    x = rows_of(patches, text_rows)
    dy = rows_of(patch_cotangent, text_cotangent)
    in_full = first[:, : 3 * model]
    q, k, v = qkv(x, in_full, vecs)
    keys = [rotate(k, r) for r in range(seq_size)]
    values = [rotate(v, r) for r in range(seq_size)]

    spans = []
    for r in range(seq_size):
        slot = lax.rem(seq + r, seq_size) * share + jnp.arange(text)
        spans.append((jnp.arange(text) < share)[None, :] & (slot[None, :] < lengths[:, None]))
    valid = jnp.concatenate([jnp.ones((items, patch * seq_size), jnp.bool_)] + spans, axis=1)
    span = round_up(valid.shape[1], LANES)
    valid = jnp.pad(valid, ((0, 0), (0, span - valid.shape[1])))
    bias = jnp.where(valid, 0.0, NEG_FILL).astype(f32)[:, None, :]

    attended, logs = attend(q, keys, values, bias, patch, head, width)
    flat = (items * x.shape[1], model)
    result, grad_branch, grad_att, part, down_part = ffn(
        x.reshape(flat), attended.reshape(flat), dy.reshape(flat), weights, w_down, vecs
    )
    sums, down_sums = reduce([part, down_part], devices, seq_size, 2)
    dq, dks, dvs = attend_back(
        q, keys, values, bias, attended, logs, grad_att.reshape(x.shape), patch, head, width
    )
    dks = [rotate_back(part, r).reshape(flat) for r, part in enumerate(dks)]
    dvs = [rotate_back(part, r).reshape(flat) for r, part in enumerate(dvs)]
    grad_rows, in_part = in_back(x.reshape(flat), grad_branch, in_full, vecs, dq.reshape(flat), dks, dvs)
    (in_sums,) = reduce([in_part], devices, seq_size, 3)

    def split(rows):
        rows = rows.reshape(x.shape)
        own = rows[:, patch : patch + share]
        blocks = [rotate(own, r) for r in range(seq_size)]
        order = jnp.stack(blocks, axis=1)
        order = jnp.roll(order, seq, axis=1)
        return rows[:, :patch], order.reshape(items, -1, model)[:, :slots]

    out_patches, out_text = split(result)
    grad_patches, grad_text = split(grad_rows)
    vec1 = in_sums[:, 3 * model :].T
    vec2 = sums[:, units + model :].T
    return (
        out_patches,
        out_text,
        grad_patches,
        grad_text,
        vec1[GAIN1],
        vec1[SHIFT1],
        in_sums[:, : 3 * model],
        vec1[QBIAS],
        vec1[VBIAS],
        sums[:, units : units + model],
        vec2[BRANCH],
        vec2[GAIN2],
        vec2[SHIFT2],
        sums[:, :units],
        down_sums[:, model],
        down_sums[:, :model],
        vec2[DOWNB],
    )


def solution(mesh):
    both = ("dp", "seq")
    rows, slots, vector, matrix = P("dp", "seq", None), P("dp", None, None), P(both), P(both, None)
    weights = (vector, vector, matrix, vector, vector, matrix, vector, vector, vector, matrix, vector, matrix, vector)
    return jax.shard_map(
        functools.partial(per_device, mesh.shape["seq"], mesh.size),
        mesh=mesh,
        in_specs=(rows, slots, P("dp")) + weights + (rows, slots),
        out_specs=(rows, slots, rows, slots) + weights,
        check_vma=False,
    )
```

time: 1130 us -> 327 us (0.29)
  waiting for transfers between devices: 416 us -> 0.02 us
  matrix products: 306 us -> 0 us
  Pallas kernels: 0 us -> 283 us
  blocking collectives: 130 us -> 0 us
  local copies, waits for them, and re-layouts: 128 us -> 31.8 us
  other arithmetic: 98.4 us -> 9.06 us
  loops' own time: 26.5 us -> 0 us
  between operations: 15.1 us -> 0.83 us
    reduce_scatter x6 -> x0, waiting for transfers between devices: 408 us -> none  [the longest x1 140 us: per_device(): lax.psum_scatter(up_grad, ('dp', 'seq'), scatter_dimension=0, tiled=True)]
    dot_general x68 -> x0, matrix products: 306 us -> none  [the longest x16 70.5 us: head_scores(): jnp.einsum('iqe,ike->iqk', head_slice(queries, head_index, head_size), he...]
    pallas_call x0 -> x9, Pallas kernels: none -> 283 us  [the longest x2 71.9 us: reduce(): pl.pallas_call(functools.partial(reduce_kernel, seq_size, len(parts)), ou...]
    unnamed x2 -> x0, blocking collectives: 79.7 us -> none
    convert_element_type x20 -> x0, other arithmetic: 49.4 us -> none  [the longest x1 35.7 us: forward(): hidden = jax.nn.gelu(hidden_pre, approximate=False).astype(jnp.bfloat16)]
    unnamed x157 -> x29, local copies, waits for them, and re-layouts: 52.6 us -> 3.62 us
    all_gather x1 -> x0, blocking collectives: 44 us -> none  [per_device(): lax.all_gather(out_weight, ('dp', 'seq'), axis=0, tiled=True)]
    another operation x2 -> x0, loops' own time: 26.5 us -> none  [the longest x1 21.2 us: attend_back(): lax.map(one_head, jnp.arange(head_count))]
  transfers between devices with their start and end apart: 11 -> 6, of which waited for: 5 -> 0; matrix products, arithmetic and copies ran while one was open for 23% -> 7% of each run, Pallas kernels for 0% -> 33%
where the time goes in v1:
time: 327 us; the launch traced here: 326 us
  Pallas kernels  283 us (87%)
  local copies, waits for them, and re-layouts  31.8 us (10%)
  other arithmetic  9.06 us (3%)
    pallas_call x2, Pallas kernels, reduce(): pl.pallas_call(functools.partial(reduce_kernel, seq_size, len(parts)), ou...  71.9 us
    pallas_call x2, Pallas kernels, gather(): pl.pallas_call(functools.partial(gather_kernel, seq_size, len(shards)), o...  57.5 us
    pallas_call x1, Pallas kernels, attend_back(): pl.pallas_call(functools.partial(attend_back_kernel, count, patch, head),...  50.5 us
    pallas_call x1, Pallas kernels, ffn(): pl.pallas_call(functools.partial(ffn_kernel, steps, 512), grid=(steps,),...  45.4 us
    pallas_call x1, Pallas kernels, attend(): pl.pallas_call(functools.partial(attend_kernel, count, patch, head), grid...  35.3 us
    pallas_call x1, Pallas kernels, in_back(): pl.pallas_call(functools.partial(in_back_kernel, steps, count), grid=(ste...  15.8 us
    pallas_call x1, Pallas kernels, qkv(): pl.pallas_call(qkv_kernel, grid=(x.shape[0],), in_specs=[block, WHOLE, WH...  6.65 us
  transfers between devices with their start and end apart: 6, of which 0 were waited for; matrix products, arithmetic and copies ran while one was open for 7% of the time, Pallas kernels for 33%

profile of v1, /device:TPU:0, one launch (start us, length us, event | category | flops | bytes accessed | tf_op | source)
XLA Modules:
  0.0 326.3 jit_solution(16879282094437614208)
XLA Ops:
  6.7 1.4 fusion.13.refs_0_
  8.1 22.5 %gather.2 = bf16[4,2,2,2,16,1664]{5,4,3,2,1,0:T(8,128)(2,1)} custom-call(bf16[16,1664]{1,0:T(8,128)(2,1)} %fusion.13.refs_0_), custom_call_target="tpu_custom_call" | custom-call | tf_op jit(solution)/shard_map/gather/pallas_call | solution.py:190
  30.6 0.9 slice.93
  31.6 2.8 slice.92.w_ref.refs_2_
  36.0 1.3 fusion.2.x_ref
  37.3 6.6 %qkv.1 = (bf16[3,560,512]{2,1,0:T(8,128)(2,1)}, bf16[3,560,512]{2,1,0:T(8,128)(2,1)}, bf16[3,560,512]{2,1,0:T(8,128)(2,1)}) custom-call(bf16[3,560,512]{2,1,0:T(8,128)(2,1)} %fusion.2.x_ref, bf16[512,1536]{1,0:T(8,128)(2,1)} %slice.92.w_ref.refs_2_, f32[128,512]{1,0:T(8,128)} %convert_bitcast_fusion.vec_ref.refs_3_), custom_call_target="tpu_custom_call" | custom-call | tf_op jit(solution)/shard_map/qkv/pallas_call | solution.py:362
  46.1 1.5 pad_maximum_fusion.refs_0_
  47.6 35.0 %gather.3 = (bf16[4,2,2,2,16,2560]{5,4,3,2,1,0:T(8,128)(2,1)}, bf16[4,2,2,2,64,640]{5,4,3,2,1,0:T(8,128)(2,1)}) custom-call(bf16[16,2560]{1,0:T(8,128)(2,1)} %pad_maximum_fusion.refs_0_, bf16[64,640]{1,0:T(8,128)(2,1)} %fusion.12.refs_1_), custom_call_target="tpu_custom_call" | custom-call | tf_op jit(solution)/shard_map/gather/pallas_call | solution.py:190
  82.6 2.9 fusion.3
  85.6 1.2 copy-done
  87.3 35.3 %attend.1 = (bf16[3,560,512]{2,1,0:T(8,128)(2,1)}, f32[3,560,512]{2,1,0:T(8,128)}) custom-call(bf16[3,560,512]{2,1,0:T(8,128)(2,1)} %get-tuple-element.39.refs_0_, bf16[3,560,512]{2,1,0:T(8,128)(2,1)} %get-tuple-element.40.refs_1_, bf16[3,560,512]{2,1,0:T(8,128)(2,1)} %copy-done, bf16[3,560,512]{2,1,0:T(8,128)(2,1)} %get-tuple-element.41.refs_3_, ...), custom_call_target="tpu_custom_call" | custom-call | tf_op jit(solution)/shard_map/attend/pallas_call | solution.py:414
  122.6 45.4 %ffn.1 = (bf16[1680,512]{1,0:T(8,128)(2,1)}, bf16[1680,512]{1,0:T(8,128)(2,1)}, bf16[1680,512]{1,0:T(8,128)(2,1)}, bf16[512,2688]{1,0:T(8,128)(2,1)}, bf16[2048,640]{1,0:T(8,128)(2,1)}) custom-call(bf16[1680,512]{1,0:T(8,128)(2,1)} %bitcast.40, bf16[1680,512]{1,0:T(8,128)(2,1)} %bitcast.43, bf16[1680,512]{1,0:T(8,128)(2,1)} %bitcast.42, ...), custom_call_target="tpu_custom_call" | custom-call | tf_op jit(solution)/shard_map/ffn/pallas_call | solution.py:534
  167.9 50.5 %attend_back.1 = (bf16[3,560,512]{2,1,0:T(8,128)(2,1)}, bf16[3,560,512]{2,1,0:T(8,128)(2,1)}, bf16[3,560,512]{2,1,0:T(8,128)(2,1)}, bf16[3,560,512]{2,1,0:T(8,128)(2,1)}, bf16[3,560,512]{2,1,0:T(8,128)(2,1)}) custom-call(bf16[3,560,512]{2,1,0:T(8,128)(2,1)} %get-tuple-element.39.refs_0_, bf16[3,560,512]{2,1,0:T(8,128)(2,1)} %get-tuple-element.40.refs_1_, ...), custom_call_target="tpu_custom_call" | custom-call | tf_op jit(solution)/shard_map/attend_back/pallas_call | solution.py:468
  219.0 0.9 fusion.15
  220.4 47.4 %reduce.21 = (f32[16,2688]{1,0:T(8,128)}, f32[64,640]{1,0:T(8,128)}) custom-call(bf16[4,2,2,2,16,2688]{5,4,3,2,1,0:T(8,128)(2,1)} %bitcast.46, bf16[4,2,2,2,64,640]{5,4,3,2,1,0:T(8,128)(2,1)} %bitcast.47), custom_call_target="tpu_custom_call" | custom-call | tf_op jit(solution)/shard_map/reduce/pallas_call | solution.py:300
  269.2 1.6 slice.88
  270.8 1.4 slice.83
  272.2 2.7 slice.94
  277.0 1.7 reshape.112
  278.7 1.2 copy-done.2
  280.5 15.8 %in_back.1 = (bf16[1680,512]{1,0:T(8,128)(2,1)}, bf16[512,1664]{1,0:T(8,128)(2,1)}) custom-call(bf16[1680,512]{1,0:T(8,128)(2,1)} %bitcast.41, bf16[1680,512]{1,0:T(8,128)(2,1)} %get-tuple-element.46.refs_1_, bf16[512,1536]{1,0:T(8,128)(2,1)} %slice.92.w_ref.refs_2_, f32[128,512]{1,0:T(8,128)} %convert_bitcast_fusion.vec_ref.refs_3_, ...), custom_call_target="tpu_custom_call" | custom-call | tf_op jit(solution)/shard_map/in_back/pallas_call | solution.py:594
  296.3 1.0 fusion.14
  297.4 24.5 %reduce.20 = f32[16,1664]{1,0:T(8,128)} custom-call(bf16[4,2,2,2,16,1664]{5,4,3,2,1,0:T(8,128)(2,1)} %bitcast.56), custom_call_target="tpu_custom_call" | custom-call | tf_op jit(solution)/shard_map/reduce/pallas_call | solution.py:300
  322.7 1.3 slice.97
  (71 shorter events, 18.7 us)
Async XLA Ops:
  31.5 3.7 %copy-start.7 = (bf16[3,77,512]{2,1,0:T(8,128)(2,1)S(1)}, bf16[3,77,512]{2,1,0:T(8,128)(2,1)}, u32[]{:S(2)}) copy-start(bf16[3,77,512]{2,1,0:T(8,128)(2,1)} %param.37) | copy-start | bytes 709636
  31.5 3.7 %copy-start.8 = (bf16[3,77,512]{2,1,0:T(8,128)(2,1)S(1)}, bf16[3,77,512]{2,1,0:T(8,128)(2,1)}, u32[]{:S(2)}) copy-start(bf16[3,77,512]{2,1,0:T(8,128)(2,1)} %param.21) | copy-start | bytes 709636
  31.6 4.4 %copy-start.5 = (bf16[3,512,512]{2,1,0:T(8,128)(2,1)S(1)}, bf16[3,512,512]{2,1,0:T(8,128)(2,1)}, u32[]{:S(2)}) copy-start(bf16[3,512,512]{2,1,0:T(8,128)(2,1)} %param.20) | copy-start | bytes 4718596
  37.3 7.2 %copy-start.13 = (s32[3]{0:T(128)S(1)}, s32[3]{0:T(128)}, u32[]{:S(2)}) copy-start(s32[3]{0:T(128)} %param.22) | copy-start | bytes 40
  37.3 8.0 %copy-start.12 = (bf16[64]{0:T(256)(128)(2,1)S(1)}, bf16[64]{0:T(256)(128)(2,1)}, u32[]{:S(2)}) copy-start(bf16[64]{0:T(256)(128)(2,1)} %param.33) | copy-start | bytes 388
  37.3 8.1 %copy-start.10 = (bf16[64,512]{1,0:T(8,128)(2,1)S(1)}, bf16[64,512]{1,0:T(8,128)(2,1)}, u32[]{:S(2)}) copy-start(bf16[64,512]{1,0:T(8,128)(2,1)} %param.34) | copy-start | bytes 196612
  37.3 8.8 %copy-start.11 = (bf16[16,512]{1,0:T(8,128)(2,1)S(1)}, bf16[16,512]{1,0:T(8,128)(2,1)}, u32[]{:S(2)}) copy-start(bf16[16,512]{1,0:T(8,128)(2,1)} %param.28) | copy-start | bytes 49156
  44.0 41.6 %collective-permute-start = (bf16[3,560,512]{2,1,0:T(8,128)(2,1)}, bf16[3,560,512]{2,1,0:T(8,128)(2,1)S(1)}, u32[]{:S(2)}, u32[]{:S(2)}) collective-permute-start(bf16[3,560,512]{2,1,0:T(8,128)(2,1)} %get-tuple-element.40.refs_1_), channel_id=1, source_target_pairs={{1,0},{0,1},{3,2},{2,3},{5,4},{4,5},{7,6},{6,7},{9,8},{8,9},{11,10... | collective-permute-start | bytes 5160968 | tf_op jit(solution)/shard_map/ppermute | solution.py:653
  44.4 41.2 %collective-permute-start.1 = (bf16[3,560,512]{2,1,0:T(8,128)(2,1)}, bf16[3,560,512]{2,1,0:T(8,128)(2,1)S(1)}, u32[]{:S(2)}, u32[]{:S(2)}) collective-permute-start(bf16[3,560,512]{2,1,0:T(8,128)(2,1)} %get-tuple-element.41.refs_3_), channel_id=1, source_target_pairs={{1,0},{0,1},{3,2},{2,3},{5,4},{4,5},{7,6},{6,7},{9,8},{8,9},{11,10... | collective-permute-start | bytes 5160968 | tf_op jit(solution)/shard_map/ppermute | solution.py:653
  85.5 1.2 copy-start
  85.6 1.7 copy-start.1
  218.4 60.3 %collective-permute-start.3 = (bf16[3,560,512]{2,1,0:T(8,128)(2,1)}, bf16[3,560,512]{2,1,0:T(8,128)(2,1)S(1)}, u32[]{:S(2)}, u32[]{:S(2)}) collective-permute-start(bf16[3,560,512]{2,1,0:T(8,128)(2,1)} %get-tuple-element.51), channel_id=1, source_target_pairs={{0,1},{1,0},{2,3},{3,2},{4,5},{5,4},{6,7},{7,6},{8,9},{9,8},{10,11... | collective-permute-start | bytes 5160968 | tf_op jit(solution)/shard_map/ppermute | solution.py:658
  218.9 59.8 %collective-permute-start.4 = (bf16[3,560,512]{2,1,0:T(8,128)(2,1)}, bf16[3,560,512]{2,1,0:T(8,128)(2,1)S(1)}, u32[]{:S(2)}, u32[]{:S(2)}) collective-permute-start(bf16[3,560,512]{2,1,0:T(8,128)(2,1)} %get-tuple-element.53), channel_id=1, source_target_pairs={{0,1},{1,0},{2,3},{3,2},{4,5},{5,4},{6,7},{7,6},{8,9},{9,8},{10,11... | collective-permute-start | bytes 5160968 | tf_op jit(solution)/shard_map/ppermute | solution.py:658
  219.9 56.2 %collective-permute-start.2 = (bf16[3,39,512]{2,1,0:T(8,128)(2,1)S(1)}, bf16[3,39,512]{2,1,0:T(8,128)(2,1)S(1)}, u32[]{:S(2)}, u32[]{:S(2)}) collective-permute-start(bf16[3,39,512]{2,1,0:T(8,128)(2,1)S(1)} %get-tuple-element.70), channel_id=1, source_target_pairs={{1,0},{0,1},{3,2},{2,3},{5,4},{4,5},{7,6},{6,7},{9,8},{8,9},{11,10... | collective-permute-start | bytes 359432 | tf_op jit(solution)/shard_map/ppermute | solution.py:653
  269.2 5.6 %copy-start.9 = (f32[64,640]{1,0:T(8,128)S(1)}, f32[64,640]{1,0:T(8,128)}, u32[]{:S(2)}) copy-start(f32[64,640]{1,0:T(8,128)} %get-tuple-element.59) | copy-start | bytes 491524
  278.7 1.2 copy-start.2
  278.7 1.7 copy-start.3
  296.3 26.4 %copy-start.4 = (bf16[1680,512]{1,0:T(8,128)(2,1)S(1)}, bf16[1680,512]{1,0:T(8,128)(2,1)}, u32[]{:S(2)}) copy-start(bf16[1680,512]{1,0:T(8,128)(2,1)} %get-tuple-element.54) | copy-start | bytes 5160964
  297.3 28.0 %collective-permute-start.5 = (bf16[3,39,512]{2,1,0:T(8,128)(2,1)S(1)}, bf16[3,39,512]{2,1,0:T(8,128)(2,1)S(1)}, u32[]{:S(2)}, u32[]{:S(2)}) collective-permute-start(bf16[3,39,512]{2,1,0:T(8,128)(2,1)S(1)} %get-tuple-element.68), channel_id=1, source_target_pairs={{1,0},{0,1},{3,2},{2,3},{5,4},{4,5},{7,6},{6,7},{9,8},{8,9},{11,10... | collective-permute-start | bytes 359432 | tf_op jit(solution)/shard_map/ppermute | solution.py:653
  321.9 2.0 copy-start.6

commit v2 on v1

--- a/solution.py
+++ b/solution.py
@@ -42,6 +42,7 @@
 
 
 WHOLE = pl.BlockSpec(memory_space=pltpu.VMEM)
+ANY = pl.BlockSpec(memory_space=pl.ANY)
 
 
 class Place:
@@ -87,10 +88,14 @@
     def above(self, k):
         return self.device(self.ahead(k), self.y, self.x, self.core)
 
+    def mate(self, step):
+        return (lax.axis_index("dp"), lax.rem(lax.axis_index("seq") + self.seq_size - step, self.seq_size))
+
     def greet(self):
         barrier = pltpu.get_barrier_semaphore()
         friends = [self.above(k) for k in range(1, self.depth)]
         friends += [self.first(), self.second(), self.other_core()]
+        friends += [self.mate(step) for step in range(1, self.seq_size)]
         for friend in friends:
             pl.semaphore_signal(barrier, inc=1, device_id=friend, device_id_type=MESH)
         pl.semaphore_wait(barrier, len(friends))
@@ -105,7 +110,6 @@
 class Gather:
     def __init__(self, place, shard, full, out, into, local):
         self.place, self.shard, self.full, self.out, self.into, self.local = place, shard, full, out, into, local
-        self.sends = []
 
     def block(self, k, column, core):
         y, x = self.place.columns[column]
@@ -115,9 +119,7 @@
         return remote(src, dst, self.out.at[lane, k], self.into.at[lane, k], device)
 
     def send(self, src, dst, lane, k, device):
-        copy = self.copy(src, dst, lane, k, device)
-        copy.start()
-        self.sends.append(copy)
+        self.copy(src, dst, lane, k, device).start()
 
     def arrived(self, lane, k, column, core):
         here = self.block(k, column, core)
@@ -127,8 +129,7 @@
     def start(self):
         place = self.place
         mine = self.block(0, 0, place.core)
-        self.own = pltpu.make_async_copy(self.shard, mine, self.local)
-        self.own.start()
+        pltpu.make_async_copy(self.shard, mine, self.local).start()
         for k in range(1, place.depth):
             self.send(self.shard, mine, 0, k, place.above(k))
         self.forward_line(0)
@@ -154,49 +155,17 @@
         for column in range(4):
             for k in range(self.place.depth):
                 self.arrived(4 + column, k, column, 1 - self.place.core)
-        self.own.wait()
-        for copy in self.sends:
-            copy.wait_send()
+        mine = self.block(0, 0, self.place.core)
+        pltpu.make_async_copy(self.shard, mine, self.local).wait()
+        for lane in range(8):
+            for k in range(self.place.depth):
+                if lane or k:
+                    self.copy(mine, mine, lane, k, self.place.other_core()).wait_send()
 
 
 def gather_sems(depth):
     sems = pltpu.SemaphoreType.DMA
     return [sems((8, depth)), sems((8, depth)), sems]
-
-
-def gather_kernel(seq_size, arrays, *refs):
-    shards, fulls, sems = refs[:arrays], refs[arrays : 2 * arrays], refs[2 * arrays :]
-    place = Place(fulls[0].shape[0], seq_size)
-    place.greet()
-    moves = [Gather(place, shards[n], fulls[n], *sems[3 * n : 3 * n + 3]) for n in range(arrays)]
-    for move in moves:
-        move.start()
-    for k in range(1, place.depth):
-        for move in moves:
-            move.forward_line(k)
-    for k in range(place.depth):
-        for move in moves:
-            move.forward_first(k)
-    for half in range(2):
-        for k in range(place.depth):
-            for move in moves:
-                move.forward_second(half, k)
-    for move in moves:
-        move.finish()
-
-
-def gather(shards, devices, seq_size, number):
-    depth = devices // 8
-    fulls = pl.pallas_call(
-        functools.partial(gather_kernel, seq_size, len(shards)),
-        out_shape=[jax.ShapeDtypeStruct((depth, 2, 2, 2) + shard.shape, shard.dtype) for shard in shards],
-        in_specs=[WHOLE] * len(shards),
-        out_specs=[WHOLE] * len(shards),
-        scratch_shapes=gather_sems(depth) * len(shards),
-        compiler_params=compiler_params(collective_id=number, has_side_effects=True),
-        name="gather",
-    )(*shards)
-    return [full.reshape(-1, full.shape[-1]) for full in fulls]
 
 
 class Reduce:
@@ -345,29 +314,101 @@
     return jnp.transpose(jnp.concatenate([rows, jnp.zeros((LANES - count, width), f32)], axis=0)).astype(bf16)
 
 
-def qkv_kernel(x_ref, w_ref, vec_ref, q_ref, k_ref, v_ref):
-    width = x_ref.shape[2]
-    scaled, _ = norm_rows(x_ref[0].astype(f32))
-    first_in = (scaled * vec_ref[GAIN1 : GAIN1 + 1] + vec_ref[SHIFT1 : SHIFT1 + 1]).astype(bf16)
-    scale = LOG2E / math.sqrt(width // HEADS)
-    q = mm(first_in, w_ref[:, :width]) + vec_ref[QBIAS : QBIAS + 1]
-    q_ref[0] = (q * scale).astype(bf16)
-    k_ref[0] = mm(first_in, w_ref[:, width : 2 * width]).astype(bf16)
-    v = mm(first_in, w_ref[:, 2 * width : 3 * width]) + vec_ref[VBIAS : VBIAS + 1]
-    v_ref[0] = v.astype(bf16)
-
-
-def qkv(x, weight, vecs):
-    block = pl.BlockSpec((1,) + x.shape[1:], lambda i: (i, 0, 0))
-    return pl.pallas_call(
-        qkv_kernel,
-        grid=(x.shape[0],),
-        in_specs=[block, WHOLE, WHOLE],
-        out_specs=[block] * 3,
-        out_shape=[jax.ShapeDtypeStruct(x.shape, bf16)] * 3,
-        compiler_params=compiler_params(),
-        name="qkv",
-    )(x, weight, vecs)
+def own_text(ref, item, text, seq):
+    slots, width = ref.shape[1:]
+    own = jnp.zeros((text, width), ref.dtype)
+    for r in range(-(-slots // text)):
+        share = ref[item, r * text : min(slots, (r + 1) * text), :]
+        if share.shape[0] < text:
+            share = jnp.concatenate([share, jnp.zeros((text - share.shape[0], width), ref.dtype)], axis=0)
+        own = jnp.where(seq == r, share, own)
+    return own
+
+
+def as_column(row, count):
+    length = row.shape[1] // count
+    rows = [row[:, n * length : (n + 1) * length].astype(f32) for n in range(count)]
+    rows = jnp.concatenate(rows + [jnp.zeros((LANES - count, length), f32)], axis=0)
+    rows = jnp.concatenate([rows, jnp.zeros((LANES, LANES - length), f32)], axis=1)
+    return jnp.transpose(rows)[:length].astype(bf16)
+
+
+def front_kernel(seq_size, text, *refs):
+    shard_ref, vec_ref, up_bias_ref, down_ref, x_ref, slot_ref = refs[:6]
+    outs = refs[6 : 11 + 2 * seq_size]
+    w_full, vecs, side_ref, xtext_ref, q_ref = outs[:5]
+    k_refs, v_refs = outs[5 : 5 + seq_size], outs[5 + seq_size :]
+    shard, out, into, local, kv_out, kv_in = refs[11 + 2 * seq_size :]
+    items, patch, model = x_ref.shape
+    wide = shard_ref.shape[1]
+    place = Place(w_full.shape[0], seq_size)
+    seq = lax.axis_index("seq")
+    place.greet()
+    shard[:, :wide] = shard_ref[...]
+    shard[:, wide:] = as_column(vec_ref[...], 8)
+    move = Gather(place, shard, w_full, out, into, local)
+    move.start()
+    side_ref[:, :model] = down_ref[...]
+    side_ref[:, model:] = as_column(up_bias_ref[...], 1)
+    for i in range(items):
+        xtext_ref[i] = own_text(slot_ref, i, text, seq)
+    for k in range(1, place.depth):
+        move.forward_line(k)
+    for k in range(place.depth):
+        move.forward_first(k)
+    for half in range(2):
+        for k in range(place.depth):
+            move.forward_second(half, k)
+    move.finish()
+    rows = w_full.shape[0] * 8 * w_full.shape[4]
+    weight = w_full[...].reshape(rows, w_full.shape[5])
+    table = jnp.transpose(weight[:, wide:].astype(f32))
+    vecs[...] = table
+    scale = LOG2E / math.sqrt(model // HEADS)
+    copies = []
+    for i in range(items):
+        scaled, _ = norm_rows(jnp.concatenate([x_ref[i], xtext_ref[i]], axis=0).astype(f32))
+        first_in = (scaled * table[GAIN1 : GAIN1 + 1] + table[SHIFT1 : SHIFT1 + 1]).astype(bf16)
+        k_refs[0][i] = mm(first_in, weight[:, model : 2 * model]).astype(bf16)
+        v = mm(first_in, weight[:, 2 * model : 3 * model]) + table[VBIAS : VBIAS + 1]
+        v_refs[0][i] = v.astype(bf16)
+        for r in range(1, seq_size):
+            for n, ref in enumerate((k_refs, v_refs)):
+                at = (2 * i + n) * seq_size + r
+                copies.append(remote(ref[0].at[i], ref[r].at[i], kv_out.at[at], kv_in.at[at], place.mate(r)))
+                copies[-1].start()
+        q = mm(first_in, weight[:, :model]) + table[QBIAS : QBIAS + 1]
+        q_ref[i] = (q * scale).astype(bf16)
+    for copy in copies:
+        copy.wait()
+
+
+def front(in_weight, vectors, up_bias, down_weight, patches, text_rows, text, devices, seq_size):
+    items, patch, model = patches.shape
+    depth = devices // 8
+    rows, cols = in_weight.shape
+    tokens = jax.ShapeDtypeStruct((items, patch + text, model), bf16)
+    sems = pltpu.SemaphoreType.DMA
+    outs = pl.pallas_call(
+        functools.partial(front_kernel, seq_size, text),
+        in_specs=[WHOLE] * 6,
+        out_specs=[WHOLE] * (5 + 2 * seq_size),
+        out_shape=[
+            jax.ShapeDtypeStruct((depth, 2, 2, 2, rows, cols + LANES), bf16),
+            jax.ShapeDtypeStruct((LANES, model), f32),
+            jax.ShapeDtypeStruct((down_weight.shape[0], model + LANES), bf16),
+            jax.ShapeDtypeStruct((items, text, model), bf16),
+            tokens,
+        ]
+        + [tokens] * (2 * seq_size),
+        scratch_shapes=[pltpu.VMEM((rows, cols + LANES), bf16)]
+        + gather_sems(depth)
+        + [sems((2 * items * seq_size,)), sems((2 * items * seq_size,))],
+        compiler_params=compiler_params(collective_id=0, has_side_effects=True),
+        name="front",
+    )(in_weight, vectors, up_bias, down_weight, patches, text_rows)
+    full = outs[0].reshape(model, cols + LANES)
+    return full, outs[1], outs[2], outs[3], outs[4], outs[5 : 5 + seq_size], outs[5 + seq_size :]
 
 
 def collect(dst, refs, patch, text):
@@ -381,11 +422,48 @@
         dst[filled:, :width] = jnp.zeros((dst.shape[0] - filled, width), dst.dtype)
 
 
-def attend_kernel(count, patch, head, *refs):
+def gather_turns(move, depth):
+    turns = {}
+
+    def add(turn, *action):
+        turns.setdefault(turn, []).append(action)
+
+    for k in range(depth):
+        quarter = 4 * k // depth
+        if k:
+            add((1, 1, 3, 4)[quarter], move.forward_line, k)
+        add((3, 4, 5, 6)[quarter], move.forward_first, k)
+        add((4, 5, 6, 7)[quarter], move.forward_second, 0, k)
+        add((6, 7, 8, 9)[quarter], move.forward_second, 1, k)
+    return turns
+
+
+def attend_kernel(count, patch, head, seq_size, *refs):
     q_ref, k_refs, v_refs = refs[0], refs[1 : 1 + count], refs[1 + count : 1 + 2 * count]
-    bias_ref, out_ref, log_ref, keys, values = refs[1 + 2 * count :]
+    bias_ref, shard_a, shard_b, out_ref, log_ref, full_a, full_b, keys, values = refs[1 + 2 * count : 10 + 2 * count]
+    sems = refs[10 + 2 * count :]
     width = q_ref.shape[2]
     text = q_ref.shape[1] - patch
+    place = Place(full_a.shape[0], seq_size)
+    turn = pl.program_id(0) * pl.num_programs(1) + pl.program_id(1)
+    last = pl.num_programs(0) * pl.num_programs(1) - 1
+    moves = [Gather(place, shard_a, full_a, *sems[:3]), Gather(place, shard_b, full_b, *sems[3:])]
+
+    @pl.when(turn == 0)
+    def _():
+        place.greet()
+        for move in moves:
+            move.start()
+
+    turns = [gather_turns(move, place.depth) for move in moves]
+    for at in sorted(turns[0]):
+
+        @pl.when(turn == at)
+        def _(at=at):
+            for pair in zip(*[each[at] for each in turns]):
+                for action in pair:
+                    action[0](*action[1:])
+
     collect(keys, k_refs, patch, text)
     collect(values, v_refs, patch, text)
     values[:, width:] = jnp.ones((values.shape[0], values.shape[1] - width), bf16)
@@ -406,28 +484,37 @@
     out_ref[0] = out.astype(bf16)
     log_ref[0] = logs
 
-
-def attend(q, keys, values, bias, patch, head, width):
+    @pl.when(turn == last)
+    def _():
+        for move in moves:
+            move.finish()
+
+
+def attend(q, keys, values, bias, shards, patch, head, width, devices, seq_size):
     items, _, model = q.shape
     count, span = len(keys), bias.shape[-1]
+    depth = devices // 8
     block = pl.BlockSpec((1, q.shape[1], width), lambda i, p: (i, 0, p))
-    return pl.pallas_call(
-        functools.partial(attend_kernel, count, patch, head),
+    outs = pl.pallas_call(
+        functools.partial(attend_kernel, count, patch, head, seq_size),
         grid=(items, model // width),
-        in_specs=[block] * (1 + 2 * count) + [pl.BlockSpec((1, 1, span), lambda i, p: (i, 0, 0))],
-        out_specs=[block, block],
-        out_shape=[jax.ShapeDtypeStruct(q.shape, bf16), jax.ShapeDtypeStruct(q.shape, f32)],
-        scratch_shapes=[pltpu.VMEM((span, width), bf16), pltpu.VMEM((span, 2 * width), bf16)],
-        compiler_params=compiler_params(),
+        in_specs=[block] * (1 + 2 * count) + [pl.BlockSpec((1, 1, span), lambda i, p: (i, 0, 0))] + [ANY] * 2,
+        out_specs=[block, block, ANY, ANY],
+        out_shape=[jax.ShapeDtypeStruct(q.shape, bf16), jax.ShapeDtypeStruct(q.shape, f32)]
+        + [jax.ShapeDtypeStruct((depth, 2, 2, 2) + shard.shape, shard.dtype) for shard in shards],
+        scratch_shapes=[pltpu.VMEM((span, width), bf16), pltpu.VMEM((span, 2 * width), bf16)]
+        + gather_sems(depth) * 2,
+        compiler_params=compiler_params(collective_id=1, has_side_effects=True),
         name="attend",
-    )(q, *keys, *values, bias)
+    )(q, *keys, *values, bias, *shards)
+    return outs[0], outs[1], [full.reshape(-1, full.shape[-1]) for full in outs[2:]]
 
 
 def attend_back_kernel(count, patch, head, *refs):
     q_ref, k_refs, v_refs = refs[0], refs[1 : 1 + count], refs[1 + count : 1 + 2 * count]
-    bias_ref, out_ref, log_ref, grad_ref, dq_ref = refs[1 + 2 * count : 6 + 2 * count]
-    dk_refs, dv_refs = refs[6 + 2 * count : 6 + 3 * count], refs[6 + 3 * count : 6 + 4 * count]
-    keys, values = refs[6 + 4 * count :]
+    bias_ref, log_ref, grad_ref, dq_ref = refs[1 + 2 * count : 5 + 2 * count]
+    dk_refs, dv_refs = refs[5 + 2 * count : 5 + 3 * count], refs[5 + 3 * count : 5 + 4 * count]
+    keys, values = refs[5 + 4 * count :]
     width = q_ref.shape[2]
     text = q_ref.shape[1] - patch
     collect(keys, k_refs, patch, text)
@@ -435,16 +522,15 @@
     q, grad = q_ref[0], grad_ref[0]
     lane = lax.broadcasted_iota(jnp.int32, (1, width), 1) // head
     row = lax.broadcasted_iota(jnp.int32, (width, 1), 0) // head
-    inner = grad.astype(f32) * out_ref[0].astype(f32)
     dq = dk = dv = None
     for h in range(width // head):
         mine = lane == h
         q_head = jnp.where(mine, q, jnp.zeros_like(q))
         grad_head = jnp.where(mine, grad, jnp.zeros_like(grad))
-        delta = jnp.sum(jnp.where(mine, inner, 0.0), axis=1, keepdims=True)
         scores = mm_t(q_head, keys[...]) + bias_ref[0]
         probs = jnp.exp2(scores - log_ref[0, :, h * head : h * head + 1])
         grad_probs = mm_t(grad_head, values[...])
+        delta = jnp.sum(probs * grad_probs, axis=1, keepdims=True)
         grad_scores = (probs * (grad_probs - delta)).astype(bf16)
         dv_head = t_mm(grad, probs.astype(bf16))
         dk_head = t_mm(q, grad_scores)
@@ -461,20 +547,20 @@
             parts[r][0, patch:, :] = grads[at : at + text]
 
 
-def attend_back(q, keys, values, bias, attended, logs, grad_att, patch, head, width):
+def attend_back(q, keys, values, bias, logs, grad_att, patch, head, width):
     items, _, model = q.shape
     count, span = len(keys), bias.shape[-1]
     block = pl.BlockSpec((1, q.shape[1], width), lambda i, p: (i, 0, p))
     grads = pl.pallas_call(
         functools.partial(attend_back_kernel, count, patch, head),
         grid=(items, model // width),
-        in_specs=[block] * (1 + 2 * count) + [pl.BlockSpec((1, 1, span), lambda i, p: (i, 0, 0))] + [block] * 3,
+        in_specs=[block] * (1 + 2 * count) + [pl.BlockSpec((1, 1, span), lambda i, p: (i, 0, 0))] + [block] * 2,
         out_specs=[block] * (1 + 2 * count),
         out_shape=[jax.ShapeDtypeStruct(q.shape, bf16)] * (1 + 2 * count),
         scratch_shapes=[pltpu.VMEM((span, width), bf16), pltpu.VMEM((span, width), bf16)],
         compiler_params=compiler_params(),
         name="attend_back",
-    )(q, *keys, *values, bias, attended, logs, grad_att)
+    )(q, *keys, *values, bias, logs, grad_att)
     return grads[0], grads[1 : 1 + count], grads[1 + count :]
 
 
@@ -637,15 +723,8 @@
     units = up_weight.shape[1]
     head = model // HEADS
     width = min(LANES, model)
-    share = -(-slots // seq_size)
-    text = round_up(share, ROW_TILE)
+    text = round_up(-(-slots // seq_size), ROW_TILE)
     seq = lax.axis_index("seq")
-
-    def rows_of(patch_rows, slot_rows):
-        padded = jnp.pad(slot_rows, ((0, 0), (0, share * seq_size - slots), (0, 0)))
-        mine = lax.dynamic_slice_in_dim(padded, seq * share, share, 1)
-        mine = jnp.pad(mine, ((0, 0), (0, text - share), (0, 0)))
-        return jnp.concatenate([patch_rows, mine], axis=1)
 
     def rotate(array, step):
         if step == 0:
@@ -657,53 +736,45 @@
             return array
         return lax.ppermute(array, "seq", [(i, (i + step) % seq_size) for i in range(seq_size)])
 
-    vec_shard = jnp.stack(
-        [first_gain, first_shift, query_bias, value_bias, branch_bias, second_gain, second_shift, down_bias], axis=1
+    vectors = [first_gain, first_shift, query_bias, value_bias, branch_bias, second_gain, second_shift, down_bias]
+    in_full, vecs, side_shard, x_text, q, keys, values = front(
+        in_weight, jnp.concatenate(vectors)[None], up_bias[None], down_weight, patches, text_rows, text, devices, seq_size
     )
-    vec_shard = jnp.pad(vec_shard, ((0, 0), (0, LANES - vec_shard.shape[1])))
-    (first,) = gather([jnp.concatenate([in_weight, vec_shard], axis=1)], devices, seq_size, 0)
-    up_column = jnp.pad(up_bias[:, None], ((0, 0), (0, LANES - 1)))
-    weights, w_down = gather(
-        [jnp.concatenate([up_weight, out_weight], axis=1), jnp.concatenate([down_weight, up_column], axis=1)],
-        devices,
-        seq_size,
-        1,
-    )
-    vecs = first[:, 3 * model :].astype(f32).T
-
-    x = rows_of(patches, text_rows)
-    dy = rows_of(patch_cotangent, text_cotangent)
-    in_full = first[:, : 3 * model]
-    q, k, v = qkv(x, in_full, vecs)
-    keys = [rotate(k, r) for r in range(seq_size)]
-    values = [rotate(v, r) for r in range(seq_size)]
+    shards = [jnp.concatenate([up_weight, out_weight], axis=1), side_shard]
+
+    slot_pad = ((0, 0), (0, text * seq_size - slots), (0, 0))
+    dy_text = lax.dynamic_slice_in_dim(jnp.pad(text_cotangent, slot_pad), seq * text, text, 1)
+    dy = jnp.concatenate([patch_cotangent, dy_text], axis=1)
+    x = jnp.concatenate([patches, x_text], axis=1)
 
     spans = []
     for r in range(seq_size):
-        slot = lax.rem(seq + r, seq_size) * share + jnp.arange(text)
-        spans.append((jnp.arange(text) < share)[None, :] & (slot[None, :] < lengths[:, None]))
+        slot = lax.rem(seq + r, seq_size) * text + jnp.arange(text)
+        spans.append(slot[None, :] < lengths[:, None])
     valid = jnp.concatenate([jnp.ones((items, patch * seq_size), jnp.bool_)] + spans, axis=1)
     span = round_up(valid.shape[1], LANES)
     valid = jnp.pad(valid, ((0, 0), (0, span - valid.shape[1])))
     bias = jnp.where(valid, 0.0, NEG_FILL).astype(f32)[:, None, :]
 
-    attended, logs = attend(q, keys, values, bias, patch, head, width)
+    attended, logs, (weights, w_down) = attend(
+        q, keys, values, bias, shards, patch, head, width, devices, seq_size
+    )
     flat = (items * x.shape[1], model)
     result, grad_branch, grad_att, part, down_part = ffn(
         x.reshape(flat), attended.reshape(flat), dy.reshape(flat), weights, w_down, vecs
     )
     sums, down_sums = reduce([part, down_part], devices, seq_size, 2)
     dq, dks, dvs = attend_back(
-        q, keys, values, bias, attended, logs, grad_att.reshape(x.shape), patch, head, width
+        q, keys, values, bias, logs, grad_att.reshape(x.shape), patch, head, width
     )
     dks = [rotate_back(part, r).reshape(flat) for r, part in enumerate(dks)]
     dvs = [rotate_back(part, r).reshape(flat) for r, part in enumerate(dvs)]
-    grad_rows, in_part = in_back(x.reshape(flat), grad_branch, in_full, vecs, dq.reshape(flat), dks, dvs)
+    grad_rows, in_part = in_back(x.reshape(flat), grad_branch, in_full[:, : 3 * model], vecs, dq.reshape(flat), dks, dvs)
     (in_sums,) = reduce([in_part], devices, seq_size, 3)
 
     def split(rows):
         rows = rows.reshape(x.shape)
-        own = rows[:, patch : patch + share]
+        own = rows[:, patch:]
         blocks = [rotate(own, r) for r in range(seq_size)]
         order = jnp.stack(blocks, axis=1)
         order = jnp.roll(order, seq, axis=1)

time: 327 us -> 320 us (0.979); the launches traced: 326 us -> 315 us
  local copies, waits for them, and re-layouts: 31.8 us -> 22.3 us
    pallas_call x4 -> x2, Pallas kernels: 99.4 us -> 83.5 us  [the longest x1 50 us: attend(): pl.pallas_call(functools.partial(attend_kernel, count, patch, head, seq_s...]
    pallas_call x1, Pallas kernels: 45.4 us -> 56.5 us  [ffn(): pl.pallas_call(functools.partial(ffn_kernel, steps, 512), grid=(steps,),...]
    pallas_call x1, Pallas kernels: 50.5 us -> 57.3 us  [attend_back(): pl.pallas_call(functools.partial(attend_back_kernel, count, patch, head),...]
    another operation x9 -> x0, local copies, waits for them, and re-layouts: 6.05 us -> none  [per_device(): jnp.stack([first_gain, first_shift, query_bias, value_bias, branch_bias,...]
    concatenate x0 -> x1, local copies, waits for them, and re-layouts: none -> 5.94 us  [per_device(): jnp.concatenate(vectors)[None]]
    concatenate x5 -> x3, other arithmetic: 7.83 us -> 4.39 us  [the longest x1 2.38 us: per_device(): x = jnp.concatenate([patches, x_text], axis=1)]
  transfers between devices with their start and end apart: 6 -> 4, of which waited for: 0 -> 0; matrix products, arithmetic and copies ran while one was open for 7% -> 5% of each run, Pallas kernels for 33% -> 15%
where the time goes in v2:
time: 320 us; the launch traced here: 315 us
  Pallas kernels  284 us (89%)
  local copies, waits for them, and re-layouts  22.3 us (7%)
  other arithmetic  6.66 us (2%)
    pallas_call x2, Pallas kernels, reduce(): pl.pallas_call(functools.partial(reduce_kernel, seq_size, len(parts)), ou...  71.1 us
    pallas_call x1, Pallas kernels, attend_back(): pl.pallas_call(functools.partial(attend_back_kernel, count, patch, head),...  57.3 us
    pallas_call x1, Pallas kernels, ffn(): pl.pallas_call(functools.partial(ffn_kernel, steps, 512), grid=(steps,),...  56.5 us
    pallas_call x1, Pallas kernels, attend(): pl.pallas_call(functools.partial(attend_kernel, count, patch, head, seq_s...  50 us
    pallas_call x1, Pallas kernels, front(): pl.pallas_call(functools.partial(front_kernel, seq_size, text), in_specs=...  33.5 us
    pallas_call x1, Pallas kernels, in_back(): pl.pallas_call(functools.partial(in_back_kernel, steps, count), grid=(ste...  15.8 us
  transfers between devices with their start and end apart: 4, of which 0 were waited for; matrix products, arithmetic and copies ran while one was open for 5% of the time, Pallas kernels for 15%

profile of v2, /device:TPU:0, one launch (start us, length us, event | category | flops | bytes accessed | tf_op | source)
XLA Modules:
  0.0 314.9 jit_solution(11771000725006693446)
XLA Ops:
  0.7 0.8 broadcast_compare_fusion
  2.3 5.9 %concatenate.18 = bf16[128]{0:T(256)(128)(2,1)} concatenate(bf16[16]{0:T(256)(128)(2,1)} %param.23, bf16[16]{0:T(256)(128)(2,1)} %param.24, bf16[16]{0:T(256)(128)(2,1)} %param.26, bf16[16]{0:T(256)(128)(2,1)} %param.27, bf16[16]{0:T(256)(128)(2,1)} %param.29, bf16[16]{0:T(256)(128)(2,1)} %param.30, bf16[16]{0:T(256)(128)(2,1)} %param.31, bf16[16]{0:T(256)(128)(2,1)} %param.35), dimensions={0} | concatenate | bytes 512 | tf_op jit(solution)/shard_map/concatenate | solution.py:741
  8.2 33.5 %front.1 = (bf16[4,2,2,2,16,1664]{5,4,3,2,1,0:T(8,128)(2,1)}, f32[128,512]{1,0:T(8,128)}, bf16[64,640]{1,0:T(8,128)(2,1)}, bf16[3,48,512]{2,1,0:T(8,128)(2,1)}, ...) custom-call(bf16[16,1536]{1,0:T(8,128)(2,1)} %refs_0_.1, ...), custom_call_target="tpu_custom_call" | custom-call | tf_op jit(solution)/shard_map/front/pallas_call | solution.py:392
  41.8 2.4 pad_maximum_fusion
  44.9 1.4 pad_maximum_fusion.1
  46.2 50.0 %attend.1 = (bf16[3,560,512]{2,1,0:T(8,128)(2,1)}, f32[3,560,512]{2,1,0:T(8,128)}, bf16[4,2,2,2,16,2560]{5,4,3,2,1,0:T(8,128)(2,1)}, bf16[4,2,2,2,64,640]{5,4,3,2,1,0:T(8,128)(2,1)}) custom-call(bf16[3,560,512]{2,1,0:T(8,128)(2,1)} %get-tuple-element.46.refs_0_, bf16[3,560,512]{2,1,0:T(8,128)(2,1)} %get-tuple-element.47.refs_1_, ...), custom_call_target="tpu_custom_call" | custom-call | tf_op jit(solution)/shard_map/attend/pallas_call | solution.py:498
  96.2 56.5 %ffn.1 = (bf16[1680,512]{1,0:T(8,128)(2,1)}, bf16[1680,512]{1,0:T(8,128)(2,1)}, bf16[1680,512]{1,0:T(8,128)(2,1)}, bf16[512,2688]{1,0:T(8,128)(2,1)}, bf16[2048,640]{1,0:T(8,128)(2,1)}) custom-call(bf16[1680,512]{1,0:T(8,128)(2,1)} %bitcast.31, bf16[1680,512]{1,0:T(8,128)(2,1)} %bitcast.47, bf16[1680,512]{1,0:T(8,128)(2,1)} %bitcast.33, ...), custom_call_target="tpu_custom_call" | custom-call | tf_op jit(solution)/shard_map/ffn/pallas_call | solution.py:620
  152.8 57.3 %attend_back.1 = (bf16[3,560,512]{2,1,0:T(8,128)(2,1)}, bf16[3,560,512]{2,1,0:T(8,128)(2,1)}, bf16[3,560,512]{2,1,0:T(8,128)(2,1)}, bf16[3,560,512]{2,1,0:T(8,128)(2,1)}, bf16[3,560,512]{2,1,0:T(8,128)(2,1)}) custom-call(bf16[3,560,512]{2,1,0:T(8,128)(2,1)} %get-tuple-element.46.refs_0_, bf16[3,560,512]{2,1,0:T(8,128)(2,1)} %get-tuple-element.47.refs_1_, ...), custom_call_target="tpu_custom_call" | custom-call | tf_op jit(solution)/shard_map/attend_back/pallas_call | solution.py:554
  210.7 0.7 fusion.7
  211.5 48.1 %reduce.21 = (f32[16,2688]{1,0:T(8,128)}, f32[64,640]{1,0:T(8,128)}) custom-call(bf16[4,2,2,2,16,2688]{5,4,3,2,1,0:T(8,128)(2,1)} %bitcast.34, bf16[4,2,2,2,64,640]{5,4,3,2,1,0:T(8,128)(2,1)} %bitcast.35), custom_call_target="tpu_custom_call" | custom-call | tf_op jit(solution)/shard_map/reduce/pallas_call | solution.py:269
  259.6 0.7 slice_bitcast_fusion
  260.3 0.7 slice_reduce_fusion.1
  261.1 1.3 slice.88
  263.6 2.7 slice.91.refs_2_
  267.6 1.2 fusion.4
  268.9 0.7 slice.90
  269.6 1.2 copy-done.3
  270.7 15.8 %in_back.1 = (bf16[1680,512]{1,0:T(8,128)(2,1)}, bf16[512,1664]{1,0:T(8,128)(2,1)}) custom-call(bf16[1680,512]{1,0:T(8,128)(2,1)} %bitcast.32, bf16[1680,512]{1,0:T(8,128)(2,1)} %get-tuple-element.57.refs_1_, bf16[512,1536]{1,0:T(8,128)(2,1)} %slice.91.refs_2_, f32[128,512]{1,0:T(8,128)} %get-tuple-element.55.vec_ref.refs_3_, bf16[1680,512]{1,0:T(8,128)(2,1)} %bitcast.43, ...), custom_call_target="tpu_custom_call" | custom-call | tf_op jit(solution)/shard_map/in_back/pallas_call | solution.py:680
  286.5 23.0 %reduce.20 = f32[16,1664]{1,0:T(8,128)} custom-call(bf16[4,2,2,2,16,1664]{5,4,3,2,1,0:T(8,128)(2,1)} %bitcast.48), custom_call_target="tpu_custom_call" | custom-call | tf_op jit(solution)/shard_map/reduce/pallas_call | solution.py:269
  309.6 0.7 slice_bitcast_fusion.1
  310.3 1.5 slice.76
  311.9 1.3 slice.92
  313.2 0.7 slice_reduce_fusion.5
  314.1 0.7 slice.94
  (44 shorter events, 5.0 us)
Async XLA Ops:
  0.7 41.1 %copy-start = (bf16[3,512,512]{2,1,0:T(8,128)(2,1)S(1)}, bf16[3,512,512]{2,1,0:T(8,128)(2,1)}, u32[]{:S(2)}) copy-start(bf16[3,512,512]{2,1,0:T(8,128)(2,1)} %refs_4_.1) | copy-start | bytes 4718596
  41.7 2.4 copy-start.9
  41.7 2.4 copy-start.10
  41.7 3.1 copy-start.6
  41.8 3.1 copy-start.4
  152.8 57.9 %copy-start.1 = (bf16[1680,512]{1,0:T(8,128)(2,1)S(1)}, bf16[1680,512]{1,0:T(8,128)(2,1)}, u32[]{:S(2)}) copy-start(bf16[1680,512]{1,0:T(8,128)(2,1)} %get-tuple-element.56) | copy-start | bytes 5160964
  210.1 59.5 %collective-permute-start.1 = (bf16[3,560,512]{2,1,0:T(8,128)(2,1)}, bf16[3,560,512]{2,1,0:T(8,128)(2,1)S(1)}, u32[]{:S(2)}, u32[]{:S(2)}) collective-permute-start(bf16[3,560,512]{2,1,0:T(8,128)(2,1)} %get-tuple-element.63), channel_id=1, source_target_pairs={{0,1},{1,0},{2,3},{3,2},{4,5},{5,4},{6,7},{7,6},{8,9},{9,8},{10,11... | collective-permute-start | bytes 5160968 | tf_op jit(solution)/shard_map/ppermute | solution.py:737
  210.2 59.4 %collective-permute-start.2 = (bf16[3,560,512]{2,1,0:T(8,128)(2,1)}, bf16[3,560,512]{2,1,0:T(8,128)(2,1)}, u32[]{:S(2)}, u32[]{:S(2)}) collective-permute-start(bf16[3,560,512]{2,1,0:T(8,128)(2,1)} %get-tuple-element.65), channel_id=1, source_target_pairs={{0,1},{1,0},{2,3},{3,2},{4,5},{5,4},{6,7},{7,6},{8,9},{9,8},{10,11... | collective-permute-start | bytes 5160968 | tf_op jit(solution)/shard_map/ppermute | solution.py:737
  211.4 56.2 %collective-permute-start = (bf16[3,48,512]{2,1,0:T(8,128)(2,1)}, bf16[3,48,512]{2,1,0:T(8,128)(2,1)}, u32[]{:S(2)}, u32[]{:S(2)}) collective-permute-start(bf16[3,48,512]{2,1,0:T(8,128)(2,1)} %get-tuple-element.82), channel_id=1, source_target_pairs={{1,0},{0,1},{3,2},{2,3},{5,4},{4,5},{7,6},{6,7},{9,8},{8,9},{11,10... | collective-permute-start | bytes 442376 | tf_op jit(solution)/shard_map/ppermute | solution.py:732
  261.1 1.3 copy-start.7
  263.0 3.4 %copy-start.8 = (f32[64,640]{1,0:T(8,128)S(1)}, f32[64,640]{1,0:T(8,128)}, u32[]{:S(2)}) copy-start(f32[64,640]{1,0:T(8,128)} %get-tuple-element.71) | copy-start | bytes 491524
  263.6 4.0 %copy-start.5 = (bf16[3,1,48,512]{3,2,0,1:T(8,128)(2,1)S(1)}, bf16[3,1,48,512]{3,2,0,1:T(8,128)(2,1)}, u32[]{:S(2)}) copy-start(bf16[3,1,48,512]{3,2,0,1:T(8,128)(2,1)} %get-tuple-element.83) | copy-start | bytes 442372
  269.6 1.2 copy-start.3
  286.5 23.0 %copy-start.2 = (bf16[1680,512]{1,0:T(8,128)(2,1)S(1)}, bf16[1680,512]{1,0:T(8,128)(2,1)}, u32[]{:S(2)}) copy-start(bf16[1680,512]{1,0:T(8,128)(2,1)} %get-tuple-element.66) | copy-start | bytes 5160964
  309.6 4.3 %collective-permute-start.3 = (bf16[3,48,512]{2,1,0:T(8,128)(2,1)S(1)}, bf16[3,48,512]{2,1,0:T(8,128)(2,1)S(1)}, u32[]{:S(2)}, u32[]{:S(2)}) collective-permute-start(bf16[3,48,512]{2,1,0:T(8,128)(2,1)S(1)} %get-tuple-element.80), channel_id=1, source_target_pairs={{1,0},{0,1},{3,2},{2,3},{5,4},{4,5},{7,6},{6,7},{9,8},{8,9},{11,10... | collective-permute-start | bytes 442376 | tf_op jit(solution)/shard_map/ppermute | solution.py:732

commit v3 on v2

v3 whole, which is shorter than its diff:
```python
import functools
import math

import jax
import jax.numpy as jnp
from jax import lax
from jax.experimental import pallas as pl
from jax.experimental.pallas import tpu as pltpu
from jax.sharding import PartitionSpec as P

HEADS = 8
EPSILON = 1e-05
NEG_FILL = -1e30
LOG2E = math.log2(math.e)
LN2 = math.log(2.0)
ROW_TILE = 16
LANES = 128
MESH = pl.DeviceIdType.MESH
f32, bf16 = jnp.float32, jnp.bfloat16

GAIN1, SHIFT1, QBIAS, VBIAS, BRANCH, GAIN2, SHIFT2, DOWNB = range(8)


def round_up(value, unit):
    return -(-value // unit) * unit


def mm(a, b):
    return lax.dot_general(a, b, (((1,), (0,)), ((), ())), preferred_element_type=f32)


def mm_t(a, b):
    return lax.dot_general(a, b, (((1,), (1,)), ((), ())), preferred_element_type=f32)


def t_mm(a, b):
    return lax.dot_general(a, b, (((0,), (0,)), ((), ())), preferred_element_type=f32)


def compiler_params(**more):
    return pltpu.CompilerParams(vmem_limit_bytes=60 * 2**20, **more)


WHOLE = pl.BlockSpec(memory_space=pltpu.VMEM)
ANY = pl.BlockSpec(memory_space=pl.ANY)


class Place:
    def __init__(self, depth, seq_size):
        self.depth, self.seq_size = depth, seq_size
        index = lax.axis_index("dp") * seq_size + lax.axis_index("seq")
        self.core = lax.rem(index, 2)
        self.x = lax.rem(index // 2, 2)
        self.y = lax.rem(index // 4, 2)
        self.z = index // 8
        core = self.core
        flip_x, flip_y = 1 - self.x, 1 - self.y
        x_first = self.x * core + flip_x * (1 - core)
        y_first = self.y * (1 - core) + flip_y * core
        x_second = self.x * (1 - core) + flip_x * core
        y_second = self.y * core + flip_y * (1 - core)
        self.columns = (
            (self.y, self.x),
            (y_first, x_first),
            (y_second, x_second),
            (flip_y, flip_x),
        )

    def device(self, z, y, x, core):
        index = ((z * 2 + y) * 2 + x) * 2 + core
        return (index // self.seq_size, lax.rem(index, self.seq_size))

    def layer(self, k):
        return lax.rem(self.z + self.depth - k, self.depth)

    def ahead(self, k):
        return lax.rem(self.z + k, self.depth)

    def first(self):
        return self.device(self.z, *self.columns[1], self.core)

    def second(self):
        return self.device(self.z, *self.columns[2], self.core)

    def other_core(self):
        return self.device(self.z, self.y, self.x, 1 - self.core)

    def above(self, k):
        return self.device(self.ahead(k), self.y, self.x, self.core)

    def mate(self, step):
        return (lax.axis_index("dp"), lax.rem(lax.axis_index("seq") + self.seq_size - step, self.seq_size))

    def octant(self, n):
        column, core = n % 4, n // 4
        y, x = self.columns[column]
        core = self.core * (1 - core) + (1 - self.core) * core
        return self.device(self.z, y, x, core), (y, x, core)

    def greet(self, corners=False):
        barrier = pltpu.get_barrier_semaphore()
        friends = [self.above(k) for k in range(1, self.depth)]
        friends += [self.octant(n)[0] for n in range(1, 8)] if corners else [self.first(), self.second(), self.other_core()]
        friends += [self.mate(step) for step in range(1, self.seq_size)]
        for friend in friends:
            pl.semaphore_signal(barrier, inc=1, device_id=friend, device_id_type=MESH)
        pl.semaphore_wait(barrier, len(friends))


def remote(src, dst, send, recv, device):
    return pltpu.make_async_remote_copy(
        src_ref=src, dst_ref=dst, send_sem=send, recv_sem=recv, device_id=device, device_id_type=MESH
    )


class Line:
    def __init__(self, place, shard, line, out, into, local):
        self.place, self.shard, self.line, self.out, self.into, self.local = place, shard, line, out, into, local

    def copy(self, k):
        return remote(self.shard, self.line.at[k], self.out.at[k], self.into.at[k], self.place.above(k))

    def start(self):
        pltpu.make_async_copy(self.shard, self.line.at[0], self.local).start()
        for k in range(1, self.place.depth):
            self.copy(k).start()

    def finish(self):
        pltpu.make_async_copy(self.shard, self.line.at[0], self.local).wait()
        for k in range(1, self.place.depth):
            self.copy(k).wait()


def line_sems(depth):
    sems = pltpu.SemaphoreType.DMA
    return [sems((depth,)), sems((depth,)), sems]


class Spread:
    def __init__(self, place, source, full, out, into, local):
        self.place, self.source, self.full, self.out, self.into, self.local = place, source, full, out, into, local

    def block(self, k, column, core):
        y, x = self.place.columns[column]
        return self.full.at[self.place.layer(k), y, x, core]

    def copy(self, src, dst, lane, k, device):
        return remote(src, dst, self.out.at[lane, k], self.into.at[lane, k], device)

    def arrived(self, lane, k, column, core):
        here = self.block(k, column, core)
        self.copy(here, here, lane, k, self.place.other_core()).wait_recv()
        return here

    def send_line(self, k):
        place, src, here = self.place, self.source(k), self.block(k, 0, self.place.core)
        self.copy(src, here, 0, k, place.first()).start()
        self.copy(src, here, 1, k, place.second()).start()
        self.copy(src, here, 3, k, place.other_core()).start()
        pltpu.make_async_copy(src, here, self.local.at[k]).start()

    def forward_first(self, k):
        here = self.arrived(0, k, 1, self.place.core)
        self.copy(here, here, 2, k, self.place.second()).start()
        self.copy(here, here, 4, k, self.place.other_core()).start()

    def forward_second(self, half, k):
        here = self.arrived(1 + half, k, 2 + half, self.place.core)
        self.copy(here, here, 5 + half, k, self.place.other_core()).start()

    def finish(self):
        for k in range(self.place.depth):
            src, here = self.source(k), self.block(k, 0, self.place.core)
            pltpu.make_async_copy(src, here, self.local.at[k]).wait()
            for column in range(4):
                self.arrived(3 + column, k, column, 1 - self.place.core)
            for lane in range(7):
                self.copy(here, here, lane, k, self.place.other_core()).wait_send()


def spread_sems(depth):
    sems = pltpu.SemaphoreType.DMA
    return [sems((7, depth)), sems((7, depth)), sems((depth,))]


class Reduce:
    def __init__(self, place, part, from_core, held, from_second, pair, from_first, line, from_line, out, into, local):
        self.place, self.part, self.local = place, part, local
        self.from_core, self.held, self.from_second, self.pair = from_core, held, from_second, pair
        self.from_first, self.line, self.from_line = from_first, line, from_line
        self.out, self.into = out, into

    def copy(self, src, dst, lane, device):
        return remote(src, dst, self.out.at[lane], self.into.at[lane], device)

    def own_copy(self):
        return pltpu.make_async_copy(self.part.at[:, :, :, self.place.core], self.held, self.local)

    def core_copy(self):
        return self.copy(self.part.at[:, :, :, 1 - self.place.core], self.from_core, 0, self.place.other_core())

    def second_copies(self):
        columns = self.place.columns
        return [
            self.copy(self.held.at[:, columns[2 + k][0], columns[2 + k][1]], self.from_second.at[k], 1 + k,
                      self.place.second())
            for k in range(2)
        ]

    def first_copy(self):
        return self.copy(self.pair.at[1], self.from_first, 3, self.place.first())

    def line_copies(self):
        place = self.place
        return [
            self.copy(self.line.at[place.ahead(k)], self.from_line.at[k - 1], 3 + k, place.above(k))
            for k in range(1, place.depth)
        ]

    def to_core(self):
        self.core_copy().start()
        self.own_copy().start()

    def to_second(self):
        self.own_copy().wait()
        self.core_copy().wait()
        self.held[...] = (self.held[...].astype(f32) + self.from_core[...].astype(f32)).astype(bf16)
        for copy in self.second_copies():
            copy.start()

    def to_first(self):
        for copy in self.second_copies():
            copy.wait()
        for k in range(2):
            y, x = self.place.columns[k]
            self.pair[k] = (self.held[:, y, x].astype(f32) + self.from_second[k].astype(f32)).astype(bf16)
        self.first_copy().start()

    def to_line(self):
        self.first_copy().wait()
        self.line[...] = (self.pair[0].astype(f32) + self.from_first[...].astype(f32)).astype(bf16)
        for copy in self.line_copies():
            copy.start()

    def last(self):
        for copy in self.line_copies():
            copy.wait()
        result = self.line[self.place.z].astype(f32)
        for k in range(self.place.depth - 1):
            result = result + self.from_line[k].astype(f32)
        return result


def reduce_scratch(depth, rows, cols):
    shapes = [(depth, 2, 2), (depth, 2, 2), (2, depth), (2, depth), (depth,), (depth,), (depth - 1,)]
    sems = pltpu.SemaphoreType.DMA
    return [pltpu.VMEM(shape + (rows, cols), bf16) for shape in shapes] + [sems((3 + depth,))] * 2 + [sems]


class ShortReduce:
    def __init__(self, place, part, from_octant, line, from_line, out, into):
        self.place, self.part, self.from_octant, self.line, self.from_line = place, part, from_octant, line, from_line
        self.out, self.into = out, into

    def octant_copy(self, n):
        device, (y, x, core) = self.place.octant(n)
        return remote(
            self.part.at[:, y, x, core], self.from_octant.at[n - 1], self.out.at[n - 1], self.into.at[n - 1], device
        )

    def line_copy(self, k):
        return remote(
            self.line.at[self.place.ahead(k)], self.from_line.at[k - 1], self.out.at[6 + k], self.into.at[6 + k],
            self.place.above(k)
        )

    def start(self):
        for n in range(1, 8):
            self.octant_copy(n).start()

    def to_line(self):
        place = self.place
        total = self.part[:, place.y, place.x, place.core].astype(f32)
        for n in range(1, 8):
            self.octant_copy(n).wait()
            total = total + self.from_octant[n - 1].astype(f32)
        self.line[...] = total.astype(bf16)
        for k in range(1, place.depth):
            self.line_copy(k).start()

    def last(self):
        total = self.line[self.place.z].astype(f32)
        for k in range(1, self.place.depth):
            self.line_copy(k).wait()
            total = total + self.from_line[k - 1].astype(f32)
        return total


def short_reduce_scratch(depth, rows, cols):
    sems = pltpu.SemaphoreType.DMA
    shapes = [(depth, 2, 2, 2), (7, depth), (depth,), (depth - 1,)]
    return [pltpu.VMEM(shape + (rows, cols), bf16) for shape in shapes] + [sems((6 + depth,))] * 2


def norm_rows(rows):
    centred = rows - jnp.mean(rows, axis=1, keepdims=True)
    inverse = lax.rsqrt(jnp.mean(centred * centred, axis=1, keepdims=True) + EPSILON)
    return centred * inverse, inverse


def norm_back(grad, scaled, inverse, gain):
    inner = grad * gain
    return inverse * (
        inner
        - jnp.mean(inner, axis=1, keepdims=True)
        - scaled * jnp.mean(inner * scaled, axis=1, keepdims=True)
    )


def gelu_both(v):
    power = jnp.exp2(v * v * (-0.5 * LOG2E))
    base = 1.0 + (0.3275911 / math.sqrt(2.0)) * jnp.abs(v)
    t = pl.reciprocal(base, approx=True)
    t = t * (2.0 - base * t)
    series = 0.5 * 1.061405429
    for factor in (-1.453152027, 1.421413741, -0.284496736, 0.254829592):
        series = series * t + 0.5 * factor
    tail = series * t * power
    cdf = jnp.where(v >= 0, 1.0 - tail, tail)
    return v * cdf, cdf + v * power * (1.0 / math.sqrt(2.0 * math.pi))


def column_sum(rows):
    return jnp.sum(rows.astype(f32), axis=0, keepdims=True)


def to_columns(rows):
    count, width = rows.shape
    return jnp.transpose(jnp.concatenate([rows, jnp.zeros((LANES - count, width), f32)], axis=0)).astype(bf16)


def own_text(ref, text, seq):
    slots, width = ref.shape
    own = jnp.zeros((text, width), ref.dtype)
    for r in range(-(-slots // text)):
        share = ref[r * text : min(slots, (r + 1) * text), :]
        if share.shape[0] < text:
            share = jnp.concatenate([share, jnp.zeros((text - share.shape[0], width), ref.dtype)], axis=0)
        own = jnp.where(seq == r, share, own)
    return own


def as_columns(vectors):
    length = vectors[0].shape[0]
    rows = [vector.reshape(1, length).astype(f32) for vector in vectors]
    rows = jnp.concatenate(rows + [jnp.zeros((LANES - len(rows), length), f32)], axis=0)
    rows = jnp.concatenate([rows, jnp.zeros((LANES, LANES - length), f32)], axis=1)
    return jnp.transpose(rows)[:length].astype(bf16)


def front_kernel(seq_size, text, width, *refs):
    shard_ref, vec_refs, up_ref, up_bias_ref, out_w_ref, down_ref, x_ref, slot_ref = (
        refs[0], refs[1:9], *refs[9:15]
    )
    outs, refs = refs[15 : 22 + 2 * seq_size], refs[22 + 2 * seq_size :]
    w_full, vecs, line_a, line_b, xtext_ref, first_ref, q_ref = outs[:7]
    k_refs, v_refs = outs[7 : 7 + seq_size], outs[7 + seq_size :]
    shard, shard_a, shard_b, line = refs[:4]
    sems, kv_out, kv_in = refs[4:-2], refs[-2], refs[-1]
    items, patch, model = x_ref.shape
    wide, units = shard_ref.shape[1], up_ref.shape[1]
    pairs = model // width
    place = Place(w_full.shape[0], seq_size)
    seq = lax.axis_index("seq")
    for p in range(pairs):
        for n in range(3):
            at = n * model + p * width
            to = (3 * p + n) * width
            shard[:, to : to + width] = shard_ref[:, at : at + width]
    shard[:, wide:] = as_columns([ref[...] for ref in vec_refs])
    place.greet()
    lines = Line(place, shard, line, *sems[:3])
    lines.start()

    def source(k):
        return line.at[k] if k else shard

    move = Spread(place, source, w_full, *sems[3:6])
    move.send_line(0)
    shard_a[:, :units] = up_ref[...]
    shard_a[:, units:] = out_w_ref[...]
    shard_b[:, :model] = down_ref[...]
    shard_b[:, model:] = as_columns([up_bias_ref[...]])
    more = [Line(place, shard_a, line_a, *sems[6:9]), Line(place, shard_b, line_b, *sems[9:12])]
    for i in range(items):
        xtext_ref[i] = own_text(slot_ref.at[i], text, seq)
    for k in range(1, place.depth):
        lines.copy(k).wait_recv()
        move.send_line(k)
    for each in more:
        each.start()
    for k in range(place.depth):
        move.forward_first(k)
    for half in range(2):
        for k in range(place.depth):
            move.forward_second(half, k)
    pltpu.make_async_copy(shard, line.at[0], lines.local).wait()
    for k in range(1, place.depth):
        lines.copy(k).wait_send()
    move.finish()
    weight = w_full[...].reshape(model, wide + LANES)
    table = jnp.transpose(weight[:, wide:].astype(f32))
    vecs[...] = table
    scale = LOG2E / math.sqrt(model // HEADS)
    copies = []
    for i in range(items):
        scaled, _ = norm_rows(jnp.concatenate([x_ref[i], xtext_ref[i]], axis=0).astype(f32))
        first_in = (scaled * table[GAIN1 : GAIN1 + 1] + table[SHIFT1 : SHIFT1 + 1]).astype(bf16)
        first_ref[i] = first_in
        for p in range(pairs):
            cols = slice(p * width, (p + 1) * width)
            projected = mm(first_in, weight[:, 3 * p * width : 3 * (p + 1) * width])
            q_ref[i, :, cols] = ((projected[:, :width] + table[QBIAS : QBIAS + 1, cols]) * scale).astype(bf16)
            k_refs[0][i, :, cols] = projected[:, width : 2 * width].astype(bf16)
            v_refs[0][i, :, cols] = (projected[:, 2 * width :] + table[VBIAS : VBIAS + 1, cols]).astype(bf16)
        for r in range(1, seq_size):
            for n, ref in enumerate((k_refs, v_refs)):
                at = (2 * i + n) * seq_size + r
                copies.append(remote(ref[0].at[i], ref[r].at[i], kv_out.at[at], kv_in.at[at], place.mate(r)))
                copies[-1].start()
    for each in more:
        each.finish()
    for copy in copies:
        copy.wait()


def front(in_weight, vectors, up_weight, up_bias, out_weight, down_weight, patches, text_rows, text, width, devices,
          seq_size):
    items, patch, model = patches.shape
    depth = devices // 8
    rows, cols = in_weight.shape
    shape_a = (rows, up_weight.shape[1] + model)
    shape_b = (down_weight.shape[0], model + LANES)
    tokens = jax.ShapeDtypeStruct((items, patch + text, model), bf16)
    sems = pltpu.SemaphoreType.DMA
    outs = pl.pallas_call(
        functools.partial(front_kernel, seq_size, text, width),
        in_specs=[WHOLE] * 15,
        out_specs=[WHOLE] * 2 + [ANY] * 2 + [WHOLE] * (3 + 2 * seq_size),
        out_shape=[
            jax.ShapeDtypeStruct((depth, 2, 2, 2, rows, cols + LANES), bf16),
            jax.ShapeDtypeStruct((LANES, model), f32),
            jax.ShapeDtypeStruct((depth,) + shape_a, bf16),
            jax.ShapeDtypeStruct((depth,) + shape_b, bf16),
            jax.ShapeDtypeStruct((items, text, model), bf16),
            tokens,
            tokens,
        ]
        + [tokens] * (2 * seq_size),
        scratch_shapes=[
            pltpu.VMEM((rows, cols + LANES), bf16),
            pltpu.VMEM(shape_a, bf16),
            pltpu.VMEM(shape_b, bf16),
            pltpu.VMEM((depth, rows, cols + LANES), bf16),
        ]
        + line_sems(depth)
        + spread_sems(depth)
        + line_sems(depth) * 2
        + [sems((2 * items * seq_size,)), sems((2 * items * seq_size,))],
        compiler_params=compiler_params(collective_id=0, has_side_effects=True),
        name="front",
    )(in_weight, *vectors, up_weight, up_bias, out_weight, down_weight, patches, text_rows)
    full = outs[0].reshape(model, cols + LANES)
    return full, outs[1], outs[2:4], outs[4], outs[5], outs[6], outs[7 : 7 + seq_size], outs[7 + seq_size :]


def collect(dst, refs, patch, text):
    count, width = len(refs), refs[0].shape[2]
    for r, ref in enumerate(refs):
        dst[r * patch : (r + 1) * patch, :width] = ref[0, :patch, :]
        at = count * patch + r * text
        dst[at : at + text, :width] = ref[0, patch:, :]
    filled = count * (patch + text)
    if dst.shape[0] > filled:
        dst[filled:, :width] = jnp.zeros((dst.shape[0] - filled, width), dst.dtype)


def spread_turns(move, depth):
    turns = {}

    def add(turn, *action):
        turns.setdefault(turn, []).append(action)

    for k in range(depth):
        quarter = 4 * k // depth
        add((2, 3, 4, 5)[quarter], move.forward_first, k)
        add((3, 4, 5, 6)[quarter], move.forward_second, 0, k)
        add((6, 7, 8, 9)[quarter], move.forward_second, 1, k)
    return turns


def attend_kernel(count, patch, head, seq_size, *refs):
    q_ref, k_refs, v_refs = refs[0], refs[1 : 1 + count], refs[1 + count : 1 + 2 * count]
    bias_ref, line_a, line_b, out_ref, rest_ref, log_ref, full_a, full_b = refs[1 + 2 * count : 9 + 2 * count]
    keys, values, *sems = refs[9 + 2 * count :]
    width = q_ref.shape[2]
    text = q_ref.shape[1] - patch
    place = Place(full_a.shape[0], seq_size)
    turn = pl.program_id(0) * pl.num_programs(1) + pl.program_id(1)
    last = pl.num_programs(0) * pl.num_programs(1) - 1
    moves = [
        Spread(place, lambda k: line_a.at[k], full_a, *sems[:3]),
        Spread(place, lambda k: line_b.at[k], full_b, *sems[3:]),
    ]

    @pl.when(turn == 0)
    def _():
        place.greet()
        for k in range(place.depth):
            for move in moves:
                move.send_line(k)

    turns = [spread_turns(move, place.depth) for move in moves]
    for at in sorted(turns[0]):

        @pl.when(turn == at)
        def _(at=at):
            for pair in zip(*[each[at] for each in turns]):
                for action in pair:
                    action[0](*action[1:])

    collect(keys, k_refs, patch, text)
    collect(values, v_refs, patch, text)
    values[:, width:] = jnp.ones((values.shape[0], values.shape[1] - width), bf16)
    q = q_ref[0]
    lane = lax.broadcasted_iota(jnp.int32, (1, width), 1) // head
    out = logs = None
    for h in range(width // head):
        q_head = jnp.where(lane == h, q, jnp.zeros_like(q))
        scores = mm_t(q_head, keys[...]) + bias_ref[0]
        top = jnp.max(scores, axis=1, keepdims=True)
        powers = jnp.exp2(scores - top).astype(bf16)
        mixed = mm(powers, values[...])
        total = mixed[:, width:]
        head_out = mixed[:, :width] * (1.0 / total)
        head_log = top + jnp.log2(total)
        out = head_out if out is None else jnp.where(lane == h, head_out, out)
        logs = head_log if logs is None else jnp.where(lane == h, head_log, logs)
    high = out.astype(bf16)
    out_ref[0] = high
    rest_ref[0] = (out - high.astype(f32)).astype(bf16)
    log_ref[0] = logs

    @pl.when(turn == last)
    def _():
        for move in moves:
            move.finish()


def attend(q, keys, values, bias, lines, patch, head, width, devices, seq_size):
    items, _, model = q.shape
    count, span = len(keys), bias.shape[-1]
    depth = devices // 8
    block = pl.BlockSpec((1, q.shape[1], width), lambda i, p: (i, 0, p))
    outs = pl.pallas_call(
        functools.partial(attend_kernel, count, patch, head, seq_size),
        grid=(items, model // width),
        in_specs=[block] * (1 + 2 * count) + [pl.BlockSpec((1, 1, span), lambda i, p: (i, 0, 0))] + [ANY] * 2,
        out_specs=[block, block, block, ANY, ANY],
        out_shape=[jax.ShapeDtypeStruct(q.shape, bf16)] * 2
        + [jax.ShapeDtypeStruct(q.shape, f32)]
        + [jax.ShapeDtypeStruct((depth, 2, 2, 2) + line.shape[1:], line.dtype) for line in lines],
        scratch_shapes=[pltpu.VMEM((span, width), bf16), pltpu.VMEM((span, 2 * width), bf16)]
        + spread_sems(depth) * 2,
        compiler_params=compiler_params(collective_id=1, has_side_effects=True),
        name="attend",
    )(q, *keys, *values, bias, *lines)
    return outs[0], outs[1], outs[2], [full.reshape(-1, full.shape[-1]) for full in outs[3:]]


def ffn_kernel(steps, chunk, seq_ref, x_ref, xtext_ref, at_ref, dy_ref, dy_slot_ref, w_ref, wd_ref, vec_ref,
               res_ref, restext_ref, gb_ref, ga_ref, part_ref, down_ref,
               second_s, hidden_s, pre_s, dy_s, sums_s, bias_s, out_s):
    step = pl.program_id(0)
    patch, model = x_ref.shape[1:]
    text = xtext_ref.shape[1]
    block, units = patch + text, wd_ref.shape[0]
    rows = pl.ds(pl.multiple_of(step * block, ROW_TILE), block)
    gain = vec_ref[GAIN2 : GAIN2 + 1]
    w_out = w_ref[:, units:]

    @pl.when(step == 0)
    def _():
        sums_s[...] = jnp.zeros_like(sums_s)
        bias_s[...] = jnp.transpose(wd_ref[:, model:].astype(f32))[:8]

    x = jnp.concatenate([x_ref[0], xtext_ref[0]], axis=0).astype(f32)
    dy = jnp.concatenate([dy_ref[0], own_text(dy_slot_ref.at[0], text, seq_ref[0])], axis=0)
    dy_s[rows, :] = dy
    middle = x + (mm(at_ref[0], w_out) + vec_ref[BRANCH : BRANCH + 1])
    scaled, inverse = norm_rows(middle)
    second_in = (scaled * gain + vec_ref[SHIFT2 : SHIFT2 + 1]).astype(bf16)
    second_s[rows, :] = second_in
    result = middle + vec_ref[DOWNB : DOWNB + 1]
    grad_second = jnp.zeros_like(middle)
    for c in range(units // chunk):
        cols = slice(c * chunk, (c + 1) * chunk)
        value, slope = gelu_both(mm(second_in, w_ref[:, cols]) + bias_s[:1, cols])
        hidden = value.astype(bf16)
        hidden_s[rows, cols] = hidden
        grad_pre = (mm_t(dy, wd_ref[cols, :model]) * slope).astype(bf16)
        pre_s[rows, cols] = grad_pre
        result = result + mm(hidden, wd_ref[cols, :model])
        grad_second = grad_second + mm_t(grad_pre, w_ref[:, cols])
    result = result.astype(bf16)
    res_ref[0] = result[:patch]
    restext_ref[0] = result[patch:]
    grad_branch = (dy.astype(f32) + norm_back(grad_second, scaled, inverse, gain)).astype(bf16)
    gb_ref[0] = grad_branch
    ga_ref[0] = mm_t(grad_branch, w_out).astype(bf16)
    out_grad = t_mm(at_ref[0], grad_branch)

    @pl.when(step == 0)
    def _():
        out_s[...] = out_grad

    @pl.when(step > 0)
    def _():
        out_s[...] += out_grad

    for at, grad in ((BRANCH, grad_branch), (GAIN2, grad_second * scaled), (SHIFT2, grad_second), (DOWNB, dy)):
        sums_s[at : at + 1, :] += column_sum(grad)

    @pl.when(step == steps - 1)
    def _():
        for c in range(units // model):
            cols = slice(c * model, (c + 1) * model)
            grad_pre = pre_s[:, cols]
            part_ref[:, cols] = t_mm(second_s[...], grad_pre).astype(bf16)
            down_ref[cols, :model] = jnp.transpose(t_mm(dy_s[...], hidden_s[:, cols])).astype(bf16)
            down_ref[cols, model:] = to_columns(column_sum(grad_pre))
        part_ref[:, units : units + model] = out_s[...].astype(bf16)
        part_ref[:, units + model :] = to_columns(sums_s[...])


def ffn(seq, patches, x_text, attended, patch_cotangent, text_cotangent, weights, w_down, vecs):
    items, patch, model = patches.shape
    units, rows, text, slots = w_down.shape[0], attended.shape[1], x_text.shape[1], text_cotangent.shape[1]

    def item(count):
        return pl.BlockSpec((1, count, model), lambda i: (i, 0, 0))

    def shape(count):
        return jax.ShapeDtypeStruct((items, count, model), bf16)

    return pl.pallas_call(
        functools.partial(ffn_kernel, items, 512),
        grid=(items,),
        in_specs=[pl.BlockSpec(memory_space=pltpu.SMEM)]
        + [item(patch), item(text), item(rows), item(patch), item(slots)]
        + [WHOLE] * 3,
        out_specs=[item(patch), item(text), item(rows), item(rows), WHOLE, WHOLE],
        out_shape=[shape(patch), shape(text), shape(rows), shape(rows)]
        + [
            jax.ShapeDtypeStruct((model, units + model + LANES), bf16),
            jax.ShapeDtypeStruct((units, model + LANES), bf16),
        ],
        scratch_shapes=[
            pltpu.VMEM((items * rows, model), bf16),
            pltpu.VMEM((items * rows, units), bf16),
            pltpu.VMEM((items * rows, units), bf16),
            pltpu.VMEM((items * rows, model), bf16),
            pltpu.VMEM((8, model), f32),
            pltpu.VMEM((8, units), f32),
            pltpu.VMEM((model, model), f32),
        ],
        compiler_params=compiler_params(),
        name="ffn",
    )(seq, patches, x_text, attended, patch_cotangent, text_cotangent, weights, w_down, vecs)


def back_kernel(count, patch, head, seq_size, pairs, items, *refs):
    refs = list(refs)

    def take(number):
        taken = refs[:number]
        del refs[:number]
        return taken

    (q_ref,), k_refs, v_refs = take(1), take(count), take(count)
    bias_ref, log_ref, at_ref, rest_ref, grad_ref = take(5)
    part_a, part_b, w_any, vec_ref, first_any, x_any, xtext_any, gb_any, restext_any = take(9)
    grad_out, text_grad_out, text_out, total_a, total_b, total_in, vec_out, vec2_out, upb_out = take(9)
    keys, values, mixed_s, own_s, dkv_out, dkv_in, sums_s, gacc_s = take(8)
    w_s, first_s, x_s, xtext_s, gb_s, text_s = take(6)
    fetch_sem, dkv_sem, dkv_in_sem, text_sem, text_in_sem = take(5)
    scratch_a, scratch_b = take(10), take(10)
    scratch_in = [take(11) for _ in range(pairs)]
    scratch_vec = take(6)

    width, rows = q_ref.shape[2], q_ref.shape[1]
    text, model = rows - patch, pairs * width
    place = Place(part_a.shape[0], seq_size)
    seq = lax.axis_index("seq")
    p, i = pl.program_id(0), pl.program_id(1)
    turn, last = p * items + i, pairs * items - 1
    sums_a, sums_b = Reduce(place, part_a, *scratch_a), Reduce(place, part_b, *scratch_b)
    sums_in = [Reduce(place, each[0], *each[1:]) for each in scratch_in]
    sums_vec = ShortReduce(place, *scratch_vec)
    fetches = [
        pltpu.make_async_copy(src, dst, fetch_sem.at[n])
        for n, (src, dst) in enumerate(
            ((w_any, w_s), (first_any, first_s), (x_any, x_s), (xtext_any, xtext_s), (gb_any, gb_s))
        )
    ]

    def text_copies(src, dst, row):
        to = dst.at[:, pl.ds(pl.multiple_of(seq * text, ROW_TILE), text)]
        own = pltpu.make_async_copy(src, to, text_sem.at[row, 0])
        away = [
            remote(src, to, text_sem.at[row, r], text_in_sem.at[row, r], place.mate(r)) for r in range(1, seq_size)
        ]
        return [own] + away

    def dkv_copy(slot, r):
        return remote(
            dkv_out.at[slot, r - 1], dkv_in.at[slot, r - 1], dkv_sem.at[slot, r - 1], dkv_in_sem.at[slot, r - 1],
            place.mate(-r)
        )

    def settle(of):
        slot, pair, item = lax.rem(of, 2), of // items, lax.rem(of, items)
        total = own_s[slot]
        for r in range(1, seq_size):
            dkv_copy(slot, r).wait_recv()
            total = total + dkv_in[slot, r - 1].astype(f32)
        at = pl.ds(pl.multiple_of(item * rows, ROW_TILE), rows)
        mixed_s[lax.rem(pair, 2), at, width:] = total.astype(bf16)

    def pair_done(pair):
        mixed = mixed_s[pair % 2]
        if pair == 0:
            fetches[0].wait()
            fetches[1].wait()
        grad = t_mm(first_s[...].reshape(items * rows, model), mixed).astype(bf16)
        sums_in[pair].part[...] = grad.reshape(sums_in[pair].part.shape)
        sums_in[pair].to_core()
        back = mm_t(mixed, w_s[:, 3 * pair * width : 3 * (pair + 1) * width])
        gacc_s[...] = back if pair == 0 else gacc_s[...] + back
        cols = slice(pair * width, (pair + 1) * width)
        sums_s[QBIAS : QBIAS + 1, cols] = column_sum(mixed[:, :width])
        sums_s[VBIAS : VBIAS + 1, cols] = column_sum(mixed[:, 2 * width :])

    def finish_in(pair):
        total = sums_in[pair].last()
        for n in range(3):
            at = n * model + pair * width
            total_in[:, at : at + width] = total[:, n * width : (n + 1) * width]

    def finish_a():
        total = sums_a.last()
        total_a[...] = total[:, : total_a.shape[1]]
        vec2_out[...] = total[:, total_a.shape[1] :]

    def finish_b():
        total = sums_b.last()
        total_b[...] = total[:, :model]
        upb_out[...] = total[:, model:]

    agenda = [(2, sums_a.to_second), (2, sums_b.to_second), (6, sums_a.to_first), (6, sums_b.to_first),
              (8, sums_a.to_line), (8, sums_b.to_line)]
    for pair in range(pairs):
        done = items * (pair + 1)
        steps = (sums_in[pair].to_second, sums_in[pair].to_first, sums_in[pair].to_line, functools.partial(finish_in, pair))
        agenda += [(done + 1 + n, step) for n, step in enumerate(steps)]
    agenda += [(last + 2, finish_a), (last + 3, finish_b)]
    agenda.sort(key=lambda entry: entry[0])

    @pl.when(turn == 0)
    def _():
        place.greet(corners=True)
        sums_a.to_core()
        sums_b.to_core()
        for copy in fetches:
            copy.start()
        for copy in text_copies(restext_any, text_out, 0):
            copy.start()
        sums_s[...] = jnp.zeros_like(sums_s)

    for at in sorted({at for at, _ in agenda if at <= last}):

        @pl.when(turn == at)
        def _(at=at):
            for when, step in agenda:
                if when == at:
                    step()

    collect(keys, k_refs, patch, text)
    collect(values, v_refs, patch, text)
    q, grad = q_ref[0], grad_ref[0]
    lane = lax.broadcasted_iota(jnp.int32, (1, width), 1) // head
    row = lax.broadcasted_iota(jnp.int32, (width, 1), 0) // head
    inner = grad.astype(f32) * (at_ref[0].astype(f32) + rest_ref[0].astype(f32))
    dq = dk = dv = None
    for h in range(width // head):
        mine = lane == h
        q_head = jnp.where(mine, q, jnp.zeros_like(q))
        grad_head = jnp.where(mine, grad, jnp.zeros_like(grad))
        delta = jnp.sum(jnp.where(mine, inner, 0.0), axis=1, keepdims=True)
        scores = mm_t(q_head, keys[...]) + bias_ref[0]
        probs = jnp.exp2(scores - log_ref[0, :, h * head : h * head + 1])
        grad_probs = mm_t(grad_head, values[...])
        grad_scores = (probs * (grad_probs - delta)).astype(bf16)
        dv_head = t_mm(grad, probs.astype(bf16))
        dk_head = t_mm(q, grad_scores)
        dq_head = mm(grad_scores, keys[...])
        dq = dq_head if dq is None else jnp.where(mine, dq_head, dq)
        dk = dk_head if dk is None else jnp.where(row == h, dk_head, dk)
        dv = dv_head if dv is None else jnp.where(row == h, dv_head, dv)
    dk, dv = jnp.transpose(dk * LN2), jnp.transpose(dv)
    slot = lax.rem(turn, 2)
    at = pl.ds(pl.multiple_of(i * rows, ROW_TILE), rows)
    mixed_s[lax.rem(p, 2), at, :width] = (dq * (1.0 / math.sqrt(head))).astype(bf16)
    own_s[slot, :patch, :width] = dk[:patch]
    own_s[slot, :patch, width:] = dv[:patch]
    first_text = count * patch
    own_s[slot, patch:, :width] = dk[first_text : first_text + text]
    own_s[slot, patch:, width:] = dv[first_text : first_text + text]

    @pl.when(turn > 0)
    def _():
        settle(turn - 1)

    @pl.when(turn > 1)
    def _():
        for r in range(1, seq_size):
            dkv_copy(slot, r).wait_send()

    for r in range(1, seq_size):
        at_text = first_text + r * text
        for n, part in enumerate((dk, dv)):
            cols = slice(n * width, (n + 1) * width)
            dkv_out[slot, r - 1, :patch, cols] = part[r * patch : (r + 1) * patch].astype(bf16)
            dkv_out[slot, r - 1, patch:, cols] = part[at_text : at_text + text].astype(bf16)
        dkv_copy(slot, r).start()

    for pair in range(pairs - 1):

        @pl.when(turn == items * (pair + 1))
        def _(pair=pair):
            pair_done(pair)

    @pl.when(turn == last)
    def _():
        left = [step for when, step in agenda if when > last]
        settle(last)
        pair_done(pairs - 1)
        for copy in fetches[2:]:
            copy.wait()
        gain = vec_ref[GAIN1 : GAIN1 + 1]
        for item in range(items):
            grad_first = gacc_s[item * rows : (item + 1) * rows, :]
            scaled, inverse = norm_rows(jnp.concatenate([x_s[item], xtext_s[item]], axis=0).astype(f32))
            grad_rows = gb_s[item].astype(f32) + norm_back(grad_first, scaled, inverse, gain)
            grad_rows = grad_rows.astype(bf16)
            grad_out[item] = grad_rows[:patch]
            text_s[item] = grad_rows[patch:]
            sums_s[GAIN1 : GAIN1 + 1, :] += column_sum(grad_first * scaled)
            sums_s[SHIFT1 : SHIFT1 + 1, :] += column_sum(grad_first)
            if left:
                left.pop(0)()
        for copy in text_copies(text_s, text_grad_out, 1):
            copy.start()
        sums_vec.part[...] = to_columns(sums_s[...]).reshape(sums_vec.part.shape)
        sums_vec.start()
        if left:
            left.pop(0)()
        sums_vec.to_line()
        for step in left:
            step()
        vec_out[...] = sums_vec.last()
        for copies in (text_copies(restext_any, text_out, 0), text_copies(text_s, text_grad_out, 1)):
            for copy in copies:
                copy.wait()
        for slot in range(2):
            for r in range(1, seq_size):
                dkv_copy(slot, r).wait_send()


def back(q, keys, values, bias, logs, attended, rest, grad_att, part_a, part_b, w_in, vecs, first_in, patches, x_text,
         grad_branch, res_text, head, width, devices, seq_size):
    items, patch, model = patches.shape
    rows, text = q.shape[1], x_text.shape[1]
    count, span, pairs, depth = len(keys), bias.shape[-1], model // width, devices // 8
    block = pl.BlockSpec((1, rows, width), lambda p, i: (i, 0, p))
    parts = [part.reshape((depth, 2, 2, 2, part.shape[0] // devices, part.shape[1])) for part in (part_a, part_b)]
    (rows_a, cols_a), (rows_b, cols_b) = parts[0].shape[4:], parts[1].shape[4:]
    sems = pltpu.SemaphoreType.DMA
    others = seq_size - 1
    slots = jax.ShapeDtypeStruct((items, seq_size * text, model), bf16)
    scratch_in = [pltpu.VMEM((depth, 2, 2, 2, rows_a, 3 * width), bf16)] + reduce_scratch(depth, rows_a, 3 * width)
    return pl.pallas_call(
        functools.partial(back_kernel, count, patch, head, seq_size, pairs, items),
        grid=(pairs, items),
        in_specs=[block] * (1 + 2 * count)
        + [pl.BlockSpec((1, 1, span), lambda p, i: (i, 0, 0))]
        + [block] * 4
        + [ANY] * 3
        + [WHOLE]
        + [ANY] * 5,
        out_specs=[WHOLE] + [ANY] * 2 + [WHOLE] * 6,
        out_shape=[
            jax.ShapeDtypeStruct(patches.shape, bf16),
            slots,
            slots,
            jax.ShapeDtypeStruct((rows_a, cols_a - LANES), f32),
            jax.ShapeDtypeStruct((rows_b, cols_b - LANES), f32),
            jax.ShapeDtypeStruct((rows_a, 3 * model), f32),
            jax.ShapeDtypeStruct((rows_a, LANES), f32),
            jax.ShapeDtypeStruct((rows_a, LANES), f32),
            jax.ShapeDtypeStruct((rows_b, LANES), f32),
        ],
        scratch_shapes=[
            pltpu.VMEM((span, width), bf16),
            pltpu.VMEM((span, width), bf16),
            pltpu.VMEM((2, items * rows, 3 * width), bf16),
            pltpu.VMEM((2, rows, 2 * width), f32),
            pltpu.VMEM((2, others, rows, 2 * width), bf16),
            pltpu.VMEM((2, others, rows, 2 * width), bf16),
            pltpu.VMEM((8, model), f32),
            pltpu.VMEM((items * rows, model), f32),
            pltpu.VMEM(w_in.shape, bf16),
            pltpu.VMEM(first_in.shape, bf16),
            pltpu.VMEM(patches.shape, bf16),
            pltpu.VMEM(x_text.shape, bf16),
            pltpu.VMEM(grad_branch.shape, bf16),
            pltpu.VMEM(x_text.shape, bf16),
            sems((5,)),
            sems((2, others)),
            sems((2, others)),
            sems((2, seq_size)),
            sems((2, seq_size)),
        ]
        + reduce_scratch(depth, rows_a, cols_a)
        + reduce_scratch(depth, rows_b, cols_b)
        + scratch_in * pairs
        + short_reduce_scratch(depth, rows_a, LANES),
        compiler_params=compiler_params(collective_id=2, has_side_effects=True),
        name="back",
    )(q, *keys, *values, bias, logs, attended, rest, grad_att, *parts, w_in, vecs, first_in, patches, x_text,
      grad_branch, res_text)


def per_device(
    seq_size,
    devices,
    patches,
    text_rows,
    lengths,
    first_gain,
    first_shift,
    in_weight,
    query_bias,
    value_bias,
    out_weight,
    branch_bias,
    second_gain,
    second_shift,
    up_weight,
    up_bias,
    down_weight,
    down_bias,
    patch_cotangent,
    text_cotangent,
):
    items, patch, model = patches.shape
    slots = text_rows.shape[1]
    units = up_weight.shape[1]
    head = model // HEADS
    width = min(LANES, model)
    text = round_up(-(-slots // seq_size), ROW_TILE)
    seq = lax.axis_index("seq")
    vectors = [first_gain, first_shift, query_bias, value_bias, branch_bias, second_gain, second_shift, down_bias]
    in_full, vecs, lines, x_text, first_in, q, keys, values = front(
        in_weight, vectors, up_weight, up_bias, out_weight, down_weight, patches, text_rows, text, width, devices,
        seq_size
    )

    spans = []
    for r in range(seq_size):
        slot = lax.rem(seq + r, seq_size) * text + jnp.arange(text)
        spans.append(slot[None, :] < lengths[:, None])
    valid = jnp.concatenate([jnp.ones((items, patch * seq_size), jnp.bool_)] + spans, axis=1)
    span = round_up(valid.shape[1], LANES)
    valid = jnp.pad(valid, ((0, 0), (0, span - valid.shape[1])))
    bias = jnp.where(valid, 0.0, NEG_FILL).astype(f32)[:, None, :]

    attended, rest, logs, (weights, w_down) = attend(
        q, keys, values, bias, lines, patch, head, width, devices, seq_size
    )
    out_patches, res_text, grad_branch, grad_att, part_a, part_b = ffn(
        seq[None], patches, x_text, attended, patch_cotangent, text_cotangent, weights, w_down, vecs
    )
    grad_patches, grad_text, out_text, sums, down_grad, in_grad, vec1, vec2, up_bias_grad = back(
        q, keys, values, bias, logs, attended, rest, grad_att, part_a, part_b, in_full, vecs, first_in, patches, x_text,
        grad_branch, res_text, head, width, devices, seq_size
    )
    return (
        out_patches,
        out_text[:, :slots],
        grad_patches,
        grad_text[:, :slots],
        vec1[:, GAIN1],
        vec1[:, SHIFT1],
        in_grad,
        vec1[:, QBIAS],
        vec1[:, VBIAS],
        sums[:, units:],
        vec2[:, BRANCH],
        vec2[:, GAIN2],
        vec2[:, SHIFT2],
        sums[:, :units],
        up_bias_grad[:, 0],
        down_grad,
        vec2[:, DOWNB],
    )


def solution(mesh):
    both = ("dp", "seq")
    rows, slots, vector, matrix = P("dp", "seq", None), P("dp", None, None), P(both), P(both, None)
    weights = (vector, vector, matrix, vector, vector, matrix, vector, vector, vector, matrix, vector, matrix, vector)
    return jax.shard_map(
        functools.partial(per_device, mesh.shape["seq"], mesh.size),
        mesh=mesh,
        in_specs=(rows, slots, P("dp")) + weights + (rows, slots),
        out_specs=(rows, slots, rows, slots) + weights,
        check_vma=False,
    )
```

time: 320 us -> 248 us (0.78); the launches traced: 315 us -> 247 us
  Pallas kernels: 284 us -> 229 us
  local copies, waits for them, and re-layouts: 22.3 us -> 15.5 us
  other arithmetic: 6.66 us -> 0.75 us
    pallas_call x6 -> x3, Pallas kernels: 234 us -> 186 us  [the longest x1 95.2 us: back(): pl.pallas_call(functools.partial(back_kernel, count, patch, head, seq_siz...]
    pallas_call x1, Pallas kernels: 50 us -> 43.3 us  [attend(): pl.pallas_call(functools.partial(attend_kernel, count, patch, head, seq_s...]
    concatenate x1 -> x0, local copies, waits for them, and re-layouts: 5.94 us -> none  [per_device(): jnp.concatenate(vectors)[None]]
    concatenate x5 -> x0, other arithmetic: 5.8 us -> none  [the longest x1 2.38 us: per_device(): x = jnp.concatenate([patches, x_text], axis=1)]
    slice x13 -> x6, local copies, waits for them, and re-layouts: 12.3 us -> 9.26 us  [the longest x1 1.69 us: per_device(): grad_text[:, :slots]]
  transfers between devices with their start and end apart: 4 -> 0, of which waited for: 0 -> 0; matrix products, arithmetic and copies ran while one was open for 5% -> 0% of each run, Pallas kernels for 15% -> 0%
where the time goes in v3:
time: 248 us; the launch traced here: 247 us
  Pallas kernels  229 us (92%)
  local copies, waits for them, and re-layouts  15.5 us (6%)
    pallas_call x1, Pallas kernels, back(): pl.pallas_call(functools.partial(back_kernel, count, patch, head, seq_siz...  95.2 us
    pallas_call x1, Pallas kernels, ffn(): pl.pallas_call(functools.partial(ffn_kernel, items, 512), grid=(items,),...  56.2 us
    pallas_call x1, Pallas kernels, attend(): pl.pallas_call(functools.partial(attend_kernel, count, patch, head, seq_s...  43.3 us
    pallas_call x1, Pallas kernels, front(): pl.pallas_call(functools.partial(front_kernel, seq_size, text, width), in...  34.7 us

profile of v3, /device:TPU:0, one launch (start us, length us, event | category | flops | bytes accessed | tf_op | source)
XLA Modules:
  0.0 246.6 jit_solution(9995065475223298515)
XLA Ops:
  0.7 0.7 broadcast_compare_fusion
  1.4 0.1 concatenate.3
  1.5 0.6 broadcast_in_dim.25.refs_5_
  2.1 34.7 %front.1 = (bf16[4,2,2,2,16,1664]{5,4,3,2,1,0:T(8,128)(2,1)}, f32[128,512]{1,0:T(8,128)}, bf16[4,16,2560]{2,1,0:T(8,128)(2,1)}, bf16[4,64,640]{2,1,0:T(8,128)(2,...) custom-call(bf16[16,1536]{1,0:T(8,128)(2,1)} %refs_0_.1, ...), custom_call_target="tpu_custom_call" | custom-call | tf_op jit(solution)/shard_map/front/pallas_call | solution.py:446
  36.9 43.3 %attend.1 = (bf16[3,560,512]{2,1,0:T(8,128)(2,1)}, bf16[3,560,512]{2,1,0:T(8,128)(2,1)}, f32[3,560,512]{2,1,0:T(8,128)}, bf16[4,2,2,2,16,2560]{5,4,3,2,1,0:T(8,128)(2,1)}, bf16[4,2,2,2,64,640]{5,4,3,2,1,0:T(8,128)(2,1)}) custom-call(bf16[3,560,512]{2,1,0:T(8,128)(2,1)} %get-tuple-element.49.refs_0_, bf16[3,560,512]{2,1,0:T(8,128)(2,1)} %get-tuple-element.50.refs_1_, ...), custom_call_target="tpu_custom_call" | custom-call | tf_op jit(solution)/shard_map/attend/pallas_call | solution.py:565
  80.2 56.2 %ffn.1 = (bf16[3,512,512]{2,1,0:T(8,128)(2,1)}, bf16[3,48,512]{2,1,0:T(8,128)(2,1)}, bf16[3,560,512]{2,1,0:T(8,128)(2,1)}, bf16[3,560,512]{2,1,0:T(8,128)(2,1)},...) custom-call(s32[1]{0:T(128)} %bitcast.seq_ref, bf16[3,512,512]{2,1,0:T(8,128)(2,1)} %refs_15_.1, ...), custom_call_target="tpu_custom_call" | custom-call | tf_op jit(solution)/shard_map/ffn/pallas_call | solution.py:656
  136.4 95.2 %back.1 = (bf16[3,512,512]{2,1,0:T(8,128)(2,1)}, bf16[3,96,512]{2,1,0:T(8,128)(2,1)}, bf16[3,96,512]{2,1,0:T(8,128)(2,1)}, f32[16,2560]{1,0:T(8,128)}, f32[64,51...) custom-call(bf16[3,560,512]{2,1,0:T(8,128)(2,1)} %get-tuple-element.49.refs_0_,, ...), custom_call_target="tpu_custom_call" | custom-call | tf_op jit(solution)/shard_map/back/pallas_call | solution.py:902
  231.6 1.7 slice.39
  233.2 1.4 slice_reduce_fusion
  234.6 1.6 slice_reduce_fusion.5
  236.2 1.6 slice_reduce_fusion.1
  237.8 1.4 slice.45
  239.1 1.6 slice.49
  240.7 0.0 copy-start.1
  240.7 1.7 slice.40
  242.4 0.0 copy-start
  242.4 2.7 %copy.38 = bf16[3,512,512]{2,1,0:T(8,128)(2,1)} copy(bf16[3,512,512]{2,1,0:T(8,128)(2,1)} %get-tuple-element.110) | data formatting | bytes 3145728
  245.1 0.0 copy-done.1
  245.1 0.6 copy.39
  245.7 0.0 copy-done
  245.7 0.7 copy.40
  (3 shorter events, 0.0 us)
Async XLA Ops:
  240.7 4.4 %copy-start.1 = (f32[16,1536]{1,0:T(8,128)S(1)}, f32[16,1536]{1,0:T(8,128)}, u32[]{:S(2)}) copy-start(f32[16,1536]{1,0:T(8,128)} %get-tuple-element.114) | copy-start | bytes 294916
  242.4 3.3 %copy-start = (f32[64,512]{1,0:T(8,128)S(1)}, f32[64,512]{1,0:T(8,128)}, u32[]{:S(2)}) copy-start(f32[64,512]{1,0:T(8,128)} %get-tuple-element.123) | copy-start | bytes 393220

commit v4 on v3

v4 whole, which is shorter than its diff:
```python
import functools
import math

import jax
import jax.numpy as jnp
from jax import lax
from jax.experimental import pallas as pl
from jax.experimental.pallas import tpu as pltpu
from jax.sharding import PartitionSpec as P

HEADS = 8
EPSILON = 1e-05
NEG_FILL = -1e30
LOG2E = math.log2(math.e)
LN2 = math.log(2.0)
ROW_TILE = 16
LANES = 128
MESH = pl.DeviceIdType.MESH
f32, bf16 = jnp.float32, jnp.bfloat16

GAIN1, SHIFT1, QBIAS, VBIAS, BRANCH, GAIN2, SHIFT2, DOWNB = range(8)


def round_up(value, unit):
    return -(-value // unit) * unit


def mm(a, b):
    return lax.dot_general(a, b, (((1,), (0,)), ((), ())), preferred_element_type=f32)


def mm_t(a, b):
    return lax.dot_general(a, b, (((1,), (1,)), ((), ())), preferred_element_type=f32)


def t_mm(a, b):
    return lax.dot_general(a, b, (((0,), (0,)), ((), ())), preferred_element_type=f32)


def compiler_params(**more):
    return pltpu.CompilerParams(vmem_limit_bytes=60 * 2**20, **more)


WHOLE = pl.BlockSpec(memory_space=pltpu.VMEM)
ANY = pl.BlockSpec(memory_space=pl.ANY)


class Place:
    def __init__(self, depth, seq_size):
        self.depth, self.seq_size = depth, seq_size
        index = lax.axis_index("dp") * seq_size + lax.axis_index("seq")
        self.core = lax.rem(index, 2)
        self.x = lax.rem(index // 2, 2)
        self.y = lax.rem(index // 4, 2)
        self.z = index // 8
        core = self.core
        flip_x, flip_y = 1 - self.x, 1 - self.y
        x_first = self.x * core + flip_x * (1 - core)
        y_first = self.y * (1 - core) + flip_y * core
        x_second = self.x * (1 - core) + flip_x * core
        y_second = self.y * core + flip_y * (1 - core)
        self.columns = (
            (self.y, self.x),
            (y_first, x_first),
            (y_second, x_second),
            (flip_y, flip_x),
        )

    def device(self, z, y, x, core):
        index = ((z * 2 + y) * 2 + x) * 2 + core
        return (index // self.seq_size, lax.rem(index, self.seq_size))

    def layer(self, k):
        return lax.rem(self.z + self.depth - k, self.depth)

    def ahead(self, k):
        return lax.rem(self.z + k, self.depth)

    def first(self):
        return self.device(self.z, *self.columns[1], self.core)

    def second(self):
        return self.device(self.z, *self.columns[2], self.core)

    def other_core(self):
        return self.device(self.z, self.y, self.x, 1 - self.core)

    def above(self, k):
        return self.device(self.ahead(k), self.y, self.x, self.core)

    def mate(self, step):
        return (lax.axis_index("dp"), lax.rem(lax.axis_index("seq") + self.seq_size - step, self.seq_size))

    def octant(self, n):
        column, core = n % 4, n // 4
        y, x = self.columns[column]
        core = self.core * (1 - core) + (1 - self.core) * core
        return self.device(self.z, y, x, core), (y, x, core)

    def greet(self, corners=False):
        barrier = pltpu.get_barrier_semaphore()
        friends = [self.above(k) for k in range(1, self.depth)]
        friends += [self.octant(n)[0] for n in range(1, 8)] if corners else [self.first(), self.second(), self.other_core()]
        friends += [self.mate(step) for step in range(1, self.seq_size)]
        for friend in friends:
            pl.semaphore_signal(barrier, inc=1, device_id=friend, device_id_type=MESH)
        pl.semaphore_wait(barrier, len(friends))


def remote(src, dst, send, recv, device):
    return pltpu.make_async_remote_copy(
        src_ref=src, dst_ref=dst, send_sem=send, recv_sem=recv, device_id=device, device_id_type=MESH
    )


class Spread:
    def __init__(self, place, shard, full, out, into, local):
        self.place, self.shard, self.full, self.out, self.into, self.local = place, shard, full, out, into, local

    def column(self, n, core=None):
        y, x = self.place.columns[n]
        return self.full.at[:, y, x, self.place.core if core is None else core]

    def line_copy(self, k):
        place = self.place
        here = self.full.at[place.z, place.y, place.x, place.core]
        return remote(self.shard, here, self.out.at[6 + k], self.into.at[6 + k], place.above(k))

    def own_copy(self):
        place = self.place
        return pltpu.make_async_copy(self.shard, self.full.at[place.z, place.y, place.x, place.core], self.local)

    def copy(self, n, lane):
        here = self.column(n)
        device = (self.place.first, self.place.second, self.place.second)[lane] if lane < 3 else self.place.other_core
        return remote(here, here, self.out.at[lane], self.into.at[lane], device())

    def arrive(self, n, lane):
        self.copy(n, lane).wait_recv()

    def start(self):
        self.own_copy().start()
        for k in range(1, self.place.depth):
            self.line_copy(k).start()

    def send_line(self):
        self.own_copy().wait()
        for k in range(1, self.place.depth):
            self.line_copy(k).wait_recv()
        for lane in (0, 1, 3):
            self.copy(0, lane).start()

    def forward_first(self):
        self.arrive(1, 0)
        self.copy(1, 2).start()
        self.copy(1, 4).start()

    def forward_second(self, half):
        self.arrive(2 + half, 1 + half)
        self.copy(2 + half, 5 + half).start()

    def finish(self):
        for n in range(4):
            self.arrive(n, 3 + n)
        for k in range(1, self.place.depth):
            self.line_copy(k).wait_send()
        for lane in range(7):
            self.copy(0, lane).wait_send()


def spread_sems(depth):
    sems = pltpu.SemaphoreType.DMA
    return [sems((6 + depth,)), sems((6 + depth,)), sems]


class Line:
    def __init__(self, place, shard, line, result, out, into, local):
        self.place, self.shard, self.line, self.result = place, shard, line, result
        self.out, self.into, self.local = out, into, local

    def line_copy(self, k):
        return remote(self.shard, self.line.at[self.place.z], self.out.at[k], self.into.at[k], self.place.above(k))

    def own_copy(self):
        return pltpu.make_async_copy(self.shard, self.line.at[self.place.z], self.local.at[0])

    def result_copy(self):
        return pltpu.make_async_copy(self.line, self.result, self.local.at[1])

    def start(self):
        self.own_copy().start()
        for k in range(1, self.place.depth):
            self.line_copy(k).start()

    def finish(self):
        self.own_copy().wait()
        for k in range(1, self.place.depth):
            self.line_copy(k).wait()
        self.result_copy().start()


def line_sems(depth):
    sems = pltpu.SemaphoreType.DMA
    return [sems((depth,)), sems((depth,)), sems((2,))]


class Early:
    def __init__(self, place, shard, quads, result, out, into, local):
        self.place, self.shard, self.quads, self.result = place, shard, quads, result
        self.out, self.into, self.local = out, into, local

    def line_copy(self, k):
        here = self.quads.at[0, self.place.z]
        return remote(self.shard, here, self.out.at[1 + k], self.into.at[1 + k], self.place.above(k))

    def own_copy(self):
        return pltpu.make_async_copy(self.shard, self.quads.at[0, self.place.z], self.local.at[3])

    def way_copy(self, way):
        device = (self.place.first, self.place.second)[way]()
        return remote(self.quads.at[0], self.quads.at[1 + way], self.out.at[way], self.into.at[way], device)

    def result_copy(self, n):
        return pltpu.make_async_copy(self.quads.at[n], self.result.at[n], self.local.at[n])

    def start(self):
        self.own_copy().start()
        for k in range(1, self.place.depth):
            self.line_copy(k).start()

    def send(self):
        self.own_copy().wait()
        for k in range(1, self.place.depth):
            self.line_copy(k).wait_recv()
        for way in range(2):
            self.way_copy(way).start()
        self.result_copy(0).start()

    def finish(self):
        for way in range(2):
            self.way_copy(way).wait_recv()
            self.result_copy(1 + way).start()
        for k in range(1, self.place.depth):
            self.line_copy(k).wait_send()
        for way in range(2):
            self.way_copy(way).wait_send()
        for n in range(3):
            self.result_copy(n).wait()


def early_sems(depth):
    sems = pltpu.SemaphoreType.DMA
    return [sems((1 + depth,)), sems((1 + depth,)), sems((4,))]


class Late:
    def __init__(self, place, quads, full, result, out, into, local):
        self.place, self.quads, self.full, self.result = place, quads, full, result
        self.out, self.into, self.local = out, into, local

    def column(self, n):
        y, x = self.place.columns[n]
        return self.full.at[:, y, x, self.place.core]

    def own_copy(self, n):
        return pltpu.make_async_copy(self.quads.at[n], self.column(n), self.local.at[n])

    def way_copy(self):
        here = self.column(1)
        return remote(here, here, self.out.at[4], self.into.at[4], self.place.second())

    def core_copy(self, n):
        here = self.column(n)
        return remote(here, here, self.out.at[n], self.into.at[n], self.place.other_core())

    def result_copy(self):
        return pltpu.make_async_copy(self.full, self.result, self.local.at[3])

    def start(self):
        for n in range(3):
            self.own_copy(n).start()

    def send(self):
        for n in (1, 0, 2):
            self.own_copy(n).wait()
            if n == 1:
                self.way_copy().start()
            self.core_copy(n).start()

    def forward(self):
        self.way_copy().wait_recv()
        self.core_copy(3).start()

    def finish(self):
        for n in range(4):
            self.core_copy(n).wait()
        self.way_copy().wait_send()
        self.result_copy().start()


def late_sems():
    sems = pltpu.SemaphoreType.DMA
    return [sems((5,)), sems((5,)), sems((4,))]


class LateLine(Spread):
    def __init__(self, place, line, full, result, out, into, local):
        super().__init__(place, line, full, out, into, local)
        self.result = result

    def own_copy(self):
        return pltpu.make_async_copy(self.shard, self.column(0), self.local.at[0])

    def result_copy(self):
        return pltpu.make_async_copy(self.full, self.result, self.local.at[1])

    def start(self):
        self.own_copy().start()

    def send(self):
        self.own_copy().wait()
        for lane in (0, 1, 3):
            self.copy(0, lane).start()

    def finish(self):
        for n in range(4):
            self.arrive(n, 3 + n)
        for lane in range(7):
            self.copy(0, lane).wait_send()
        self.result_copy().start()


def late_line_sems():
    sems = pltpu.SemaphoreType.DMA
    return [sems((7,)), sems((7,)), sems((2,))]


class Reduce:
    def __init__(self, place, part, from_core, held, from_second, pair, from_first, line, from_line, out, into, local):
        self.place, self.part, self.local = place, part, local
        self.from_core, self.held, self.from_second, self.pair = from_core, held, from_second, pair
        self.from_first, self.line, self.from_line = from_first, line, from_line
        self.out, self.into = out, into

    def copy(self, src, dst, lane, device):
        return remote(src, dst, self.out.at[lane], self.into.at[lane], device)

    def own_copy(self):
        return pltpu.make_async_copy(self.part.at[:, :, :, self.place.core], self.held, self.local)

    def core_copy(self):
        return self.copy(self.part.at[:, :, :, 1 - self.place.core], self.from_core, 0, self.place.other_core())

    def second_copies(self):
        columns = self.place.columns
        return [
            self.copy(self.held.at[:, columns[2 + k][0], columns[2 + k][1]], self.from_second.at[k], 1 + k,
                      self.place.second())
            for k in range(2)
        ]

    def first_copy(self):
        return self.copy(self.pair.at[1], self.from_first, 3, self.place.first())

    def line_copies(self):
        place = self.place
        return [
            self.copy(self.line.at[place.ahead(k)], self.from_line.at[k - 1], 3 + k, place.above(k))
            for k in range(1, place.depth)
        ]

    def to_core(self):
        self.core_copy().start()
        self.own_copy().start()

    def to_second(self):
        self.own_copy().wait()
        self.core_copy().wait()
        self.held[...] += self.from_core[...]
        for copy in self.second_copies():
            copy.start()

    def to_first(self):
        for copy in self.second_copies():
            copy.wait()
        for k in range(2):
            y, x = self.place.columns[k]
            self.pair[k] = self.held[:, y, x] + self.from_second[k]
        self.first_copy().start()

    def to_line(self):
        self.first_copy().wait()
        self.line[...] = self.pair[0] + self.from_first[...]
        for copy in self.line_copies():
            copy.start()

    def last(self):
        for copy in self.line_copies():
            copy.wait()
        result = self.line[self.place.z].astype(f32)
        for k in range(self.place.depth - 1):
            result = result + self.from_line[k].astype(f32)
        return result


def reduce_scratch(depth, rows, cols):
    shapes = [(depth, 2, 2), (depth, 2, 2), (2, depth), (2, depth), (depth,), (depth,), (depth - 1,)]
    sems = pltpu.SemaphoreType.DMA
    return [pltpu.VMEM(shape + (rows, cols), bf16) for shape in shapes] + [sems((3 + depth,))] * 2 + [sems]


class ShortReduce:
    def __init__(self, place, part, from_octant, line, from_line, out, into):
        self.place, self.part, self.from_octant, self.line, self.from_line = place, part, from_octant, line, from_line
        self.out, self.into = out, into

    def octant_copy(self, n):
        device, (y, x, core) = self.place.octant(n)
        return remote(
            self.part.at[:, y, x, core], self.from_octant.at[n - 1], self.out.at[n - 1], self.into.at[n - 1], device
        )

    def line_copy(self, k):
        return remote(
            self.line.at[self.place.ahead(k)], self.from_line.at[k - 1], self.out.at[6 + k], self.into.at[6 + k],
            self.place.above(k)
        )

    def start(self):
        for n in range(1, 8):
            self.octant_copy(n).start()

    def to_line(self):
        place = self.place
        total = self.part[:, place.y, place.x, place.core].astype(f32)
        for n in range(1, 8):
            self.octant_copy(n).wait()
            total = total + self.from_octant[n - 1].astype(f32)
        self.line[...] = total.astype(bf16)
        for k in range(1, place.depth):
            self.line_copy(k).start()

    def last(self):
        total = self.line[self.place.z].astype(f32)
        for k in range(1, self.place.depth):
            self.line_copy(k).wait()
            total = total + self.from_line[k - 1].astype(f32)
        return total


def short_reduce_scratch(depth, rows, cols):
    sems = pltpu.SemaphoreType.DMA
    shapes = [(depth, 2, 2, 2), (7, depth), (depth,), (depth - 1,)]
    return [pltpu.VMEM(shape + (rows, cols), bf16) for shape in shapes] + [sems((6 + depth,))] * 2


def norm_rows(rows):
    centred = rows - jnp.mean(rows, axis=1, keepdims=True)
    inverse = lax.rsqrt(jnp.mean(centred * centred, axis=1, keepdims=True) + EPSILON)
    return centred * inverse, inverse


def norm_back(grad, scaled, inverse, gain):
    inner = grad * gain
    return inverse * (
        inner
        - jnp.mean(inner, axis=1, keepdims=True)
        - scaled * jnp.mean(inner * scaled, axis=1, keepdims=True)
    )


def gelu_both(v):
    power = jnp.exp2(v * v * (-0.5 * LOG2E))
    cdf = 0.5 + 0.5 * lax.erf(v * math.sqrt(0.5))
    return v * cdf, cdf + v * power * (1.0 / math.sqrt(2.0 * math.pi))


def column_sum(rows):
    return jnp.sum(rows.astype(f32), axis=0, keepdims=True)


def to_columns(rows):
    count, width = rows.shape
    return jnp.transpose(jnp.concatenate([rows, jnp.zeros((LANES - count, width), f32)], axis=0)).astype(bf16)


def own_text(ref, text, seq):
    slots, width = ref.shape
    own = jnp.zeros((text, width), ref.dtype)
    for r in range(-(-slots // text)):
        share = ref[r * text : min(slots, (r + 1) * text), :]
        if share.shape[0] < text:
            share = jnp.concatenate([share, jnp.zeros((text - share.shape[0], width), ref.dtype)], axis=0)
        own = jnp.where(seq == r, share, own)
    return own


def as_columns(vectors):
    length = vectors[0].shape[0]
    rows = [vector.reshape(1, length).astype(f32) for vector in vectors]
    rows = jnp.concatenate(rows + [jnp.zeros((LANES - len(rows), length), f32)], axis=0)
    rows = jnp.concatenate([rows, jnp.zeros((LANES, LANES - length), f32)], axis=1)
    return jnp.transpose(rows)[:length].astype(bf16)


def front_kernel(seq_size, text, width, *refs):
    refs = list(refs)

    def take(number):
        taken = refs[:number]
        del refs[:number]
        return taken

    (shard_ref,), vec_refs = take(1), take(8)
    up_ref, up_bias_ref, out_w_ref, down_ref, x_any, slot_ref, length_ref = take(7)
    w_out, w2_out, vecs, bias_ref, quads_a, line_b, xtext_ref, first_out, q_out = take(9)
    k_outs, v_outs = take(seq_size), take(seq_size)
    shard, shard2, shard_a, shard_b, w_full, w2_full, own_a, own_b, x_s, n_s, first_s, q_s, k_s, v_s = take(14)
    sems, sems2, sems_a, sems_b = take(3), take(3), take(3), take(3)
    x_sem, w_sem, out_sem, kv_sem, kv_in_sem, kv_out_sem = take(6)
    items, patch, model = x_s.shape
    units, wide = up_ref.shape[1], shard2.shape[1]
    pairs = model // width
    place = Place(w_full.shape[0], seq_size)
    seq = lax.axis_index("seq")
    x_copies = [pltpu.make_async_copy(x_any.at[i], x_s.at[i], x_sem.at[i]) for i in range(items)]
    for copy in x_copies:
        copy.start()
    for p in range(pairs):
        half, to = divmod(3 * p * width, wide)
        for n in range(3):
            at = n * model + p * width
            (shard, shard2)[half][:, to + n * width : to + (n + 1) * width] = shard_ref[:, at : at + width]
    shard[:, wide:] = as_columns([ref[...] for ref in vec_refs])
    place.greet()
    halves = [Spread(place, shard, w_full, *sems), Spread(place, shard2, w2_full, *sems2)]
    for move in halves:
        move.start()
    shard_a[:, :units] = up_ref[...]
    shard_a[:, units:] = out_w_ref[...]
    shard_b[:, :model] = down_ref[...]
    shard_b[:, model:] = as_columns([up_bias_ref[...]])
    early, line = Early(place, shard_a, own_a, quads_a, *sems_a), Line(place, shard_b, own_b, line_b, *sems_b)
    tail = bias_ref.shape[2]
    col = lax.broadcasted_iota(jnp.int32, (1, tail), 1)
    slot = jnp.full((1, tail), seq_size * text, jnp.int32)
    for r in range(seq_size):
        begin = lax.rem(seq + r, seq_size) * text
        slot = jnp.where((col >= r * text) & (col < (r + 1) * text), begin + col - r * text, slot)
    for i in range(items):
        xtext_ref[i] = own_text(slot_ref.at[i], text, seq)
        bias_ref[i] = jnp.where(slot < length_ref[i], 0.0, NEG_FILL)
    halves[0].send_line()
    halves[1].send_line()
    early.start()
    line.start()
    for i in range(items):
        x_copies[i].wait()
        n_s[i], _ = norm_rows(jnp.concatenate([x_s[i], xtext_ref[i]], axis=0).astype(f32))
    halves[0].forward_first()
    halves[0].forward_second(0)
    halves[1].forward_first()
    halves[0].forward_second(1)
    halves[1].forward_second(0)
    halves[0].finish()
    w_copies = [pltpu.make_async_copy(src, dst, w_sem.at[n]) for n, (src, dst) in
                enumerate(((w_full, w_out), (w2_full, w2_out)))]
    w_copies[0].start()
    weight = w_full[...].reshape(model, wide + LANES)
    table = jnp.transpose(weight[:, wide:].astype(f32))
    vecs[...] = table
    scale = LOG2E / math.sqrt(model // HEADS)
    sends, outs = [], []

    def project(i, half, weight):
        for p in range(half * pairs // 2, (half + 1) * pairs // 2):
            cols = slice(p * width, (p + 1) * width)
            at = 3 * p * width - half * wide
            projected = mm(first_s[i], weight[:, at : at + 3 * width])
            q_s[i, :, cols] = ((projected[:, :width] + table[QBIAS : QBIAS + 1, cols]) * scale).astype(bf16)
            k_s[0, i, :, cols] = projected[:, width : 2 * width].astype(bf16)
            v_s[0, i, :, cols] = (projected[:, 2 * width :] + table[VBIAS : VBIAS + 1, cols]).astype(bf16)
        cols = pl.ds(half * (model // 2), model // 2)
        for r in range(1, seq_size):
            for n, ref in enumerate((k_s, v_s)):
                at = ((2 * i + n) * 2 + half) * seq_size + r
                src, dst = ref.at[0, i, :, cols], ref.at[r, i, :, cols]
                sends.append(remote(src, dst, kv_sem.at[at], kv_in_sem.at[at], place.mate(r)))
                sends[-1].start()

    def bring(n, src, dst, i):
        outs.append(pltpu.make_async_copy(src.at[i], dst.at[i], out_sem.at[n, i]))
        outs[-1].start()

    for i in range(items):
        first_s[i] = (n_s[i] * table[GAIN1 : GAIN1 + 1] + table[SHIFT1 : SHIFT1 + 1]).astype(bf16)
        bring(0, first_s, first_out, i)
        project(i, 0, weight)
        if i == 0:
            halves[1].forward_second(1)
    early.send()
    halves[1].finish()
    w_copies[1].start()
    weight = w2_full[...].reshape(model, wide)
    for i in range(items):
        project(i, 1, weight)
        for n, (src, dst) in enumerate(((q_s, q_out), (k_s.at[0], k_outs[0]), (v_s.at[0], v_outs[0]))):
            bring(1 + n, src, dst, i)
    line.finish()
    for copy in sends:
        copy.wait()
    for i in range(items):
        for r in range(1, seq_size):
            for n, (ref, dst) in enumerate(((k_s, k_outs), (v_s, v_outs))):
                at = (2 * i + n) * seq_size + r
                outs.append(pltpu.make_async_copy(ref.at[r, i], dst[r].at[i], kv_out_sem.at[at]))
                outs[-1].start()
    early.finish()
    line.result_copy().wait()
    for copy in w_copies + outs:
        copy.wait()


def front(in_weight, vectors, up_weight, up_bias, out_weight, down_weight, patches, text_rows, lengths, text, width,
          devices, seq_size):
    items, patch, model = patches.shape
    depth = devices // 8
    rows, cols = in_weight.shape
    shape_a = (rows, up_weight.shape[1] + model)
    shape_b = (down_weight.shape[0], model + LANES)
    shape_w = (depth, 2, 2, 2, rows, cols // 2 + LANES)
    shape_w2 = (depth, 2, 2, 2, rows, cols // 2)
    shape_x = (items, patch + text, model)
    tail = round_up(seq_size * text, LANES)
    tokens = jax.ShapeDtypeStruct(shape_x, bf16)
    sems = pltpu.SemaphoreType.DMA
    outs = pl.pallas_call(
        functools.partial(front_kernel, seq_size, text, width),
        in_specs=[WHOLE] * 13 + [ANY, WHOLE, pl.BlockSpec(memory_space=pltpu.SMEM)],
        out_specs=[ANY, ANY, WHOLE, WHOLE, ANY, ANY, WHOLE] + [ANY] * (2 + 2 * seq_size),
        out_shape=[
            jax.ShapeDtypeStruct(shape_w, bf16),
            jax.ShapeDtypeStruct(shape_w2, bf16),
            jax.ShapeDtypeStruct((LANES, model), f32),
            jax.ShapeDtypeStruct((items, 1, tail), f32),
            jax.ShapeDtypeStruct((3, depth) + shape_a, bf16),
            jax.ShapeDtypeStruct((depth,) + shape_b, bf16),
            jax.ShapeDtypeStruct((items, text, model), bf16),
            tokens,
            tokens,
        ]
        + [tokens] * (2 * seq_size),
        scratch_shapes=[
            pltpu.VMEM((rows, cols // 2 + LANES), bf16),
            pltpu.VMEM((rows, cols // 2), bf16),
            pltpu.VMEM(shape_a, bf16),
            pltpu.VMEM(shape_b, bf16),
            pltpu.VMEM(shape_w, bf16),
            pltpu.VMEM(shape_w2, bf16),
            pltpu.VMEM((3, depth) + shape_a, bf16),
            pltpu.VMEM((depth,) + shape_b, bf16),
            pltpu.VMEM(patches.shape, bf16),
            pltpu.VMEM(shape_x, f32),
            pltpu.VMEM(shape_x, bf16),
            pltpu.VMEM(shape_x, bf16),
            pltpu.VMEM((seq_size,) + shape_x, bf16),
            pltpu.VMEM((seq_size,) + shape_x, bf16),
        ]
        + spread_sems(depth) * 2
        + early_sems(depth)
        + line_sems(depth)
        + [sems((items,)), sems((2,)), sems((4, items))]
        + [sems((4 * items * seq_size,))] * 2
        + [sems((2 * items * seq_size,))],
        compiler_params=compiler_params(collective_id=0, has_side_effects=True),
        name="front",
    )(in_weight, *vectors, up_weight, up_bias, out_weight, down_weight, patches, text_rows, lengths)
    weights = [full.reshape(model, full.shape[-1]) for full in outs[:2]]
    return weights, *outs[2:4], outs[4:6], *outs[6:9], outs[9 : 9 + seq_size], outs[9 + seq_size :]


def collect(dst, refs, patch, text):
    count, width = len(refs), refs[0].shape[2]
    for r, ref in enumerate(refs):
        dst[r * patch : (r + 1) * patch, :width] = ref[0, :patch, :]
        at = count * patch + r * text
        dst[at : at + text, :width] = ref[0, patch:, :]
    filled = count * (patch + text)
    if dst.shape[0] > filled:
        dst[filled:, :width] = jnp.zeros((dst.shape[0] - filled, width), dst.dtype)


def by_head(dst, src, lane, heads, ones):
    count, width = src.shape
    for h in range(heads):
        rows = slice(h * count, (h + 1) * count)
        dst[rows, :width] = jnp.where(lane == h, src, jnp.zeros_like(src))
        if ones:
            dst[rows, width:] = jnp.where(lane == h, jnp.ones_like(src), jnp.zeros_like(src))


def attend_kernel(count, patch, head, seq_size, *refs):
    q_ref, k_refs, v_refs = refs[0], refs[1 : 1 + count], refs[1 + count : 1 + 2 * count]
    bias_ref, quads_a, line_b, out_ref, rest_ref, log_ref, full_a, full_b = refs[1 + 2 * count : 9 + 2 * count]
    keys, values, text_keys, text_values, into_a, into_b, *sems = refs[9 + 2 * count :]
    width = q_ref.shape[2]
    text, edge = q_ref.shape[1] - patch, count * patch
    heads, span = width // head, keys.shape[0] - edge
    place = Place(full_a.shape[0], seq_size)
    turn = pl.program_id(0) * pl.num_programs(1) + pl.program_id(1)
    last = pl.num_programs(0) * pl.num_programs(1) - 1
    move_a, move_b = Late(place, quads_a, into_a, full_a, *sems[:3]), LateLine(place, line_b, into_b, full_b, *sems[3:])

    @pl.when(turn == 0)
    def _():
        move_a.start()
        move_b.start()
        place.greet()
        move_a.send()
        move_b.send()

    agenda = (
        (4, move_a.forward),
        (4, move_b.forward_first),
        (6, functools.partial(move_b.forward_second, 0)),
        (7, functools.partial(move_b.forward_second, 1)),
        (9, move_a.finish),
        (9, move_b.finish),
    )
    for at in sorted({at for at, _ in agenda}):

        @pl.when(turn == at)
        def _(at=at):
            for when, step in agenda:
                if when == at:
                    step()

    collect(keys, k_refs, patch, text)
    collect(values, v_refs, patch, text)
    values[:, width:] = jnp.ones((values.shape[0], values.shape[1] - width), bf16)
    lane = lax.broadcasted_iota(jnp.int32, (1, width), 1) // head
    by_head(text_keys, keys[edge:], lane, heads, False)
    by_head(text_values, values[edge:, :width], lane, heads, True)
    q = q_ref[0]
    text_bias = jnp.concatenate([bias_ref[0]] * heads, axis=1)

    def scores_of(h):
        return mm_t(jnp.where(lane == h, q, jnp.zeros_like(q)), keys[:edge])

    text_scores = mm_t(q, text_keys[...]) + text_bias
    scores = scores_of(0)
    text_powers, mixed, total, tops = [], None, None, None
    for h in range(heads):
        following = scores_of(h + 1) if h + 1 < heads else None
        text_head = text_scores[:, h * span : (h + 1) * span]
        top = jnp.maximum(jnp.max(scores, axis=1, keepdims=True), jnp.max(text_head, axis=1, keepdims=True))
        powers = jnp.exp2(scores - top).astype(bf16)
        text_powers.append(jnp.exp2(text_head - top).astype(bf16))
        both = mm(powers, values[:edge])
        mixed = both[:, :width] if mixed is None else jnp.where(lane == h, both[:, :width], mixed)
        total = both[:, width:] if total is None else jnp.where(lane == h, both[:, width:], total)
        tops = jnp.broadcast_to(top, mixed.shape) if tops is None else jnp.where(lane == h, top, tops)
        scores = following
    both = mm(jnp.concatenate(text_powers, axis=1), text_values[...])
    total = total + both[:, width:]
    out = (mixed + both[:, :width]) * (1.0 / total)
    high = out.astype(bf16)
    out_ref[0] = high
    rest_ref[0] = (out - high.astype(f32)).astype(bf16)
    log_ref[0] = tops + jnp.log2(total)

    @pl.when(turn == last)
    def _():
        move_a.result_copy().wait()
        move_b.result_copy().wait()


def attend(q, keys, values, bias, halfway, patch, head, width, devices, seq_size):
    items, _, model = q.shape
    count, tail = len(keys), bias.shape[-1]
    depth, heads, span = devices // 8, width // head, count * patch + tail
    block = pl.BlockSpec((1, q.shape[1], width), lambda i, p: (i, 0, p))
    outs = pl.pallas_call(
        functools.partial(attend_kernel, count, patch, head, seq_size),
        grid=(items, model // width),
        in_specs=[block] * (1 + 2 * count) + [pl.BlockSpec((1, 1, tail), lambda i, p: (i, 0, 0))] + [ANY] * 2,
        out_specs=[block, block, block, ANY, ANY],
        out_shape=[jax.ShapeDtypeStruct(q.shape, bf16)] * 2
        + [jax.ShapeDtypeStruct(q.shape, f32)]
        + [jax.ShapeDtypeStruct((depth, 2, 2, 2) + part.shape[-2:], part.dtype) for part in halfway],
        scratch_shapes=[
            pltpu.VMEM((span, width), bf16),
            pltpu.VMEM((span, 2 * width), bf16),
            pltpu.VMEM((heads * tail, width), bf16),
            pltpu.VMEM((heads * tail, 2 * width), bf16),
        ]
        + [pltpu.VMEM((depth, 2, 2, 2) + part.shape[-2:], part.dtype) for part in halfway]
        + late_sems()
        + late_line_sems(),
        compiler_params=compiler_params(collective_id=1, has_side_effects=True),
        name="attend",
    )(q, *keys, *values, bias, *halfway)
    return outs[0], outs[1], outs[2], [full.reshape(-1, full.shape[-1]) for full in outs[3:]]


def ffn_kernel(steps, chunk, seq_ref, x_ref, xtext_ref, at_ref, dy_ref, dy_slot_ref, w_any, wd_any, vec_ref,
               res_ref, restext_ref, gb_ref, ga_ref, part_out, down_out,
               w_ref, wd_ref, part_ref, down_ref, second_s, hidden_s, pre_s, dy_s, sums_s, bias_s, out_s, dots_s,
               w_sem, wd_sem, part_sem, down_sem):
    step = pl.program_id(0)
    patch, model = x_ref.shape[1:]
    text = xtext_ref.shape[1]
    block, units = patch + text, wd_ref.shape[0]
    chunks = units // chunk
    rows = pl.ds(pl.multiple_of(step * block, ROW_TILE), block)
    gain = vec_ref[GAIN2 : GAIN2 + 1]
    w_out = w_ref.at[:, units:]

    def fetch(cols, at):
        if cols is None:
            return (
                pltpu.make_async_copy(w_any.at[:, units:], w_ref.at[:, units:], w_sem.at[at]),
                pltpu.make_async_copy(wd_any.at[:, model:], wd_ref.at[:, model:], wd_sem.at[at]),
            )
        return (
            pltpu.make_async_copy(w_any.at[:, cols], w_ref.at[:, cols], w_sem.at[at]),
            pltpu.make_async_copy(wd_any.at[cols, :model], wd_ref.at[cols, :model], wd_sem.at[at]),
        )

    @pl.when(step == 0)
    def _():
        others = fetch(None, chunks)
        for copy in others:
            copy.start()
        for c in range(chunks):
            for copy in fetch(pl.ds(c * chunk, chunk), c):
                copy.start()
        sums_s[...] = jnp.zeros_like(sums_s)
        for copy in others:
            copy.wait()
        bias_s[...] = jnp.transpose(wd_ref[:, model:].astype(f32))[:8]

    x = jnp.concatenate([x_ref[0], xtext_ref[0]], axis=0).astype(f32)
    dy = jnp.concatenate([dy_ref[0], own_text(dy_slot_ref.at[0], text, seq_ref[0])], axis=0)
    dy_s[rows, :] = dy
    middle = x + (mm(at_ref[0], w_out[...]) + vec_ref[BRANCH : BRANCH + 1])
    scaled, inverse = norm_rows(middle)
    second_in = (scaled * gain + vec_ref[SHIFT2 : SHIFT2 + 1]).astype(bf16)
    second_s[rows, :] = second_in
    dots_s[0] = middle + vec_ref[DOWNB : DOWNB + 1]
    dots_s[1] = jnp.zeros_like(middle)

    def part(c, _):
        cols = pl.ds(pl.multiple_of(c * chunk, chunk), chunk)

        @pl.when(step == 0)
        def _():
            for copy in fetch(cols, c):
                copy.wait()

        value, slope = gelu_both(mm(second_in, w_ref[:, cols]) + bias_s[:1, cols])
        hidden = value.astype(bf16)
        hidden_s[rows, cols] = hidden
        grad_pre = (mm_t(dy, wd_ref[cols, :model]) * slope).astype(bf16)
        pre_s[rows, cols] = grad_pre
        dots_s[0] += mm(hidden, wd_ref[cols, :model])
        dots_s[1] += mm_t(grad_pre, w_ref[:, cols])
        return 0

    lax.fori_loop(0, units // chunk, part, 0)
    result, grad_second = dots_s[0], dots_s[1]
    result = result.astype(bf16)
    res_ref[0] = result[:patch]
    restext_ref[0] = result[patch:]
    grad_branch = (dy.astype(f32) + norm_back(grad_second, scaled, inverse, gain)).astype(bf16)
    gb_ref[0] = grad_branch
    ga_ref[0] = mm_t(grad_branch, w_out[...]).astype(bf16)
    out_grad = t_mm(at_ref[0], grad_branch)

    @pl.when(step == 0)
    def _():
        out_s[...] = out_grad

    @pl.when(step > 0)
    def _():
        out_s[...] += out_grad

    for at, grad in ((BRANCH, grad_branch), (GAIN2, grad_second * scaled), (SHIFT2, grad_second), (DOWNB, dy)):
        sums_s[at : at + 1, :] += column_sum(grad)

    @pl.when(step == steps - 1)
    def _():
        groups = units // model
        copies = []
        part_ref[:, units : units + model] = out_s[...].astype(bf16)
        part_ref[:, units + model :] = to_columns(sums_s[...])
        copies.append(pltpu.make_async_copy(part_ref.at[:, units:], part_out.at[:, units:], part_sem.at[groups]))
        copies[-1].start()
        for c in range(groups):
            cols = slice(c * model, (c + 1) * model)
            at = pl.ds(c * model, model)
            grad_pre = pre_s[:, cols]
            part_ref[:, cols] = t_mm(second_s[...], grad_pre).astype(bf16)
            copies.append(pltpu.make_async_copy(part_ref.at[:, at], part_out.at[:, at], part_sem.at[c]))
            copies[-1].start()
            down_ref[cols, :model] = jnp.transpose(t_mm(dy_s[...], hidden_s[:, cols])).astype(bf16)
            down_ref[cols, model:] = to_columns(column_sum(grad_pre))
            copies.append(pltpu.make_async_copy(down_ref.at[at], down_out.at[at], down_sem.at[c]))
            copies[-1].start()
        for copy in copies:
            copy.wait()


def ffn(seq, patches, x_text, attended, patch_cotangent, text_cotangent, weights, w_down, vecs):
    items, patch, model = patches.shape
    units, rows, text, slots = w_down.shape[0], attended.shape[1], x_text.shape[1], text_cotangent.shape[1]

    def item(count):
        return pl.BlockSpec((1, count, model), lambda i: (i, 0, 0))

    def shape(count):
        return jax.ShapeDtypeStruct((items, count, model), bf16)

    return pl.pallas_call(
        functools.partial(ffn_kernel, items, 1024),
        grid=(items,),
        in_specs=[pl.BlockSpec(memory_space=pltpu.SMEM)]
        + [item(patch), item(text), item(rows), item(patch), item(slots)]
        + [ANY, ANY, WHOLE],
        out_specs=[item(patch), item(text), item(rows), item(rows), ANY, ANY],
        out_shape=[shape(patch), shape(text), shape(rows), shape(rows)]
        + [
            jax.ShapeDtypeStruct((model, units + model + LANES), bf16),
            jax.ShapeDtypeStruct((units, model + LANES), bf16),
        ],
        scratch_shapes=[
            pltpu.VMEM(weights.shape, bf16),
            pltpu.VMEM(w_down.shape, bf16),
            pltpu.VMEM((model, units + model + LANES), bf16),
            pltpu.VMEM((units, model + LANES), bf16),
            pltpu.VMEM((items * rows, model), bf16),
            pltpu.VMEM((items * rows, units), bf16),
            pltpu.VMEM((items * rows, units), bf16),
            pltpu.VMEM((items * rows, model), bf16),
            pltpu.VMEM((8, model), f32),
            pltpu.VMEM((8, units), f32),
            pltpu.VMEM((model, model), f32),
            pltpu.VMEM((2, rows, model), f32),
        ]
        + [pltpu.SemaphoreType.DMA((units // 1024 + 1,))] * 2
        + [pltpu.SemaphoreType.DMA((units // model + 1,))] * 2,
        compiler_params=compiler_params(),
        name="ffn",
    )(seq, patches, x_text, attended, patch_cotangent, text_cotangent, weights, w_down, vecs)


def back_kernel(count, patch, head, seq_size, pairs, items, *refs):
    refs = list(refs)

    def take(number):
        taken = refs[:number]
        del refs[:number]
        return taken

    (q_ref,), k_refs, v_refs = take(1), take(count), take(count)
    bias_ref, log_ref, at_ref, rest_ref, grad_ref = take(5)
    part_a, part_b, w_any, w2_any, vec_ref, first_any, x_any, xtext_any, gb_any, restext_any = take(10)
    grad_out, text_grad_out, text_out, total_a, total_b, total_in, vec_out, vec2_out, upb_out = take(9)
    keys, values, text_keys, text_values, probs_s, scores_s = take(6)
    mixed_s, own_s, dkv_out, dkv_in, sums_s = take(5)
    w_s, w2_s, first_s, x_s, xtext_s, gb_s, text_s, patch_s = take(8)
    fetch_sem, dkv_sem, dkv_in_sem, text_sem, text_in_sem, patch_sem = take(6)
    scratch_a, scratch_b = take(10), take(10)
    scratch_in = [take(11) for _ in range(pairs)]
    scratch_vec = take(6)

    width, rows = q_ref.shape[2], q_ref.shape[1]
    text, model = rows - patch, pairs * width
    place = Place(part_a.shape[0], seq_size)
    seq = lax.axis_index("seq")
    p, i = pl.program_id(0), pl.program_id(1)
    turn, last = p * items + i, pairs * items - 1
    sums_a, sums_b = Reduce(place, part_a, *scratch_a), Reduce(place, part_b, *scratch_b)
    sums_in = [Reduce(place, each[0], *each[1:]) for each in scratch_in]
    sums_vec = ShortReduce(place, *scratch_vec)
    fetches = [
        pltpu.make_async_copy(src, dst, fetch_sem.at[n])
        for n, (src, dst) in enumerate(
            ((first_any, first_s), (w_any, w_s), (w2_any, w2_s), (x_any, x_s), (xtext_any, xtext_s), (gb_any, gb_s))
        )
    ]

    def text_copies(src, dst, row):
        to = dst.at[:, pl.ds(pl.multiple_of(seq * text, ROW_TILE), text)]
        own = pltpu.make_async_copy(src, to, text_sem.at[row, 0])
        away = [
            remote(src, to, text_sem.at[row, r], text_in_sem.at[row, r], place.mate(r)) for r in range(1, seq_size)
        ]
        return [own] + away

    def dkv_copy(slot, r):
        return remote(
            dkv_out.at[slot, r - 1], dkv_in.at[slot, r - 1], dkv_sem.at[slot, r - 1], dkv_in_sem.at[slot, r - 1],
            place.mate(-r)
        )

    def settle(of):
        slot, pair, item = lax.rem(of, 2), of // items, lax.rem(of, items)
        total = own_s[slot]
        for r in range(1, seq_size):
            dkv_copy(slot, r).wait_recv()
            total = total + dkv_in[slot, r - 1].astype(f32)
        at = pl.ds(pl.multiple_of(item * rows, ROW_TILE), rows)
        mixed_s[pair, at, width:] = total.astype(bf16)

    def pair_done(pair):
        mixed = mixed_s[pair]
        if pair == 0:
            fetches[0].wait()
        grad = t_mm(first_s[...].reshape(items * rows, model), mixed).astype(bf16)
        sums_in[pair].part[...] = grad.reshape(sums_in[pair].part.shape)
        sums_in[pair].to_core()
        cols = slice(pair * width, (pair + 1) * width)
        sums_s[QBIAS : QBIAS + 1, cols] = column_sum(mixed[:, :width])
        sums_s[VBIAS : VBIAS + 1, cols] = column_sum(mixed[:, 2 * width :])

    def finish_in(pair):
        total = sums_in[pair].last()
        for n in range(3):
            at = n * model + pair * width
            total_in[:, at : at + width] = total[:, n * width : (n + 1) * width]

    def finish_a():
        total = sums_a.last()
        total_a[...] = total[:, : total_a.shape[1]]
        vec2_out[...] = total[:, total_a.shape[1] :]

    def finish_b():
        total = sums_b.last()
        total_b[...] = total[:, :model]
        upb_out[...] = total[:, model:]

    agenda = [(1, sums_a.to_second), (2, sums_b.to_second), (4, sums_a.to_first), (6, sums_b.to_first),
              (6, sums_a.to_line), (8, sums_b.to_line), (8, finish_a), (11, finish_b)]
    for pair in range(pairs):
        done = items * (pair + 1)
        steps = (sums_in[pair].to_second, sums_in[pair].to_first, sums_in[pair].to_line, functools.partial(finish_in, pair))
        agenda += [(done + 1 + n, step) for n, step in enumerate(steps)]
    agenda.sort(key=lambda entry: entry[0])

    @pl.when(turn == 0)
    def _():
        place.greet(corners=True)
        sums_a.to_core()
        sums_b.to_core()
        for copy in fetches:
            copy.start()
        for copy in text_copies(restext_any, text_out, 0):
            copy.start()
        sums_s[...] = jnp.zeros_like(sums_s)

    for at in sorted({at for at, _ in agenda if at <= last}):

        @pl.when(turn == at)
        def _(at=at):
            for when, step in agenda:
                if when == at:
                    step()

    collect(keys, k_refs, patch, text)
    collect(values, v_refs, patch, text)
    q, grad = q_ref[0], grad_ref[0]
    edge, heads, span = count * patch, width // head, keys.shape[0] - count * patch
    lane = lax.broadcasted_iota(jnp.int32, (1, width), 1) // head
    row = lax.broadcasted_iota(jnp.int32, (width, 1), 0) // head
    by_head(text_keys, keys[edge:], lane, heads, False)
    by_head(text_values, values[edge:], lane, heads, False)
    text_bias = jnp.concatenate([bias_ref[0]] * heads, axis=1)
    inner = grad.astype(f32) * (at_ref[0].astype(f32) + rest_ref[0].astype(f32))
    q_heads = [jnp.where(lane == h, q, jnp.zeros_like(q)) for h in range(heads)]
    grad_heads = [jnp.where(lane == h, grad, jnp.zeros_like(grad)) for h in range(heads)]
    deltas = [jnp.sum(jnp.where(lane == h, inner, 0.0), axis=1, keepdims=True) for h in range(heads)]
    logs = [log_ref[0, :, h * head : h * head + 1] for h in range(heads)]

    def first_dots(h):
        return mm_t(q_heads[h], keys[:edge]), mm_t(grad_heads[h], values[:edge])

    scores, grad_probs = first_dots(0)
    text_scores = mm_t(q, text_keys[...]) + text_bias
    text_grad_probs = mm_t(grad, text_values[...])
    dq, text_probs, text_grads = None, [], []
    for h in range(heads):
        following = first_dots(h + 1) if h + 1 < heads else (None, None)
        cols = slice(h * span, (h + 1) * span)
        text_head = jnp.exp2(text_scores[:, cols] - logs[h])
        text_probs.append(text_head.astype(bf16))
        text_grads.append((text_head * (text_grad_probs[:, cols] - deltas[h])).astype(bf16))
        probs = jnp.exp2(scores - logs[h])
        grad_scores = (probs * (grad_probs - deltas[h])).astype(bf16)
        probs_s[h * rows : (h + 1) * rows, :] = probs.astype(bf16)
        scores_s[h * rows : (h + 1) * rows, :] = grad_scores
        dq_head = mm(grad_scores, keys[:edge])
        dq = dq_head if dq is None else jnp.where(lane == h, dq_head, dq)
        scores, grad_probs = following
    text_probs, text_grads = jnp.concatenate(text_probs, axis=1), jnp.concatenate(text_grads, axis=1)
    dq = dq + mm(text_grads, text_keys[...])
    dv = jnp.transpose(t_mm(jnp.concatenate(grad_heads, axis=0), probs_s[...]))
    dk = jnp.transpose(t_mm(jnp.concatenate(q_heads, axis=0), scores_s[...])) * LN2

    def of_heads(wide):
        own = wide[:, :span]
        for h in range(1, heads):
            own = jnp.where(row == h, wide[:, h * span : (h + 1) * span], own)
        return jnp.transpose(own)

    text_dv, text_dk = of_heads(t_mm(grad, text_probs)), of_heads(t_mm(q, text_grads)) * LN2
    slot = lax.rem(turn, 2)
    at = pl.ds(pl.multiple_of(i * rows, ROW_TILE), rows)
    mixed_s[p, at, :width] = (dq * (1.0 / math.sqrt(head))).astype(bf16)
    own_s[slot, :patch, :width] = dk[:patch]
    own_s[slot, :patch, width:] = dv[:patch]
    own_s[slot, patch:, :width] = text_dk[:text]
    own_s[slot, patch:, width:] = text_dv[:text]

    @pl.when(turn > 0)
    def _():
        settle(turn - 1)

    @pl.when(turn > 1)
    def _():
        for r in range(1, seq_size):
            dkv_copy(slot, r).wait_send()

    for r in range(1, seq_size):
        for n, (part, text_part) in enumerate(((dk, text_dk), (dv, text_dv))):
            cols = slice(n * width, (n + 1) * width)
            dkv_out[slot, r - 1, :patch, cols] = part[r * patch : (r + 1) * patch].astype(bf16)
            dkv_out[slot, r - 1, patch:, cols] = text_part[r * text : (r + 1) * text].astype(bf16)
        dkv_copy(slot, r).start()

    for pair in range(pairs - 1):

        @pl.when(turn == items * (pair + 1))
        def _(pair=pair):
            pair_done(pair)

    @pl.when(turn == last)
    def _():
        left = [step for when, step in agenda if when > last]
        settle(last)
        pair_done(pairs - 1)
        for copy in fetches[1:]:
            copy.wait()
        patch_copies = [
            pltpu.make_async_copy(patch_s.at[item], grad_out.at[item], patch_sem.at[item]) for item in range(items)
        ]
        gain = vec_ref[GAIN1 : GAIN1 + 1]
        for item in range(items):
            half, at = pairs // 2, slice(item * rows, (item + 1) * rows)
            grad_first = sum(
                mm_t(jnp.concatenate([mixed_s[n * half + m, at, :] for m in range(half)], axis=1), ref[...])
                for n, ref in enumerate((w_s.at[:, : 3 * half * width], w2_s))
            )
            scaled, inverse = norm_rows(jnp.concatenate([x_s[item], xtext_s[item]], axis=0).astype(f32))
            grad_rows = gb_s[item].astype(f32) + norm_back(grad_first, scaled, inverse, gain)
            grad_rows = grad_rows.astype(bf16)
            patch_s[item] = grad_rows[:patch]
            patch_copies[item].start()
            text_s[item] = grad_rows[patch:]
            sums_s[GAIN1 : GAIN1 + 1, :] += column_sum(grad_first * scaled)
            sums_s[SHIFT1 : SHIFT1 + 1, :] += column_sum(grad_first)
            if left:
                left.pop(0)()
        for copy in text_copies(text_s, text_grad_out, 1):
            copy.start()
        sums_vec.part[...] = to_columns(sums_s[...]).reshape(sums_vec.part.shape)
        sums_vec.start()
        if left:
            left.pop(0)()
        sums_vec.to_line()
        for step in left:
            step()
        vec_out[...] = sums_vec.last()
        for copies in (text_copies(restext_any, text_out, 0), text_copies(text_s, text_grad_out, 1)):
            for copy in copies:
                copy.wait()
        for slot in range(2):
            for r in range(1, seq_size):
                dkv_copy(slot, r).wait_send()
        for copy in patch_copies:
            copy.wait()


def back(q, keys, values, bias, logs, attended, rest, grad_att, part_a, part_b, w_in, vecs, first_in, patches, x_text,
         grad_branch, res_text, head, width, devices, seq_size):
    items, patch, model = patches.shape
    rows, text = q.shape[1], x_text.shape[1]
    count, tail, pairs, depth = len(keys), bias.shape[-1], model // width, devices // 8
    span = count * patch + tail
    block = pl.BlockSpec((1, rows, width), lambda p, i: (i, 0, p))
    parts = [part.reshape((depth, 2, 2, 2, part.shape[0] // devices, part.shape[1])) for part in (part_a, part_b)]
    (rows_a, cols_a), (rows_b, cols_b) = parts[0].shape[4:], parts[1].shape[4:]
    sems = pltpu.SemaphoreType.DMA
    others = seq_size - 1
    slots = jax.ShapeDtypeStruct((items, seq_size * text, model), bf16)
    scratch_in = [pltpu.VMEM((depth, 2, 2, 2, rows_a, 3 * width), bf16)] + reduce_scratch(depth, rows_a, 3 * width)
    return pl.pallas_call(
        functools.partial(back_kernel, count, patch, head, seq_size, pairs, items),
        grid=(pairs, items),
        in_specs=[block] * (1 + 2 * count)
        + [pl.BlockSpec((1, 1, tail), lambda p, i: (i, 0, 0))]
        + [block] * 4
        + [ANY] * 4
        + [WHOLE]
        + [ANY] * 5,
        out_specs=[ANY] * 3 + [WHOLE] * 6,
        out_shape=[
            jax.ShapeDtypeStruct(patches.shape, bf16),
            slots,
            slots,
            jax.ShapeDtypeStruct((rows_a, cols_a - LANES), f32),
            jax.ShapeDtypeStruct((rows_b, cols_b - LANES), f32),
            jax.ShapeDtypeStruct((rows_a, 3 * model), f32),
            jax.ShapeDtypeStruct((rows_a, LANES), f32),
            jax.ShapeDtypeStruct((rows_a, LANES), f32),
            jax.ShapeDtypeStruct((rows_b, LANES), f32),
        ],
        scratch_shapes=[
            pltpu.VMEM((span, width), bf16),
            pltpu.VMEM((span, width), bf16),
            pltpu.VMEM((width // head * tail, width), bf16),
            pltpu.VMEM((width // head * tail, width), bf16),
            pltpu.VMEM((width // head * rows, count * patch), bf16),
            pltpu.VMEM((width // head * rows, count * patch), bf16),
            pltpu.VMEM((pairs, items * rows, 3 * width), bf16),
            pltpu.VMEM((2, rows, 2 * width), f32),
            pltpu.VMEM((2, others, rows, 2 * width), bf16),
            pltpu.VMEM((2, others, rows, 2 * width), bf16),
            pltpu.VMEM((8, model), f32),
            pltpu.VMEM(w_in[0].shape, bf16),
            pltpu.VMEM(w_in[1].shape, bf16),
            pltpu.VMEM(first_in.shape, bf16),
            pltpu.VMEM(patches.shape, bf16),
            pltpu.VMEM(x_text.shape, bf16),
            pltpu.VMEM(grad_branch.shape, bf16),
            pltpu.VMEM(x_text.shape, bf16),
            pltpu.VMEM(patches.shape, bf16),
            sems((6,)),
            sems((2, others)),
            sems((2, others)),
            sems((2, seq_size)),
            sems((2, seq_size)),
            sems((items,)),
        ]
        + reduce_scratch(depth, rows_a, cols_a)
        + reduce_scratch(depth, rows_b, cols_b)
        + scratch_in * pairs
        + short_reduce_scratch(depth, rows_a, LANES),
        compiler_params=compiler_params(collective_id=2, has_side_effects=True),
        name="back",
    )(q, *keys, *values, bias, logs, attended, rest, grad_att, *parts, *w_in, vecs, first_in, patches, x_text,
      grad_branch, res_text)


def outputs_kernel(*refs):
    text_ref, patch_grad, text_grad, total_a, total_b, total_in, vec1, vec2, upb = refs[:9]
    outs = list(refs[9:])
    out_text, grad_patches, grad_text = outs[:3]
    first_gain, first_shift, in_weight, query_bias, value_bias, out_weight, branch_bias = outs[3:10]
    second_gain, second_shift, up_weight, up_bias, down_weight, down_bias = outs[10:]
    slots, units = out_text.shape[1], up_weight.shape[1]
    out_text[...] = text_ref[:, :slots]
    grad_text[...] = text_grad[:, :slots]
    grad_patches[...] = patch_grad[...]

    def row_of(ref, at):
        count = ref.shape[0]
        tall = jnp.concatenate([ref[...], jnp.zeros((LANES - count, LANES), f32)], axis=0)
        return jnp.transpose(tall)[at, :count]

    @pl.when(pl.program_id(0) == 0)
    def _():
        in_weight[...] = total_in[...]
        out_weight[...] = total_a[:, units:]
        up_weight[...] = total_a[:, :units]
        down_weight[...] = total_b[...]
        for ref, at in ((first_gain, GAIN1), (first_shift, SHIFT1), (query_bias, QBIAS), (value_bias, VBIAS)):
            ref[...] = row_of(vec1, at)
        for ref, at in ((branch_bias, BRANCH), (second_gain, GAIN2), (second_shift, SHIFT2), (down_bias, DOWNB)):
            ref[...] = row_of(vec2, at)
        up_bias[...] = row_of(upb, 0)


def outputs(text, patch_grad, text_grad, total_a, total_b, total_in, vec1, vec2, upb, slots, units):
    items, patch, model = patch_grad.shape
    padded = text.shape[1]

    def item(count):
        return pl.BlockSpec((1, count, model), lambda i: (i, 0, 0))

    def shape(*dims):
        return jax.ShapeDtypeStruct(dims, f32)

    count = total_in.shape[0]
    vector, texts = shape(count), jax.ShapeDtypeStruct((items, slots, model), bf16)
    return pl.pallas_call(
        outputs_kernel,
        grid=(items,),
        in_specs=[item(padded), item(patch), item(padded)] + [WHOLE] * 6,
        out_specs=[item(slots), item(patch), item(slots)] + [WHOLE] * 13,
        out_shape=[texts, jax.ShapeDtypeStruct(patch_grad.shape, bf16), texts]
        + [vector, vector, shape(count, 3 * model), vector, vector, shape(count, model), vector, vector, vector]
        + [shape(count, units), shape(upb.shape[0]), shape(*total_b.shape), vector],
        compiler_params=compiler_params(),
        name="outputs",
    )(text, patch_grad, text_grad, total_a, total_b, total_in, vec1, vec2, upb)


def per_device(
    seq_size,
    devices,
    patches,
    text_rows,
    lengths,
    first_gain,
    first_shift,
    in_weight,
    query_bias,
    value_bias,
    out_weight,
    branch_bias,
    second_gain,
    second_shift,
    up_weight,
    up_bias,
    down_weight,
    down_bias,
    patch_cotangent,
    text_cotangent,
):
    items, patch, model = patches.shape
    slots = text_rows.shape[1]
    units = up_weight.shape[1]
    head = model // HEADS
    width = min(LANES, model)
    text = round_up(-(-slots // seq_size), ROW_TILE)
    seq = lax.axis_index("seq")
    vectors = [first_gain, first_shift, query_bias, value_bias, branch_bias, second_gain, second_shift, down_bias]
    w_in, vecs, bias, halfway, x_text, first_in, q, keys, values = front(
        in_weight, vectors, up_weight, up_bias, out_weight, down_weight, patches, text_rows, lengths, text, width,
        devices, seq_size
    )
    attended, rest, logs, (weights, w_down) = attend(
        q, keys, values, bias, halfway, patch, head, width, devices, seq_size
    )
    out_patches, res_text, grad_branch, grad_att, part_a, part_b = ffn(
        seq[None], patches, x_text, attended, patch_cotangent, text_cotangent, weights, w_down, vecs
    )
    grad_patches, grad_text, out_text, sums, down_grad, in_grad, vec1, vec2, up_bias_grad = back(
        q, keys, values, bias, logs, attended, rest, grad_att, part_a, part_b, w_in, vecs, first_in, patches, x_text,
        grad_branch, res_text, head, width, devices, seq_size
    )
    rest = outputs(
        out_text, grad_patches, grad_text, sums, down_grad, in_grad, vec1, vec2, up_bias_grad, slots, units
    )
    return (out_patches, *rest)


def solution(mesh):
    both = ("dp", "seq")
    rows, slots, vector, matrix = P("dp", "seq", None), P("dp", None, None), P(both), P(both, None)
    weights = (vector, vector, matrix, vector, vector, matrix, vector, vector, vector, matrix, vector, matrix, vector)
    return jax.shard_map(
        functools.partial(per_device, mesh.shape["seq"], mesh.size),
        mesh=mesh,
        in_specs=(rows, slots, P("dp")) + weights + (rows, slots),
        out_specs=(rows, slots, rows, slots) + weights,
        check_vma=False,
    )
```

time: 248 us -> 196 us (0.79)
  Pallas kernels: 229 us -> 194 us
  local copies, waits for them, and re-layouts: 15.5 us -> 0 us
    pallas_call x1 -> x2, Pallas kernels: 56.2 us -> 43.5 us  [the longest x1 39.3 us: ffn(): pl.pallas_call(functools.partial(ffn_kernel, items, 1024), grid=(items,),...]
    pallas_call x1, Pallas kernels: 43.3 us -> 31.2 us  [attend(): pl.pallas_call(functools.partial(attend_kernel, count, patch, head, seq_s...]
    slice x7 -> x0, local copies, waits for them, and re-layouts: 10.8 us -> none  [the longest x1 1.69 us: per_device(): grad_text[:, :slots]]
    pallas_call x1, Pallas kernels: 95.2 us -> 84.8 us  [back(): pl.pallas_call(functools.partial(back_kernel, count, patch, head, seq_siz...]
    unnamed x7 -> x0, local copies, waits for them, and re-layouts: 3.99 us -> none
where the time goes in v4:
time: 196 us; the launch traced here: 195 us
  Pallas kernels  194 us (99%)
    pallas_call x1, Pallas kernels, back(): pl.pallas_call(functools.partial(back_kernel, count, patch, head, seq_siz...  84.8 us
    pallas_call x1, Pallas kernels, ffn(): pl.pallas_call(functools.partial(ffn_kernel, items, 1024), grid=(items,),...  39.3 us
    pallas_call x1, Pallas kernels, front(): pl.pallas_call(functools.partial(front_kernel, seq_size, text, width), in...  34.9 us
    pallas_call x1, Pallas kernels, attend(): pl.pallas_call(functools.partial(attend_kernel, count, patch, head, seq_s...  31.2 us
    pallas_call x1, Pallas kernels, outputs(): pl.pallas_call(outputs_kernel, grid=(items,), in_specs=[item(padded), ite...  4.24 us

profile of v4, /device:TPU:0, one launch (start us, length us, event | category | flops | bytes accessed | tf_op | source)
XLA Modules:
  0.0 195.3 jit_solution(16549794101464492713)
XLA Ops:
  0.7 34.9 %front.1 = (bf16[4,2,2,2,16,896]{5,4,3,2,1,0:T(8,128)(2,1)}, bf16[4,2,2,2,16,768]{5,4,3,2,1,0:T(8,128)(2,1)}, f32[128,512]{1,0:T(8,128)}, f32[3,1,128]{2,1,0:T(1...) custom-call(bf16[16,1536]{1,0:T(8,128)(2,1)} %refs_0_.1, ...), custom_call_target="tpu_custom_call" | custom-call | tf_op jit(solution)/shard_map/front/pallas_call | solution.py:637
  35.6 31.2 %attend.1 = (bf16[3,560,512]{2,1,0:T(8,128)(2,1)}, bf16[3,560,512]{2,1,0:T(8,128)(2,1)}, f32[3,560,512]{2,1,0:T(8,128)}, bf16[4,2,2,2,16,2560]{5,4,3,2,1,0:T(8,128)(2,1)}, bf16[4,2,2,2,64,640]{5,4,3,2,1,0:T(8,128)(2,1)}) custom-call(bf16[3,560,512]{2,1,0:T(8,128)(2,1)} %get-tuple-element.67.refs_0_, bf16[3,560,512]{2,1,0:T(8,128)(2,1)} %get-tuple-element.68.refs_1_, ...), custom_call_target="tpu_custom_call" | custom-call | tf_op jit(solution)/shard_map/attend/pallas_call | solution.py:783
  66.8 39.3 %ffn.1 = (bf16[3,512,512]{2,1,0:T(8,128)(2,1)}, bf16[3,48,512]{2,1,0:T(8,128)(2,1)}, bf16[3,560,512]{2,1,0:T(8,128)(2,1)}, bf16[3,560,512]{2,1,0:T(8,128)(2,1)},...) custom-call(s32[1]{0:T(128)} %bitcast.seq_ref, bf16[3,512,512]{2,1,0:T(8,128)(2,1)} %refs_16_.1, ...), custom_call_target="tpu_custom_call" | custom-call | tf_op jit(solution)/shard_map/ffn/pallas_call | solution.py:924
  106.1 84.8 %back.1 = (bf16[3,512,512]{2,1,0:T(8,128)(2,1)}, bf16[3,96,512]{2,1,0:T(8,128)(2,1)}, bf16[3,96,512]{2,1,0:T(8,128)(2,1)}, f32[16,2560]{1,0:T(8,128)}, f32[64,51...) custom-call(bf16[3,560,512]{2,1,0:T(8,128)(2,1)} %get-tuple-element.67.refs_0_,, ...), custom_call_target="tpu_custom_call" | custom-call | tf_op jit(solution)/shard_map/back/pallas_call | solution.py:1207
  190.9 4.2 %outputs.1 = (bf16[3,77,512]{2,1,0:T(8,128)(2,1)}, bf16[3,512,512]{2,1,0:T(8,128)(2,1)}, bf16[3,77,512]{2,1,0:T(8,128)(2,1)}, f32[16]{0:T(128)}, f32[16]{0:T(128...) custom-call(bf16[3,96,512]{2,1,0:T(8,128)(2,1)} %get-tuple-element.9, ...), custom_call_target="tpu_custom_call" | custom-call | tf_op jit(solution)/shard_map/outputs/pallas_call | solution.py:1306

commit v5 on v4

--- a/solution.py
+++ b/solution.py
@@ -97,14 +97,18 @@
         core = self.core * (1 - core) + (1 - self.core) * core
         return self.device(self.z, y, x, core), (y, x, core)
 
+    def friends(self, corners):
+        friends = [self.above(k) for k in range(1, self.depth)]
+        friends += [self.octant(n)[0] for n in range(1, 8)] if corners else [self.first(), self.second(), self.other_core()]
+        return friends + [self.mate(step) for step in range(1, self.seq_size)]
+
     def greet(self, corners=False):
         barrier = pltpu.get_barrier_semaphore()
-        friends = [self.above(k) for k in range(1, self.depth)]
-        friends += [self.octant(n)[0] for n in range(1, 8)] if corners else [self.first(), self.second(), self.other_core()]
-        friends += [self.mate(step) for step in range(1, self.seq_size)]
-        for friend in friends:
+        for friend in self.friends(corners):
             pl.semaphore_signal(barrier, inc=1, device_id=friend, device_id_type=MESH)
-        pl.semaphore_wait(barrier, len(friends))
+
+    def meet(self, corners=False):
+        pl.semaphore_wait(pltpu.get_barrier_semaphore(), len(self.friends(corners)))
 
 
 def remote(src, dst, send, recv, device):
@@ -211,14 +215,13 @@
 
     def line_copy(self, k):
         here = self.quads.at[0, self.place.z]
-        return remote(self.shard, here, self.out.at[1 + k], self.into.at[1 + k], self.place.above(k))
+        return remote(self.shard, here, self.out.at[k], self.into.at[k], self.place.above(k))
 
     def own_copy(self):
-        return pltpu.make_async_copy(self.shard, self.quads.at[0, self.place.z], self.local.at[3])
-
-    def way_copy(self, way):
-        device = (self.place.first, self.place.second)[way]()
-        return remote(self.quads.at[0], self.quads.at[1 + way], self.out.at[way], self.into.at[way], device)
+        return pltpu.make_async_copy(self.shard, self.quads.at[0, self.place.z], self.local.at[2])
+
+    def way_copy(self):
+        return remote(self.quads.at[0], self.quads.at[1], self.out.at[0], self.into.at[0], self.place.first())
 
     def result_copy(self, n):
         return pltpu.make_async_copy(self.quads.at[n], self.result.at[n], self.local.at[n])
@@ -232,31 +235,47 @@
         self.own_copy().wait()
         for k in range(1, self.place.depth):
             self.line_copy(k).wait_recv()
-        for way in range(2):
-            self.way_copy(way).start()
+        self.way_copy().start()
         self.result_copy(0).start()
 
     def finish(self):
-        for way in range(2):
-            self.way_copy(way).wait_recv()
-            self.result_copy(1 + way).start()
+        self.way_copy().wait_recv()
+        self.result_copy(1).start()
         for k in range(1, self.place.depth):
             self.line_copy(k).wait_send()
-        for way in range(2):
-            self.way_copy(way).wait_send()
-        for n in range(3):
+        self.way_copy().wait_send()
+        for n in range(2):
             self.result_copy(n).wait()
 
 
 def early_sems(depth):
     sems = pltpu.SemaphoreType.DMA
-    return [sems((1 + depth,)), sems((1 + depth,)), sems((4,))]
-
-
-class Late:
-    def __init__(self, place, quads, full, result, out, into, local):
+    return [sems((depth,)), sems((depth,)), sems((3,))]
+
+
+class Results:
+    def result_copy(self, n, other):
+        y, x = self.place.columns[(0, 2, 1, 3)[n] if other else n]
+        core = 1 - self.place.core if other else self.place.core
+        here = (slice(None), y, x, core)
+        return pltpu.make_async_copy(self.full.at[here], self.result.at[here], self.results.at[n, other])
+
+    def land(self, n):
+        self.arrive_core(n)
+        for other in range(2):
+            self.result_copy(n, other).start()
+
+    def finish(self):
+        for n in range(4):
+            for other in range(2):
+                self.result_copy(n, other).wait()
+        self.sent()
+
+
+class Late(Results):
+    def __init__(self, place, quads, full, result, out, into, local, results):
         self.place, self.quads, self.full, self.result = place, quads, full, result
-        self.out, self.into, self.local = out, into, local
+        self.out, self.into, self.local, self.results = out, into, local, results
 
     def column(self, n):
         y, x = self.place.columns[n]
@@ -265,54 +284,53 @@
     def own_copy(self, n):
         return pltpu.make_async_copy(self.quads.at[n], self.column(n), self.local.at[n])
 
-    def way_copy(self):
-        here = self.column(1)
-        return remote(here, here, self.out.at[4], self.into.at[4], self.place.second())
+    def way_copy(self, n):
+        here = self.column(n)
+        return remote(here, here, self.out.at[4 + n], self.into.at[4 + n], self.place.second())
 
     def core_copy(self, n):
         here = self.column(n)
         return remote(here, here, self.out.at[n], self.into.at[n], self.place.other_core())
 
-    def result_copy(self):
-        return pltpu.make_async_copy(self.full, self.result, self.local.at[3])
+    def arrive_core(self, n):
+        self.core_copy(n).wait_recv()
 
     def start(self):
-        for n in range(3):
+        for n in range(2):
             self.own_copy(n).start()
 
     def send(self):
-        for n in (1, 0, 2):
+        for n in range(2):
             self.own_copy(n).wait()
-            if n == 1:
-                self.way_copy().start()
+            self.way_copy(n).start()
             self.core_copy(n).start()
 
-    def forward(self):
-        self.way_copy().wait_recv()
-        self.core_copy(3).start()
-
-    def finish(self):
+    def forward(self, n):
+        self.way_copy(n).wait_recv()
+        self.core_copy(2 + n).start()
+
+    def sent(self):
         for n in range(4):
-            self.core_copy(n).wait()
-        self.way_copy().wait_send()
-        self.result_copy().start()
+            self.core_copy(n).wait_send()
+        for n in range(2):
+            self.way_copy(n).wait_send()
 
 
 def late_sems():
     sems = pltpu.SemaphoreType.DMA
-    return [sems((5,)), sems((5,)), sems((4,))]
-
-
-class LateLine(Spread):
-    def __init__(self, place, line, full, result, out, into, local):
-        super().__init__(place, line, full, out, into, local)
-        self.result = result
+    return [sems((6,)), sems((6,)), sems((2,)), sems((4, 2))]
+
+
+class LateLine(Results, Spread):
+    def __init__(self, place, line, full, result, out, into, local, results):
+        Spread.__init__(self, place, line, full, out, into, local)
+        self.result, self.results = result, results
 
     def own_copy(self):
-        return pltpu.make_async_copy(self.shard, self.column(0), self.local.at[0])
-
-    def result_copy(self):
-        return pltpu.make_async_copy(self.full, self.result, self.local.at[1])
+        return pltpu.make_async_copy(self.shard, self.column(0), self.local)
+
+    def arrive_core(self, n):
+        self.arrive(n, 3 + n)
 
     def start(self):
         self.own_copy().start()
@@ -322,17 +340,14 @@
         for lane in (0, 1, 3):
             self.copy(0, lane).start()
 
-    def finish(self):
-        for n in range(4):
-            self.arrive(n, 3 + n)
+    def sent(self):
         for lane in range(7):
             self.copy(0, lane).wait_send()
-        self.result_copy().start()
 
 
 def late_line_sems():
     sems = pltpu.SemaphoreType.DMA
-    return [sems((7,)), sems((7,)), sems((2,))]
+    return [sems((7,)), sems((7,)), sems, sems((4, 2))]
 
 
 class Reduce:
@@ -526,13 +541,13 @@
     x_copies = [pltpu.make_async_copy(x_any.at[i], x_s.at[i], x_sem.at[i]) for i in range(items)]
     for copy in x_copies:
         copy.start()
-    for p in range(pairs):
-        half, to = divmod(3 * p * width, wide)
+    place.greet()
+    for half, to in enumerate((shard, shard2)):
         for n in range(3):
-            at = n * model + p * width
-            (shard, shard2)[half][:, to + n * width : to + (n + 1) * width] = shard_ref[:, at : at + width]
+            at = (n + 1) % 3 * model + half * (model // 2)
+            to[:, n * (model // 2) : (n + 1) * (model // 2)] = shard_ref[:, at : at + model // 2]
     shard[:, wide:] = as_columns([ref[...] for ref in vec_refs])
-    place.greet()
+    place.meet()
     halves = [Spread(place, shard, w_full, *sems), Spread(place, shard2, w2_full, *sems2)]
     for move in halves:
         move.start()
@@ -572,15 +587,12 @@
     scale = LOG2E / math.sqrt(model // HEADS)
     sends, outs = [], []
 
-    def project(i, half, weight):
-        for p in range(half * pairs // 2, (half + 1) * pairs // 2):
-            cols = slice(p * width, (p + 1) * width)
-            at = 3 * p * width - half * wide
-            projected = mm(first_s[i], weight[:, at : at + 3 * width])
-            q_s[i, :, cols] = ((projected[:, :width] + table[QBIAS : QBIAS + 1, cols]) * scale).astype(bf16)
-            k_s[0, i, :, cols] = projected[:, width : 2 * width].astype(bf16)
-            v_s[0, i, :, cols] = (projected[:, 2 * width :] + table[VBIAS : VBIAS + 1, cols]).astype(bf16)
-        cols = pl.ds(half * (model // 2), model // 2)
+    def keys_and_values(i, half, weight):
+        span = model // 2
+        cols = pl.ds(half * span, span)
+        projected = mm(first_s[i], weight[:, : 2 * span])
+        k_s[0, i, :, cols] = projected[:, :span].astype(bf16)
+        v_s[0, i, :, cols] = (projected[:, span:] + table[VBIAS : VBIAS + 1, half * span : (half + 1) * span]).astype(bf16)
         for r in range(1, seq_size):
             for n, ref in enumerate((k_s, v_s)):
                 at = ((2 * i + n) * 2 + half) * seq_size + r
@@ -588,6 +600,11 @@
                 sends.append(remote(src, dst, kv_sem.at[at], kv_in_sem.at[at], place.mate(r)))
                 sends[-1].start()
 
+    def queries(i, half, weight):
+        span = model // 2
+        q = mm(first_s[i], weight[:, 2 * span : 3 * span]) + table[QBIAS : QBIAS + 1, half * span : (half + 1) * span]
+        q_s[i, :, half * span : (half + 1) * span] = (q * scale).astype(bf16)
+
     def bring(n, src, dst, i):
         outs.append(pltpu.make_async_copy(src.at[i], dst.at[i], out_sem.at[n, i]))
         outs[-1].start()
@@ -595,17 +612,21 @@
     for i in range(items):
         first_s[i] = (n_s[i] * table[GAIN1 : GAIN1 + 1] + table[SHIFT1 : SHIFT1 + 1]).astype(bf16)
         bring(0, first_s, first_out, i)
-        project(i, 0, weight)
+        keys_and_values(i, 0, weight)
         if i == 0:
             halves[1].forward_second(1)
     early.send()
     halves[1].finish()
     w_copies[1].start()
-    weight = w2_full[...].reshape(model, wide)
+    weight2 = w2_full[...].reshape(model, wide)
     for i in range(items):
-        project(i, 1, weight)
-        for n, (src, dst) in enumerate(((q_s, q_out), (k_s.at[0], k_outs[0]), (v_s.at[0], v_outs[0]))):
-            bring(1 + n, src, dst, i)
+        keys_and_values(i, 1, weight2)
+        bring(1, k_s.at[0], k_outs[0], i)
+        bring(2, v_s.at[0], v_outs[0], i)
+    for i in range(items):
+        queries(i, 0, weight)
+        queries(i, 1, weight2)
+        bring(3, q_s, q_out, i)
     line.finish()
     for copy in sends:
         copy.wait()
@@ -643,7 +664,7 @@
             jax.ShapeDtypeStruct(shape_w2, bf16),
             jax.ShapeDtypeStruct((LANES, model), f32),
             jax.ShapeDtypeStruct((items, 1, tail), f32),
-            jax.ShapeDtypeStruct((3, depth) + shape_a, bf16),
+            jax.ShapeDtypeStruct((2, depth) + shape_a, bf16),
             jax.ShapeDtypeStruct((depth,) + shape_b, bf16),
             jax.ShapeDtypeStruct((items, text, model), bf16),
             tokens,
@@ -657,7 +678,7 @@
             pltpu.VMEM(shape_b, bf16),
             pltpu.VMEM(shape_w, bf16),
             pltpu.VMEM(shape_w2, bf16),
-            pltpu.VMEM((3, depth) + shape_a, bf16),
+            pltpu.VMEM((2, depth) + shape_a, bf16),
             pltpu.VMEM((depth,) + shape_b, bf16),
             pltpu.VMEM(patches.shape, bf16),
             pltpu.VMEM(shape_x, f32),
@@ -709,23 +730,30 @@
     place = Place(full_a.shape[0], seq_size)
     turn = pl.program_id(0) * pl.num_programs(1) + pl.program_id(1)
     last = pl.num_programs(0) * pl.num_programs(1) - 1
-    move_a, move_b = Late(place, quads_a, into_a, full_a, *sems[:3]), LateLine(place, line_b, into_b, full_b, *sems[3:])
+    move_a, move_b = Late(place, quads_a, into_a, full_a, *sems[:4]), LateLine(place, line_b, into_b, full_b, *sems[4:])
 
     @pl.when(turn == 0)
     def _():
+        place.greet()
         move_a.start()
         move_b.start()
-        place.greet()
-        move_a.send()
-        move_b.send()
 
     agenda = (
-        (4, move_a.forward),
-        (4, move_b.forward_first),
+        (1, place.meet),
+        (1, move_b.send),
+        (1, move_a.send),
+        (5, move_b.forward_first),
         (6, functools.partial(move_b.forward_second, 0)),
-        (7, functools.partial(move_b.forward_second, 1)),
-        (9, move_a.finish),
-        (9, move_b.finish),
+        (6, functools.partial(move_b.land, 0)),
+        (7, functools.partial(move_a.land, 0)),
+        (7, functools.partial(move_a.land, 1)),
+        (8, functools.partial(move_a.forward, 0)),
+        (8, functools.partial(move_a.forward, 1)),
+        (9, functools.partial(move_b.land, 1)),
+        (9, functools.partial(move_b.land, 2)),
+        (10, functools.partial(move_a.land, 2)),
+        (10, functools.partial(move_a.land, 3)),
+        (10, functools.partial(move_b.forward_second, 1)),
     )
     for at in sorted({at for at, _ in agenda}):
 
@@ -771,8 +799,9 @@
 
     @pl.when(turn == last)
     def _():
-        move_a.result_copy().wait()
-        move_b.result_copy().wait()
+        move_b.land(3)
+        move_a.finish()
+        move_b.finish()
 
 
 def attend(q, keys, values, bias, halfway, patch, head, width, devices, seq_size):
@@ -969,10 +998,11 @@
     keys, values, text_keys, text_values, probs_s, scores_s = take(6)
     mixed_s, own_s, dkv_out, dkv_in, sums_s = take(5)
     w_s, w2_s, first_s, x_s, xtext_s, gb_s, text_s, patch_s = take(8)
+    first_grad_s, scaled_s, inverse_s = take(3)
     fetch_sem, dkv_sem, dkv_in_sem, text_sem, text_in_sem, patch_sem = take(6)
     scratch_a, scratch_b = take(10), take(10)
-    scratch_in = [take(11) for _ in range(pairs)]
-    scratch_vec = take(6)
+    scratch_in = [take(11) for _ in range(2)]
+    scratch_last, scratch_vec = take(6), take(6)
 
     width, rows = q_ref.shape[2], q_ref.shape[1]
     text, model = rows - patch, pairs * width
@@ -981,7 +1011,9 @@
     p, i = pl.program_id(0), pl.program_id(1)
     turn, last = p * items + i, pairs * items - 1
     sums_a, sums_b = Reduce(place, part_a, *scratch_a), Reduce(place, part_b, *scratch_b)
+    chunks = ((0, pairs - 2), (pairs - 2, pairs - 1), (pairs - 1, pairs))
     sums_in = [Reduce(place, each[0], *each[1:]) for each in scratch_in]
+    sums_in.append(ShortReduce(place, *scratch_last))
     sums_vec = ShortReduce(place, *scratch_vec)
     fetches = [
         pltpu.make_async_copy(src, dst, fetch_sem.at[n])
@@ -997,6 +1029,13 @@
             remote(src, to, text_sem.at[row, r], text_in_sem.at[row, r], place.mate(r)) for r in range(1, seq_size)
         ]
         return [own] + away
+
+    def begin():
+        place.meet(corners=True)
+        sums_a.to_core()
+        sums_b.to_core()
+        for copy in text_copies(restext_any, text_out, 0):
+            copy.start()
 
     def dkv_copy(slot, r):
         return remote(
@@ -1018,17 +1057,25 @@
         if pair == 0:
             fetches[0].wait()
         grad = t_mm(first_s[...].reshape(items * rows, model), mixed).astype(bf16)
-        sums_in[pair].part[...] = grad.reshape(sums_in[pair].part.shape)
-        sums_in[pair].to_core()
+        chunk = sum(pair >= first for first, _ in chunks) - 1
+        first, end = chunks[chunk]
+        part = sums_in[chunk].part
+        part[..., 3 * (pair - first) * width : 3 * (pair - first + 1) * width] = grad.reshape(
+            part.shape[:-1] + (3 * width,)
+        )
+        if pair == end - 1:
+            (sums_in[chunk].start if end == pairs else sums_in[chunk].to_core)()
         cols = slice(pair * width, (pair + 1) * width)
         sums_s[QBIAS : QBIAS + 1, cols] = column_sum(mixed[:, :width])
         sums_s[VBIAS : VBIAS + 1, cols] = column_sum(mixed[:, 2 * width :])
 
-    def finish_in(pair):
-        total = sums_in[pair].last()
-        for n in range(3):
-            at = n * model + pair * width
-            total_in[:, at : at + width] = total[:, n * width : (n + 1) * width]
+    def finish_in(chunk):
+        total = sums_in[chunk].last()
+        first, end = chunks[chunk]
+        for m in range(end - first):
+            for n in range(3):
+                at, of = n * model + (first + m) * width, (3 * m + n) * width
+                total_in[:, at : at + width] = total[:, of : of + width]
 
     def finish_a():
         total = sums_a.last()
@@ -1040,32 +1087,23 @@
         total_b[...] = total[:, :model]
         upb_out[...] = total[:, model:]
 
-    agenda = [(1, sums_a.to_second), (2, sums_b.to_second), (4, sums_a.to_first), (6, sums_b.to_first),
-              (6, sums_a.to_line), (8, sums_b.to_line), (8, finish_a), (11, finish_b)]
-    for pair in range(pairs):
-        done = items * (pair + 1)
-        steps = (sums_in[pair].to_second, sums_in[pair].to_first, sums_in[pair].to_line, functools.partial(finish_in, pair))
-        agenda += [(done + 1 + n, step) for n, step in enumerate(steps)]
+    tail_at = last + 1
+    agenda = [(2, sums_a.to_second), (3, sums_b.to_second), (5, sums_a.to_first), (7, sums_b.to_first),
+              (8, sums_a.to_line), (9, sums_b.to_line), (11, finish_a), (tail_at + 1, finish_b)]
+    turns_in = ((9, 10, 11, tail_at + 1), (11, tail_at, tail_at + 1, tail_at + 2))
+    for chunk, turns in enumerate(turns_in):
+        steps = (sums_in[chunk].to_second, sums_in[chunk].to_first, sums_in[chunk].to_line)
+        steps += (functools.partial(finish_in, chunk),)
+        agenda += [(max(at, items * chunks[chunk][1] + 2), step) for at, step in zip(turns, steps)]
+    agenda += [(tail_at + 1, sums_in[2].to_line), (tail_at + 3, functools.partial(finish_in, 2))]
     agenda.sort(key=lambda entry: entry[0])
 
     @pl.when(turn == 0)
     def _():
         place.greet(corners=True)
-        sums_a.to_core()
-        sums_b.to_core()
         for copy in fetches:
             copy.start()
-        for copy in text_copies(restext_any, text_out, 0):
-            copy.start()
         sums_s[...] = jnp.zeros_like(sums_s)
-
-    for at in sorted({at for at, _ in agenda if at <= last}):
-
-        @pl.when(turn == at)
-        def _(at=at):
-            for when, step in agenda:
-                if when == at:
-                    step()
 
     collect(keys, k_refs, patch, text)
     collect(values, v_refs, patch, text)
@@ -1115,6 +1153,19 @@
 
     text_dv, text_dk = of_heads(t_mm(grad, text_probs)), of_heads(t_mm(q, text_grads)) * LN2
     slot = lax.rem(turn, 2)
+
+    @pl.when(turn == 0)
+    def _():
+        begin()
+
+    for at in sorted({at for at, _ in agenda if at <= last}):
+
+        @pl.when(turn == at - 1)
+        def _(at=at):
+            for when, step in agenda:
+                if when == at:
+                    step()
+
     at = pl.ds(pl.multiple_of(i * rows, ROW_TILE), rows)
     mixed_s[p, at, :width] = (dq * (1.0 / math.sqrt(head))).astype(bf16)
     own_s[slot, :patch, :width] = dk[:patch]
@@ -1146,40 +1197,57 @@
 
     @pl.when(turn == last)
     def _():
-        left = [step for when, step in agenda if when > last]
+        left = [[step for when, step in agenda if when == at] for at in sorted({at for at, _ in agenda if at > last})]
+
+        def more():
+            if left:
+                for step in left.pop(0):
+                    step()
+
+        half = pairs // 2
+        sides = (w_s.at[:, : 3 * half * width], w2_s)
+
+        def grad_first(item, side):
+            at = slice(item * rows, (item + 1) * rows)
+            mixed = [
+                mixed_s[side * half + m, at, n * width : (n + 1) * width] for n in (1, 2, 0) for m in range(half)
+            ]
+            return mm_t(jnp.concatenate(mixed, axis=1), sides[side][...])
+
+        for copy in fetches[1:]:
+            copy.wait()
+        for item in range(items):
+            first_grad_s[item] = grad_first(item, 0)
         settle(last)
         pair_done(pairs - 1)
-        for copy in fetches[1:]:
-            copy.wait()
+        for item in range(items):
+            grad = first_grad_s[item] + grad_first(item, 1)
+            first_grad_s[item] = grad
+            scaled, inverse = norm_rows(jnp.concatenate([x_s[item], xtext_s[item]], axis=0).astype(f32))
+            scaled_s[item] = scaled
+            inverse_s[item] = jnp.broadcast_to(inverse, (rows, LANES))
+            sums_s[GAIN1 : GAIN1 + 1, :] += column_sum(grad * scaled)
+            sums_s[SHIFT1 : SHIFT1 + 1, :] += column_sum(grad)
+        sums_vec.part[...] = to_columns(sums_s[...]).reshape(sums_vec.part.shape)
+        sums_vec.start()
+        more()
+        gain = vec_ref[GAIN1 : GAIN1 + 1]
         patch_copies = [
             pltpu.make_async_copy(patch_s.at[item], grad_out.at[item], patch_sem.at[item]) for item in range(items)
         ]
-        gain = vec_ref[GAIN1 : GAIN1 + 1]
         for item in range(items):
-            half, at = pairs // 2, slice(item * rows, (item + 1) * rows)
-            grad_first = sum(
-                mm_t(jnp.concatenate([mixed_s[n * half + m, at, :] for m in range(half)], axis=1), ref[...])
-                for n, ref in enumerate((w_s.at[:, : 3 * half * width], w2_s))
-            )
-            scaled, inverse = norm_rows(jnp.concatenate([x_s[item], xtext_s[item]], axis=0).astype(f32))
-            grad_rows = gb_s[item].astype(f32) + norm_back(grad_first, scaled, inverse, gain)
-            grad_rows = grad_rows.astype(bf16)
+            grad_rows = norm_back(first_grad_s[item], scaled_s[item], inverse_s[item][:, :1], gain)
+            grad_rows = (gb_s[item].astype(f32) + grad_rows).astype(bf16)
             patch_s[item] = grad_rows[:patch]
             patch_copies[item].start()
             text_s[item] = grad_rows[patch:]
-            sums_s[GAIN1 : GAIN1 + 1, :] += column_sum(grad_first * scaled)
-            sums_s[SHIFT1 : SHIFT1 + 1, :] += column_sum(grad_first)
-            if left:
-                left.pop(0)()
+            if item == 0:
+                sums_vec.to_line()
+            more()
         for copy in text_copies(text_s, text_grad_out, 1):
             copy.start()
-        sums_vec.part[...] = to_columns(sums_s[...]).reshape(sums_vec.part.shape)
-        sums_vec.start()
-        if left:
-            left.pop(0)()
-        sums_vec.to_line()
-        for step in left:
-            step()
+        while left:
+            more()
         vec_out[...] = sums_vec.last()
         for copies in (text_copies(restext_any, text_out, 0), text_copies(text_s, text_grad_out, 1)):
             for copy in copies:
@@ -1203,7 +1271,10 @@
     sems = pltpu.SemaphoreType.DMA
     others = seq_size - 1
     slots = jax.ShapeDtypeStruct((items, seq_size * text, model), bf16)
-    scratch_in = [pltpu.VMEM((depth, 2, 2, 2, rows_a, 3 * width), bf16)] + reduce_scratch(depth, rows_a, 3 * width)
+    scratch_in = []
+    for cols in (3 * (pairs - 2) * width, 3 * width):
+        scratch_in += [pltpu.VMEM((depth, 2, 2, 2, rows_a, cols), bf16)] + reduce_scratch(depth, rows_a, cols)
+    scratch_in += short_reduce_scratch(depth, rows_a, 3 * width)
     return pl.pallas_call(
         functools.partial(back_kernel, count, patch, head, seq_size, pairs, items),
         grid=(pairs, items),
@@ -1245,6 +1316,9 @@
             pltpu.VMEM(grad_branch.shape, bf16),
             pltpu.VMEM(x_text.shape, bf16),
             pltpu.VMEM(patches.shape, bf16),
+            pltpu.VMEM(q.shape, f32),
+            pltpu.VMEM(q.shape, f32),
+            pltpu.VMEM((items, rows, LANES), f32),
             sems((6,)),
             sems((2, others)),
             sems((2, others)),
@@ -1254,7 +1328,7 @@
         ]
         + reduce_scratch(depth, rows_a, cols_a)
         + reduce_scratch(depth, rows_b, cols_b)
-        + scratch_in * pairs
+        + scratch_in
         + short_reduce_scratch(depth, rows_a, LANES),
         compiler_params=compiler_params(collective_id=2, has_side_effects=True),
         name="back",

time: 196 us -> 179 us (0.913)
  Pallas kernels: 194 us -> 178 us
    pallas_call x1, Pallas kernels: 84.8 us -> 72.4 us  [back(): pl.pallas_call(functools.partial(back_kernel, count, patch, head, seq_siz...]
    pallas_call x1, Pallas kernels: 34.9 us -> 31.3 us  [front(): pl.pallas_call(functools.partial(front_kernel, seq_size, text, width), in...]
where the time goes in v5:
time: 179 us
  Pallas kernels  178 us (99%)
    pallas_call x1, Pallas kernels, back(): pl.pallas_call(functools.partial(back_kernel, count, patch, head, seq_siz...  72.4 us
    pallas_call x1, Pallas kernels, ffn(): pl.pallas_call(functools.partial(ffn_kernel, items, 1024), grid=(items,),...  39.3 us
    pallas_call x1, Pallas kernels, front(): pl.pallas_call(functools.partial(front_kernel, seq_size, text, width), in...  31.3 us
    pallas_call x1, Pallas kernels, attend(): pl.pallas_call(functools.partial(attend_kernel, count, patch, head, seq_s...  30.6 us
    pallas_call x1, Pallas kernels, outputs(): pl.pallas_call(outputs_kernel, grid=(items,), in_specs=[item(padded), ite...  4.24 us

profile of v5, /device:TPU:0, one launch (start us, length us, event | category | flops | bytes accessed | tf_op | source)
XLA Modules:
  0.0 178.8 jit_solution(15997131208674468058)
XLA Ops:
  0.7 31.3 %front.1 = (bf16[4,2,2,2,16,896]{5,4,3,2,1,0:T(8,128)(2,1)}, bf16[4,2,2,2,16,768]{5,4,3,2,1,0:T(8,128)(2,1)}, f32[128,512]{1,0:T(8,128)}, f32[3,1,128]{2,1,0:T(1...) custom-call(bf16[16,1536]{1,0:T(8,128)(2,1)} %refs_0_.1, ...), custom_call_target="tpu_custom_call" | custom-call | tf_op jit(solution)/shard_map/front/pallas_call | solution.py:658
  32.0 30.6 %attend.1 = (bf16[3,560,512]{2,1,0:T(8,128)(2,1)}, bf16[3,560,512]{2,1,0:T(8,128)(2,1)}, f32[3,560,512]{2,1,0:T(8,128)}, bf16[4,2,2,2,16,2560]{5,4,3,2,1,0:T(8,128)(2,1)}, bf16[4,2,2,2,64,640]{5,4,3,2,1,0:T(8,128)(2,1)}) custom-call(bf16[3,560,512]{2,1,0:T(8,128)(2,1)} %get-tuple-element.67.refs_0_, bf16[3,560,512]{2,1,0:T(8,128)(2,1)} %get-tuple-element.68.refs_1_, ...), custom_call_target="tpu_custom_call" | custom-call | tf_op jit(solution)/shard_map/attend/pallas_call | solution.py:812
  62.6 39.3 %ffn.1 = (bf16[3,512,512]{2,1,0:T(8,128)(2,1)}, bf16[3,48,512]{2,1,0:T(8,128)(2,1)}, bf16[3,560,512]{2,1,0:T(8,128)(2,1)}, bf16[3,560,512]{2,1,0:T(8,128)(2,1)},...) custom-call(s32[1]{0:T(128)} %bitcast.seq_ref, bf16[3,512,512]{2,1,0:T(8,128)(2,1)} %refs_16_.1, ...), custom_call_target="tpu_custom_call" | custom-call | tf_op jit(solution)/shard_map/ffn/pallas_call | solution.py:953
  101.9 72.4 %back.1 = (bf16[3,512,512]{2,1,0:T(8,128)(2,1)}, bf16[3,96,512]{2,1,0:T(8,128)(2,1)}, bf16[3,96,512]{2,1,0:T(8,128)(2,1)}, f32[16,2560]{1,0:T(8,128)}, f32[64,51...) custom-call(bf16[3,560,512]{2,1,0:T(8,128)(2,1)} %get-tuple-element.67.refs_0_,, ...), custom_call_target="tpu_custom_call" | custom-call | tf_op jit(solution)/shard_map/back/pallas_call | solution.py:1278
  174.3 4.2 %outputs.1 = (bf16[3,77,512]{2,1,0:T(8,128)(2,1)}, bf16[3,512,512]{2,1,0:T(8,128)(2,1)}, bf16[3,77,512]{2,1,0:T(8,128)(2,1)}, f32[16]{0:T(128)}, f32[16]{0:T(128...) custom-call(bf16[3,96,512]{2,1,0:T(8,128)(2,1)} %get-tuple-element.9, ...), custom_call_target="tpu_custom_call" | custom-call | tf_op jit(solution)/shard_map/outputs/pallas_call | solution.py:1380

commit v6 on v5

--- a/solution.py
+++ b/solution.py
@@ -177,82 +177,6 @@
     return [sems((6 + depth,)), sems((6 + depth,)), sems]
 
 
-class Line:
-    def __init__(self, place, shard, line, result, out, into, local):
-        self.place, self.shard, self.line, self.result = place, shard, line, result
-        self.out, self.into, self.local = out, into, local
-
-    def line_copy(self, k):
-        return remote(self.shard, self.line.at[self.place.z], self.out.at[k], self.into.at[k], self.place.above(k))
-
-    def own_copy(self):
-        return pltpu.make_async_copy(self.shard, self.line.at[self.place.z], self.local.at[0])
-
-    def result_copy(self):
-        return pltpu.make_async_copy(self.line, self.result, self.local.at[1])
-
-    def start(self):
-        self.own_copy().start()
-        for k in range(1, self.place.depth):
-            self.line_copy(k).start()
-
-    def finish(self):
-        self.own_copy().wait()
-        for k in range(1, self.place.depth):
-            self.line_copy(k).wait()
-        self.result_copy().start()
-
-
-def line_sems(depth):
-    sems = pltpu.SemaphoreType.DMA
-    return [sems((depth,)), sems((depth,)), sems((2,))]
-
-
-class Early:
-    def __init__(self, place, shard, quads, result, out, into, local):
-        self.place, self.shard, self.quads, self.result = place, shard, quads, result
-        self.out, self.into, self.local = out, into, local
-
-    def line_copy(self, k):
-        here = self.quads.at[0, self.place.z]
-        return remote(self.shard, here, self.out.at[k], self.into.at[k], self.place.above(k))
-
-    def own_copy(self):
-        return pltpu.make_async_copy(self.shard, self.quads.at[0, self.place.z], self.local.at[2])
-
-    def way_copy(self):
-        return remote(self.quads.at[0], self.quads.at[1], self.out.at[0], self.into.at[0], self.place.first())
-
-    def result_copy(self, n):
-        return pltpu.make_async_copy(self.quads.at[n], self.result.at[n], self.local.at[n])
-
-    def start(self):
-        self.own_copy().start()
-        for k in range(1, self.place.depth):
-            self.line_copy(k).start()
-
-    def send(self):
-        self.own_copy().wait()
-        for k in range(1, self.place.depth):
-            self.line_copy(k).wait_recv()
-        self.way_copy().start()
-        self.result_copy(0).start()
-
-    def finish(self):
-        self.way_copy().wait_recv()
-        self.result_copy(1).start()
-        for k in range(1, self.place.depth):
-            self.line_copy(k).wait_send()
-        self.way_copy().wait_send()
-        for n in range(2):
-            self.result_copy(n).wait()
-
-
-def early_sems(depth):
-    sems = pltpu.SemaphoreType.DMA
-    return [sems((depth,)), sems((depth,)), sems((3,))]
-
-
 class Results:
     def result_copy(self, n, other):
         y, x = self.place.columns[(0, 2, 1, 3)[n] if other else n]
@@ -272,82 +196,23 @@
         self.sent()
 
 
-class Late(Results):
-    def __init__(self, place, quads, full, result, out, into, local, results):
-        self.place, self.quads, self.full, self.result = place, quads, full, result
-        self.out, self.into, self.local, self.results = out, into, local, results
-
-    def column(self, n):
-        y, x = self.place.columns[n]
-        return self.full.at[:, y, x, self.place.core]
-
-    def own_copy(self, n):
-        return pltpu.make_async_copy(self.quads.at[n], self.column(n), self.local.at[n])
-
-    def way_copy(self, n):
-        here = self.column(n)
-        return remote(here, here, self.out.at[4 + n], self.into.at[4 + n], self.place.second())
-
-    def core_copy(self, n):
-        here = self.column(n)
-        return remote(here, here, self.out.at[n], self.into.at[n], self.place.other_core())
-
-    def arrive_core(self, n):
-        self.core_copy(n).wait_recv()
-
-    def start(self):
-        for n in range(2):
-            self.own_copy(n).start()
-
-    def send(self):
-        for n in range(2):
-            self.own_copy(n).wait()
-            self.way_copy(n).start()
-            self.core_copy(n).start()
-
-    def forward(self, n):
-        self.way_copy(n).wait_recv()
-        self.core_copy(2 + n).start()
-
-    def sent(self):
-        for n in range(4):
-            self.core_copy(n).wait_send()
-        for n in range(2):
-            self.way_copy(n).wait_send()
-
-
-def late_sems():
-    sems = pltpu.SemaphoreType.DMA
-    return [sems((6,)), sems((6,)), sems((2,)), sems((4, 2))]
-
-
-class LateLine(Results, Spread):
-    def __init__(self, place, line, full, result, out, into, local, results):
-        Spread.__init__(self, place, line, full, out, into, local)
+class Gather(Results, Spread):
+    def __init__(self, place, shard, full, result, out, into, local, results):
+        Spread.__init__(self, place, shard, full, out, into, local)
         self.result, self.results = result, results
-
-    def own_copy(self):
-        return pltpu.make_async_copy(self.shard, self.column(0), self.local)
 
     def arrive_core(self, n):
         self.arrive(n, 3 + n)
 
-    def start(self):
-        self.own_copy().start()
-
-    def send(self):
-        self.own_copy().wait()
-        for lane in (0, 1, 3):
-            self.copy(0, lane).start()
-
     def sent(self):
+        for k in range(1, self.place.depth):
+            self.line_copy(k).wait_send()
         for lane in range(7):
             self.copy(0, lane).wait_send()
 
 
-def late_line_sems():
-    sems = pltpu.SemaphoreType.DMA
-    return [sems((7,)), sems((7,)), sems, sems((4, 2))]
+def gather_sems(depth):
+    return spread_sems(depth) + [pltpu.SemaphoreType.DMA((4, 2))]
 
 
 class Reduce:
@@ -518,7 +383,27 @@
     return jnp.transpose(rows)[:length].astype(bf16)
 
 
-def front_kernel(seq_size, text, width, *refs):
+def collect(dst, blocks, patch, text):
+    count, width = len(blocks), blocks[0].shape[1]
+    for r, block in enumerate(blocks):
+        dst[r * patch : (r + 1) * patch, :width] = block[:patch]
+        at = count * patch + r * text
+        dst[at : at + text, :width] = block[patch:]
+    filled = count * (patch + text)
+    if dst.shape[0] > filled:
+        dst[filled:, :width] = jnp.zeros((dst.shape[0] - filled, width), dst.dtype)
+
+
+def by_head(dst, src, lane, heads, ones):
+    count, width = src.shape
+    for h in range(heads):
+        rows = slice(h * count, (h + 1) * count)
+        dst[rows, :width] = jnp.where(lane == h, src, jnp.zeros_like(src))
+        if ones:
+            dst[rows, width:] = jnp.where(lane == h, jnp.ones_like(src), jnp.zeros_like(src))
+
+
+def forward_kernel(seq_size, text, width, head, *refs):
     refs = list(refs)
 
     def take(number):
@@ -528,11 +413,12 @@
 
     (shard_ref,), vec_refs = take(1), take(8)
     up_ref, up_bias_ref, out_w_ref, down_ref, x_any, slot_ref, length_ref = take(7)
-    w_out, w2_out, vecs, bias_ref, quads_a, line_b, xtext_ref, first_out, q_out = take(9)
+    w_out, w2_out, vecs, bias_ref, full_a, full_b, xtext_ref, first_out, q_out, out_out, rest_out, log_out = take(12)
     k_outs, v_outs = take(seq_size), take(seq_size)
-    shard, shard2, shard_a, shard_b, w_full, w2_full, own_a, own_b, x_s, n_s, first_s, q_s, k_s, v_s = take(14)
-    sems, sems2, sems_a, sems_b = take(3), take(3), take(3), take(3)
-    x_sem, w_sem, out_sem, kv_sem, kv_in_sem, kv_out_sem = take(6)
+    shard, shard2, shard_a, shard_b, w_full, w2_full, into_a, into_b, x_s, n_s, first_s, q_s, k_s, v_s = take(14)
+    keys, values, text_keys, text_values, out_s, rest_s, log_s = take(7)
+    sems, sems2, sems_a, sems_b = take(3), take(3), take(4), take(4)
+    x_sem, w_sem, out_sem, kv_sem, kv_in_sem, kv_out_sem, turn_sem = take(7)
     items, patch, model = x_s.shape
     units, wide = up_ref.shape[1], shard2.shape[1]
     pairs = model // width
@@ -555,7 +441,7 @@
     shard_a[:, units:] = out_w_ref[...]
     shard_b[:, :model] = down_ref[...]
     shard_b[:, model:] = as_columns([up_bias_ref[...]])
-    early, line = Early(place, shard_a, own_a, quads_a, *sems_a), Line(place, shard_b, own_b, line_b, *sems_b)
+    move_a, move_b = Gather(place, shard_a, into_a, full_a, *sems_a), Gather(place, shard_b, into_b, full_b, *sems_b)
     tail = bias_ref.shape[2]
     col = lax.broadcasted_iota(jnp.int32, (1, tail), 1)
     slot = jnp.full((1, tail), seq_size * text, jnp.int32)
@@ -567,8 +453,8 @@
         bias_ref[i] = jnp.where(slot < length_ref[i], 0.0, NEG_FILL)
     halves[0].send_line()
     halves[1].send_line()
-    early.start()
-    line.start()
+    move_a.start()
+    move_b.start()
     for i in range(items):
         x_copies[i].wait()
         n_s[i], _ = norm_rows(jnp.concatenate([x_s[i], xtext_ref[i]], axis=0).astype(f32))
@@ -578,6 +464,7 @@
     halves[0].forward_second(1)
     halves[1].forward_second(0)
     halves[0].finish()
+    move_a.send_line()
     w_copies = [pltpu.make_async_copy(src, dst, w_sem.at[n]) for n, (src, dst) in
                 enumerate(((w_full, w_out), (w2_full, w2_out)))]
     w_copies[0].start()
@@ -615,8 +502,8 @@
         keys_and_values(i, 0, weight)
         if i == 0:
             halves[1].forward_second(1)
-    early.send()
     halves[1].finish()
+    move_b.send_line()
     w_copies[1].start()
     weight2 = w2_full[...].reshape(model, wide)
     for i in range(items):
@@ -627,214 +514,200 @@
         queries(i, 0, weight)
         queries(i, 1, weight2)
         bring(3, q_s, q_out, i)
-    line.finish()
+
+    edge, heads, span = seq_size * patch, width // head, keys.shape[0] - seq_size * patch
+    lane = lax.broadcasted_iota(jnp.int32, (1, width), 1) // head
+    values[:, width:] = jnp.ones((values.shape[0], values.shape[1] - width), bf16)
+    last = items * pairs - 1
+
+    def turn_copies(slot, i, cols):
+        return [
+            pltpu.make_async_copy(src.at[slot], dst.at[i, :, cols], turn_sem.at[slot, n])
+            for n, (src, dst) in enumerate(((out_s, out_out), (rest_s, rest_out), (log_s, log_out)))
+        ]
+
+    def kv_out_copies(i):
+        return [
+            pltpu.make_async_copy(ref.at[r, i], dst[r].at[i], kv_out_sem.at[(2 * i + n) * seq_size + r])
+            for n, (ref, dst) in enumerate(((k_s, k_outs), (v_s, v_outs)))
+            for r in range(1, seq_size)
+        ]
+
+    def exchanged(i):
+        for n, ref in enumerate((k_s, v_s)):
+            for half in range(2):
+                cols = pl.ds(half * (model // 2), model // 2)
+                for r in range(1, seq_size):
+                    at = ((2 * i + n) * 2 + half) * seq_size + r
+                    src, dst = ref.at[0, i, :, cols], ref.at[r, i, :, cols]
+                    remote(src, dst, kv_sem.at[at], kv_in_sem.at[at], place.mate(r)).wait_recv()
+        for copy in kv_out_copies(i):
+            copy.start()
+
+    agenda = (
+        (3, move_a.forward_first),
+        (3, functools.partial(move_a.forward_second, 0)),
+        (5, move_b.forward_first),
+        (5, functools.partial(move_b.forward_second, 0)),
+        (7, functools.partial(move_a.land, 0)),
+        (7, functools.partial(move_a.land, 1)),
+        (8, functools.partial(move_a.forward_second, 1)),
+        (9, functools.partial(move_a.land, 2)),
+        (9, functools.partial(move_b.land, 0)),
+        (9, functools.partial(move_b.land, 1)),
+        (10, functools.partial(move_b.forward_second, 1)),
+        (10, functools.partial(move_b.land, 2)),
+        (11, functools.partial(move_a.land, 3)),
+        (13, functools.partial(move_b.land, 3)),
+    )
+
+    def attend(turn, _):
+        i, p = turn // pairs, lax.rem(turn, pairs)
+        slot = lax.rem(turn, 2)
+        cols = pl.ds(pl.multiple_of(p * width, width), width)
+
+        @pl.when(p == 0)
+        def _():
+            exchanged(i)
+
+        for at in sorted({at for at, _ in agenda if at <= last}):
+
+            @pl.when(turn == at)
+            def _(at=at):
+                for when, step in agenda:
+                    if when == at:
+                        step()
+
+        collect(keys, [k_s[r, i, :, cols] for r in range(seq_size)], patch, text)
+        collect(values, [v_s[r, i, :, cols] for r in range(seq_size)], patch, text)
+        by_head(text_keys, keys[edge:], lane, heads, False)
+        by_head(text_values, values[edge:, :width], lane, heads, True)
+        q = q_s[i, :, cols]
+        text_bias = jnp.concatenate([bias_ref[i]] * heads, axis=1)
+
+        def scores_of(h):
+            return mm_t(jnp.where(lane == h, q, jnp.zeros_like(q)), keys[:edge])
+
+        text_scores = mm_t(q, text_keys[...]) + text_bias
+        scores = scores_of(0)
+        text_powers, mixed, total, tops = [], None, None, None
+        for h in range(heads):
+            following = scores_of(h + 1) if h + 1 < heads else None
+            text_head = text_scores[:, h * span : (h + 1) * span]
+            top = jnp.maximum(jnp.max(scores, axis=1, keepdims=True), jnp.max(text_head, axis=1, keepdims=True))
+            powers = jnp.exp2(scores - top).astype(bf16)
+            text_powers.append(jnp.exp2(text_head - top).astype(bf16))
+            both = mm(powers, values[:edge])
+            mixed = both[:, :width] if mixed is None else jnp.where(lane == h, both[:, :width], mixed)
+            total = both[:, width:] if total is None else jnp.where(lane == h, both[:, width:], total)
+            tops = jnp.broadcast_to(top, mixed.shape) if tops is None else jnp.where(lane == h, top, tops)
+            scores = following
+        both = mm(jnp.concatenate(text_powers, axis=1), text_values[...])
+        total = total + both[:, width:]
+        out = (mixed + both[:, :width]) * (1.0 / total)
+        high = out.astype(bf16)
+
+        @pl.when(turn > 1)
+        def _():
+            for copy in turn_copies(slot, i, cols):
+                copy.wait()
+
+        out_s[slot] = high
+        rest_s[slot] = (out - high.astype(f32)).astype(bf16)
+        log_s[slot] = tops + jnp.log2(total)
+        for copy in turn_copies(slot, i, cols):
+            copy.start()
+        return 0
+
+    lax.fori_loop(0, last + 1, attend, 0)
+    for when, step in agenda:
+        if when > last:
+            step()
+    move_a.finish()
+    move_b.finish()
+    for slot in range(2):
+        for copy in turn_copies(slot, 0, pl.ds(0, width)):
+            copy.wait()
     for copy in sends:
-        copy.wait()
+        copy.wait_send()
     for i in range(items):
-        for r in range(1, seq_size):
-            for n, (ref, dst) in enumerate(((k_s, k_outs), (v_s, v_outs))):
-                at = (2 * i + n) * seq_size + r
-                outs.append(pltpu.make_async_copy(ref.at[r, i], dst[r].at[i], kv_out_sem.at[at]))
-                outs[-1].start()
-    early.finish()
-    line.result_copy().wait()
+        for copy in kv_out_copies(i):
+            copy.wait()
     for copy in w_copies + outs:
         copy.wait()
 
 
-def front(in_weight, vectors, up_weight, up_bias, out_weight, down_weight, patches, text_rows, lengths, text, width,
-          devices, seq_size):
+def forward(in_weight, vectors, up_weight, up_bias, out_weight, down_weight, patches, text_rows, lengths, text, width,
+            head, devices, seq_size):
     items, patch, model = patches.shape
-    depth = devices // 8
+    depth, heads = devices // 8, width // head
     rows, cols = in_weight.shape
-    shape_a = (rows, up_weight.shape[1] + model)
-    shape_b = (down_weight.shape[0], model + LANES)
+    shape_a = (depth, 2, 2, 2, rows, up_weight.shape[1] + model)
+    shape_b = (depth, 2, 2, 2, down_weight.shape[0], model + LANES)
     shape_w = (depth, 2, 2, 2, rows, cols // 2 + LANES)
     shape_w2 = (depth, 2, 2, 2, rows, cols // 2)
     shape_x = (items, patch + text, model)
     tail = round_up(seq_size * text, LANES)
+    span = seq_size * patch + tail
     tokens = jax.ShapeDtypeStruct(shape_x, bf16)
     sems = pltpu.SemaphoreType.DMA
     outs = pl.pallas_call(
-        functools.partial(front_kernel, seq_size, text, width),
+        functools.partial(forward_kernel, seq_size, text, width, head),
         in_specs=[WHOLE] * 13 + [ANY, WHOLE, pl.BlockSpec(memory_space=pltpu.SMEM)],
-        out_specs=[ANY, ANY, WHOLE, WHOLE, ANY, ANY, WHOLE] + [ANY] * (2 + 2 * seq_size),
+        out_specs=[ANY, ANY, WHOLE, WHOLE, ANY, ANY, WHOLE] + [ANY] * (5 + 2 * seq_size),
         out_shape=[
             jax.ShapeDtypeStruct(shape_w, bf16),
             jax.ShapeDtypeStruct(shape_w2, bf16),
             jax.ShapeDtypeStruct((LANES, model), f32),
             jax.ShapeDtypeStruct((items, 1, tail), f32),
-            jax.ShapeDtypeStruct((2, depth) + shape_a, bf16),
-            jax.ShapeDtypeStruct((depth,) + shape_b, bf16),
+            jax.ShapeDtypeStruct(shape_a, bf16),
+            jax.ShapeDtypeStruct(shape_b, bf16),
             jax.ShapeDtypeStruct((items, text, model), bf16),
             tokens,
             tokens,
+            tokens,
+            tokens,
+            jax.ShapeDtypeStruct(shape_x, f32),
         ]
         + [tokens] * (2 * seq_size),
         scratch_shapes=[
-            pltpu.VMEM((rows, cols // 2 + LANES), bf16),
-            pltpu.VMEM((rows, cols // 2), bf16),
+            pltpu.VMEM(shape_w[4:], bf16),
+            pltpu.VMEM(shape_w2[4:], bf16),
+            pltpu.VMEM(shape_a[4:], bf16),
+            pltpu.VMEM(shape_b[4:], bf16),
+            pltpu.VMEM(shape_w, bf16),
+            pltpu.VMEM(shape_w2, bf16),
             pltpu.VMEM(shape_a, bf16),
             pltpu.VMEM(shape_b, bf16),
-            pltpu.VMEM(shape_w, bf16),
-            pltpu.VMEM(shape_w2, bf16),
-            pltpu.VMEM((2, depth) + shape_a, bf16),
-            pltpu.VMEM((depth,) + shape_b, bf16),
             pltpu.VMEM(patches.shape, bf16),
             pltpu.VMEM(shape_x, f32),
             pltpu.VMEM(shape_x, bf16),
             pltpu.VMEM(shape_x, bf16),
             pltpu.VMEM((seq_size,) + shape_x, bf16),
             pltpu.VMEM((seq_size,) + shape_x, bf16),
-        ]
-        + spread_sems(depth) * 2
-        + early_sems(depth)
-        + line_sems(depth)
-        + [sems((items,)), sems((2,)), sems((4, items))]
-        + [sems((4 * items * seq_size,))] * 2
-        + [sems((2 * items * seq_size,))],
-        compiler_params=compiler_params(collective_id=0, has_side_effects=True),
-        name="front",
-    )(in_weight, *vectors, up_weight, up_bias, out_weight, down_weight, patches, text_rows, lengths)
-    weights = [full.reshape(model, full.shape[-1]) for full in outs[:2]]
-    return weights, *outs[2:4], outs[4:6], *outs[6:9], outs[9 : 9 + seq_size], outs[9 + seq_size :]
-
-
-def collect(dst, refs, patch, text):
-    count, width = len(refs), refs[0].shape[2]
-    for r, ref in enumerate(refs):
-        dst[r * patch : (r + 1) * patch, :width] = ref[0, :patch, :]
-        at = count * patch + r * text
-        dst[at : at + text, :width] = ref[0, patch:, :]
-    filled = count * (patch + text)
-    if dst.shape[0] > filled:
-        dst[filled:, :width] = jnp.zeros((dst.shape[0] - filled, width), dst.dtype)
-
-
-def by_head(dst, src, lane, heads, ones):
-    count, width = src.shape
-    for h in range(heads):
-        rows = slice(h * count, (h + 1) * count)
-        dst[rows, :width] = jnp.where(lane == h, src, jnp.zeros_like(src))
-        if ones:
-            dst[rows, width:] = jnp.where(lane == h, jnp.ones_like(src), jnp.zeros_like(src))
-
-
-def attend_kernel(count, patch, head, seq_size, *refs):
-    q_ref, k_refs, v_refs = refs[0], refs[1 : 1 + count], refs[1 + count : 1 + 2 * count]
-    bias_ref, quads_a, line_b, out_ref, rest_ref, log_ref, full_a, full_b = refs[1 + 2 * count : 9 + 2 * count]
-    keys, values, text_keys, text_values, into_a, into_b, *sems = refs[9 + 2 * count :]
-    width = q_ref.shape[2]
-    text, edge = q_ref.shape[1] - patch, count * patch
-    heads, span = width // head, keys.shape[0] - edge
-    place = Place(full_a.shape[0], seq_size)
-    turn = pl.program_id(0) * pl.num_programs(1) + pl.program_id(1)
-    last = pl.num_programs(0) * pl.num_programs(1) - 1
-    move_a, move_b = Late(place, quads_a, into_a, full_a, *sems[:4]), LateLine(place, line_b, into_b, full_b, *sems[4:])
-
-    @pl.when(turn == 0)
-    def _():
-        place.greet()
-        move_a.start()
-        move_b.start()
-
-    agenda = (
-        (1, place.meet),
-        (1, move_b.send),
-        (1, move_a.send),
-        (5, move_b.forward_first),
-        (6, functools.partial(move_b.forward_second, 0)),
-        (6, functools.partial(move_b.land, 0)),
-        (7, functools.partial(move_a.land, 0)),
-        (7, functools.partial(move_a.land, 1)),
-        (8, functools.partial(move_a.forward, 0)),
-        (8, functools.partial(move_a.forward, 1)),
-        (9, functools.partial(move_b.land, 1)),
-        (9, functools.partial(move_b.land, 2)),
-        (10, functools.partial(move_a.land, 2)),
-        (10, functools.partial(move_a.land, 3)),
-        (10, functools.partial(move_b.forward_second, 1)),
-    )
-    for at in sorted({at for at, _ in agenda}):
-
-        @pl.when(turn == at)
-        def _(at=at):
-            for when, step in agenda:
-                if when == at:
-                    step()
-
-    collect(keys, k_refs, patch, text)
-    collect(values, v_refs, patch, text)
-    values[:, width:] = jnp.ones((values.shape[0], values.shape[1] - width), bf16)
-    lane = lax.broadcasted_iota(jnp.int32, (1, width), 1) // head
-    by_head(text_keys, keys[edge:], lane, heads, False)
-    by_head(text_values, values[edge:, :width], lane, heads, True)
-    q = q_ref[0]
-    text_bias = jnp.concatenate([bias_ref[0]] * heads, axis=1)
-
-    def scores_of(h):
-        return mm_t(jnp.where(lane == h, q, jnp.zeros_like(q)), keys[:edge])
-
-    text_scores = mm_t(q, text_keys[...]) + text_bias
-    scores = scores_of(0)
-    text_powers, mixed, total, tops = [], None, None, None
-    for h in range(heads):
-        following = scores_of(h + 1) if h + 1 < heads else None
-        text_head = text_scores[:, h * span : (h + 1) * span]
-        top = jnp.maximum(jnp.max(scores, axis=1, keepdims=True), jnp.max(text_head, axis=1, keepdims=True))
-        powers = jnp.exp2(scores - top).astype(bf16)
-        text_powers.append(jnp.exp2(text_head - top).astype(bf16))
-        both = mm(powers, values[:edge])
-        mixed = both[:, :width] if mixed is None else jnp.where(lane == h, both[:, :width], mixed)
-        total = both[:, width:] if total is None else jnp.where(lane == h, both[:, width:], total)
-        tops = jnp.broadcast_to(top, mixed.shape) if tops is None else jnp.where(lane == h, top, tops)
-        scores = following
-    both = mm(jnp.concatenate(text_powers, axis=1), text_values[...])
-    total = total + both[:, width:]
-    out = (mixed + both[:, :width]) * (1.0 / total)
-    high = out.astype(bf16)
-    out_ref[0] = high
-    rest_ref[0] = (out - high.astype(f32)).astype(bf16)
-    log_ref[0] = tops + jnp.log2(total)
-
-    @pl.when(turn == last)
-    def _():
-        move_b.land(3)
-        move_a.finish()
-        move_b.finish()
-
-
-def attend(q, keys, values, bias, halfway, patch, head, width, devices, seq_size):
-    items, _, model = q.shape
-    count, tail = len(keys), bias.shape[-1]
-    depth, heads, span = devices // 8, width // head, count * patch + tail
-    block = pl.BlockSpec((1, q.shape[1], width), lambda i, p: (i, 0, p))
-    outs = pl.pallas_call(
-        functools.partial(attend_kernel, count, patch, head, seq_size),
-        grid=(items, model // width),
-        in_specs=[block] * (1 + 2 * count) + [pl.BlockSpec((1, 1, tail), lambda i, p: (i, 0, 0))] + [ANY] * 2,
-        out_specs=[block, block, block, ANY, ANY],
-        out_shape=[jax.ShapeDtypeStruct(q.shape, bf16)] * 2
-        + [jax.ShapeDtypeStruct(q.shape, f32)]
-        + [jax.ShapeDtypeStruct((depth, 2, 2, 2) + part.shape[-2:], part.dtype) for part in halfway],
-        scratch_shapes=[
             pltpu.VMEM((span, width), bf16),
             pltpu.VMEM((span, 2 * width), bf16),
             pltpu.VMEM((heads * tail, width), bf16),
             pltpu.VMEM((heads * tail, 2 * width), bf16),
+            pltpu.VMEM((2, patch + text, width), bf16),
+            pltpu.VMEM((2, patch + text, width), bf16),
+            pltpu.VMEM((2, patch + text, width), f32),
         ]
-        + [pltpu.VMEM((depth, 2, 2, 2) + part.shape[-2:], part.dtype) for part in halfway]
-        + late_sems()
-        + late_line_sems(),
-        compiler_params=compiler_params(collective_id=1, has_side_effects=True),
-        name="attend",
-    )(q, *keys, *values, bias, *halfway)
-    return outs[0], outs[1], outs[2], [full.reshape(-1, full.shape[-1]) for full in outs[3:]]
-
-
-def ffn_kernel(steps, chunk, seq_ref, x_ref, xtext_ref, at_ref, dy_ref, dy_slot_ref, w_any, wd_any, vec_ref,
+        + spread_sems(depth) * 2
+        + gather_sems(depth) * 2
+        + [sems((items,)), sems((2,)), sems((4, items))]
+        + [sems((4 * items * seq_size,))] * 2
+        + [sems((2 * items * seq_size,)), sems((2, 3))],
+        compiler_params=compiler_params(collective_id=0, has_side_effects=True),
+        name="forward",
+    )(in_weight, *vectors, up_weight, up_bias, out_weight, down_weight, patches, text_rows, lengths)
+    w_in, weights = ([full.reshape(-1, full.shape[-1]) for full in pair] for pair in (outs[:2], outs[4:6]))
+    return w_in, *outs[2:4], weights, *outs[6:12], outs[12 : 12 + seq_size], outs[12 + seq_size :]
+
+
+def ffn_kernel(steps, chunk, part, seq_ref, x_ref, xtext_ref, at_ref, dy_ref, dy_slot_ref, w_any, wd_any, vec_ref,
                res_ref, restext_ref, gb_ref, ga_ref, part_out, down_out,
-               w_ref, wd_ref, part_ref, down_ref, second_s, hidden_s, pre_s, dy_s, sums_s, bias_s, out_s, dots_s,
+               w_ref, wd_ref, part_ref, down_ref, second_s, hidden_s, pre_s, dy_s, sums_s, bias_s, out_s,
                w_sem, wd_sem, part_sem, down_sem):
     step = pl.program_id(0)
     patch, model = x_ref.shape[1:]
@@ -876,28 +749,30 @@
     scaled, inverse = norm_rows(middle)
     second_in = (scaled * gain + vec_ref[SHIFT2 : SHIFT2 + 1]).astype(bf16)
     second_s[rows, :] = second_in
-    dots_s[0] = middle + vec_ref[DOWNB : DOWNB + 1]
-    dots_s[1] = jnp.zeros_like(middle)
-
-    def part(c, _):
-        cols = pl.ds(pl.multiple_of(c * chunk, chunk), chunk)
-
-        @pl.when(step == 0)
-        def _():
-            for copy in fetch(cols, c):
+    @pl.when(step == 0)
+    def _():
+        for c in range(chunks):
+            for copy in fetch(pl.ds(c * chunk, chunk), c):
                 copy.wait()
 
-        value, slope = gelu_both(mm(second_in, w_ref[:, cols]) + bias_s[:1, cols])
+    def first_dots(c):
+        cols = slice(c * part, (c + 1) * part)
+        return mm(second_in, w_ref[:, cols]) + bias_s[:1, cols], mm_t(dy, wd_ref[cols, :model])
+
+    result, grad_second = middle + vec_ref[DOWNB : DOWNB + 1], None
+    pre, grad_hidden = first_dots(0)
+    for c in range(units // part):
+        following = first_dots(c + 1) if c + 1 < units // part else (None, None)
+        cols = slice(c * part, (c + 1) * part)
+        value, slope = gelu_both(pre)
         hidden = value.astype(bf16)
         hidden_s[rows, cols] = hidden
-        grad_pre = (mm_t(dy, wd_ref[cols, :model]) * slope).astype(bf16)
+        grad_pre = (grad_hidden * slope).astype(bf16)
         pre_s[rows, cols] = grad_pre
-        dots_s[0] += mm(hidden, wd_ref[cols, :model])
-        dots_s[1] += mm_t(grad_pre, w_ref[:, cols])
-        return 0
-
-    lax.fori_loop(0, units // chunk, part, 0)
-    result, grad_second = dots_s[0], dots_s[1]
+        result = result + mm(hidden, wd_ref[cols, :model])
+        back_part = mm_t(grad_pre, w_ref[:, cols])
+        grad_second = back_part if grad_second is None else grad_second + back_part
+        pre, grad_hidden = following
     result = result.astype(bf16)
     res_ref[0] = result[:patch]
     restext_ref[0] = result[patch:]
@@ -951,7 +826,7 @@
         return jax.ShapeDtypeStruct((items, count, model), bf16)
 
     return pl.pallas_call(
-        functools.partial(ffn_kernel, items, 1024),
+        functools.partial(ffn_kernel, items, 1024, 256),
         grid=(items,),
         in_specs=[pl.BlockSpec(memory_space=pltpu.SMEM)]
         + [item(patch), item(text), item(rows), item(patch), item(slots)]
@@ -974,7 +849,6 @@
             pltpu.VMEM((8, model), f32),
             pltpu.VMEM((8, units), f32),
             pltpu.VMEM((model, model), f32),
-            pltpu.VMEM((2, rows, model), f32),
         ]
         + [pltpu.SemaphoreType.DMA((units // 1024 + 1,))] * 2
         + [pltpu.SemaphoreType.DMA((units // model + 1,))] * 2,
@@ -1088,9 +962,9 @@
         upb_out[...] = total[:, model:]
 
     tail_at = last + 1
-    agenda = [(2, sums_a.to_second), (3, sums_b.to_second), (5, sums_a.to_first), (7, sums_b.to_first),
-              (8, sums_a.to_line), (9, sums_b.to_line), (11, finish_a), (tail_at + 1, finish_b)]
-    turns_in = ((9, 10, 11, tail_at + 1), (11, tail_at, tail_at + 1, tail_at + 2))
+    agenda = [(2, sums_a.to_second), (3, sums_b.to_second), (6, sums_a.to_first), (7, sums_b.to_first),
+              (9, sums_a.to_line), (10, sums_b.to_line), (tail_at, finish_a), (tail_at + 2, finish_b)]
+    turns_in = ((9, 11, tail_at, tail_at + 1), (11, tail_at, tail_at + 1, tail_at + 2))
     for chunk, turns in enumerate(turns_in):
         steps = (sums_in[chunk].to_second, sums_in[chunk].to_first, sums_in[chunk].to_line)
         steps += (functools.partial(finish_in, chunk),)
@@ -1105,8 +979,8 @@
             copy.start()
         sums_s[...] = jnp.zeros_like(sums_s)
 
-    collect(keys, k_refs, patch, text)
-    collect(values, v_refs, patch, text)
+    collect(keys, [ref[0] for ref in k_refs], patch, text)
+    collect(values, [ref[0] for ref in v_refs], patch, text)
     q, grad = q_ref[0], grad_ref[0]
     edge, heads, span = count * patch, width // head, keys.shape[0] - count * patch
     lane = lax.broadcasted_iota(jnp.int32, (1, width), 1) // head
@@ -1337,40 +1211,47 @@
 
 
 def outputs_kernel(*refs):
-    text_ref, patch_grad, text_grad, total_a, total_b, total_in, vec1, vec2, upb = refs[:9]
-    outs = list(refs[9:])
-    out_text, grad_patches, grad_text = outs[:3]
+    text_any, patch_any, text_grad_any, total_a, total_b, total_in, vec1, vec2, upb = refs[:9]
+    outs = list(refs[9:25])
+    out_text, patch_out, grad_text = outs[:3]
     first_gain, first_shift, in_weight, query_bias, value_bias, out_weight, branch_bias = outs[3:10]
     second_gain, second_shift, up_weight, up_bias, down_weight, down_bias = outs[10:]
-    slots, units = out_text.shape[1], up_weight.shape[1]
-    out_text[...] = text_ref[:, :slots]
-    grad_text[...] = text_grad[:, :slots]
-    grad_patches[...] = patch_grad[...]
-
-    def row_of(ref, at):
-        count = ref.shape[0]
-        tall = jnp.concatenate([ref[...], jnp.zeros((LANES - count, LANES), f32)], axis=0)
-        return jnp.transpose(tall)[at, :count]
-
-    @pl.when(pl.program_id(0) == 0)
-    def _():
-        in_weight[...] = total_in[...]
-        out_weight[...] = total_a[:, units:]
-        up_weight[...] = total_a[:, :units]
-        down_weight[...] = total_b[...]
-        for ref, at in ((first_gain, GAIN1), (first_shift, SHIFT1), (query_bias, QBIAS), (value_bias, VBIAS)):
-            ref[...] = row_of(vec1, at)
-        for ref, at in ((branch_bias, BRANCH), (second_gain, GAIN2), (second_shift, SHIFT2), (down_bias, DOWNB)):
-            ref[...] = row_of(vec2, at)
-        up_bias[...] = row_of(upb, 0)
+    patch_s, text_s, text_grad_s, sem = refs[25:]
+    items, slots, units = patch_s.shape[0], out_text.shape[1], up_weight.shape[1]
+    fetches = [pltpu.make_async_copy(patch_any.at[i], patch_s.at[i], sem.at[0, i]) for i in range(items)]
+    stores = [pltpu.make_async_copy(patch_s.at[i], patch_out.at[i], sem.at[1, i]) for i in range(items)]
+    texts = [
+        pltpu.make_async_copy(text_any, text_s, sem.at[2, 0]),
+        pltpu.make_async_copy(text_grad_any, text_grad_s, sem.at[2, 1]),
+    ]
+    for copy in fetches + texts:
+        copy.start()
+
+    count, wide = vec1.shape[0], upb.shape[0]
+    empty = jnp.zeros((LANES - 2 * count - wide, LANES), f32)
+    table = jnp.transpose(jnp.concatenate([upb[...], vec1[...], vec2[...], empty], axis=0))
+    in_weight[...] = total_in[...]
+    out_weight[...] = total_a[:, units:]
+    up_weight[...] = total_a[:, :units]
+    down_weight[...] = total_b[...]
+    for ref, at in ((first_gain, GAIN1), (first_shift, SHIFT1), (query_bias, QBIAS), (value_bias, VBIAS)):
+        ref[...] = table[at, wide : wide + count]
+    for ref, at in ((branch_bias, BRANCH), (second_gain, GAIN2), (second_shift, SHIFT2), (down_bias, DOWNB)):
+        ref[...] = table[at, wide + count : wide + 2 * count]
+    up_bias[...] = table[0, :wide]
+    for fetch, store in zip(fetches, stores):
+        fetch.wait()
+        store.start()
+    for copy in texts:
+        copy.wait()
+    out_text[...] = text_s[:, :slots]
+    grad_text[...] = text_grad_s[:, :slots]
+    for copy in stores:
+        copy.wait()
 
 
 def outputs(text, patch_grad, text_grad, total_a, total_b, total_in, vec1, vec2, upb, slots, units):
     items, patch, model = patch_grad.shape
-    padded = text.shape[1]
-
-    def item(count):
-        return pl.BlockSpec((1, count, model), lambda i: (i, 0, 0))
 
     def shape(*dims):
         return jax.ShapeDtypeStruct(dims, f32)
@@ -1379,12 +1260,17 @@
     vector, texts = shape(count), jax.ShapeDtypeStruct((items, slots, model), bf16)
     return pl.pallas_call(
         outputs_kernel,
-        grid=(items,),
-        in_specs=[item(padded), item(patch), item(padded)] + [WHOLE] * 6,
-        out_specs=[item(slots), item(patch), item(slots)] + [WHOLE] * 13,
+        in_specs=[ANY] * 3 + [WHOLE] * 6,
+        out_specs=[WHOLE, ANY, WHOLE] + [WHOLE] * 13,
         out_shape=[texts, jax.ShapeDtypeStruct(patch_grad.shape, bf16), texts]
         + [vector, vector, shape(count, 3 * model), vector, vector, shape(count, model), vector, vector, vector]
         + [shape(count, units), shape(upb.shape[0]), shape(*total_b.shape), vector],
+        scratch_shapes=[
+            pltpu.VMEM(patch_grad.shape, bf16),
+            pltpu.VMEM(text.shape, bf16),
+            pltpu.VMEM(text.shape, bf16),
+            pltpu.SemaphoreType.DMA((3, max(items, 2))),
+        ],
         compiler_params=compiler_params(),
         name="outputs",
     )(text, patch_grad, text_grad, total_a, total_b, total_in, vec1, vec2, upb)
@@ -1420,12 +1306,9 @@
     text = round_up(-(-slots // seq_size), ROW_TILE)
     seq = lax.axis_index("seq")
     vectors = [first_gain, first_shift, query_bias, value_bias, branch_bias, second_gain, second_shift, down_bias]
-    w_in, vecs, bias, halfway, x_text, first_in, q, keys, values = front(
-        in_weight, vectors, up_weight, up_bias, out_weight, down_weight, patches, text_rows, lengths, text, width,
+    w_in, vecs, bias, (weights, w_down), x_text, first_in, q, attended, rest, logs, keys, values = forward(
+        in_weight, vectors, up_weight, up_bias, out_weight, down_weight, patches, text_rows, lengths, text, width, head,
         devices, seq_size
-    )
-    attended, rest, logs, (weights, w_down) = attend(
-        q, keys, values, bias, halfway, patch, head, width, devices, seq_size
     )
     out_patches, res_text, grad_branch, grad_att, part_a, part_b = ffn(
         seq[None], patches, x_text, attended, patch_cotangent, text_cotangent, weights, w_down, vecs

time: 179 us -> 171 us (0.955)
  Pallas kernels: 178 us -> 169 us
    pallas_call x4 -> x3, Pallas kernels: 105 us -> 96.7 us  [the longest x1 55.3 us: forward(): pl.pallas_call(functools.partial(forward_kernel, seq_size, text, width, h...]
where the time goes in v6:
time: 171 us; the launch traced here: 170 us
  Pallas kernels  169 us (99%)
    pallas_call x1, Pallas kernels, back(): pl.pallas_call(functools.partial(back_kernel, count, patch, head, seq_siz...  72.7 us
    pallas_call x1, Pallas kernels, forward(): pl.pallas_call(functools.partial(forward_kernel, seq_size, text, width, h...  55.3 us
    pallas_call x1, Pallas kernels, ffn(): pl.pallas_call(functools.partial(ffn_kernel, items, 1024, 256), grid=(ite...  37.1 us
    pallas_call x1, Pallas kernels, outputs(): pl.pallas_call(outputs_kernel, in_specs=[ANY] * 3 + [WHOLE] * 6, out_spec...  4.26 us

profile of v6, /device:TPU:0, one launch (start us, length us, event | category | flops | bytes accessed | tf_op | source)
XLA Modules:
  0.0 170.3 jit_solution(9066751462658293413)
XLA Ops:
  0.7 55.3 %forward.1 = (bf16[4,2,2,2,16,896]{5,4,3,2,1,0:T(8,128)(2,1)}, bf16[4,2,2,2,16,768]{5,4,3,2,1,0:T(8,128)(2,1)}, f32[128,512]{1,0:T(8,128)}, f32[3,1,128]{2,1,0:T...) custom-call(bf16[16,1536]{1,0:T(8,128)(2,1)} %refs_0_.1, ...), custom_call_target="tpu_custom_call" | custom-call | tf_op jit(solution)/shard_map/forward/pallas_call | solution.py:654
  56.0 37.1 %ffn.1 = (bf16[3,512,512]{2,1,0:T(8,128)(2,1)}, bf16[3,48,512]{2,1,0:T(8,128)(2,1)}, bf16[3,560,512]{2,1,0:T(8,128)(2,1)}, bf16[3,560,512]{2,1,0:T(8,128)(2,1)},...) custom-call(s32[1]{0:T(128)} %bitcast.seq_ref, bf16[3,512,512]{2,1,0:T(8,128)(2,1)} %refs_16_.1, ...), custom_call_target="tpu_custom_call" | custom-call | tf_op jit(solution)/shard_map/ffn/pallas_call | solution.py:828
  93.1 72.7 %back.1 = (bf16[3,512,512]{2,1,0:T(8,128)(2,1)}, bf16[3,96,512]{2,1,0:T(8,128)(2,1)}, bf16[3,96,512]{2,1,0:T(8,128)(2,1)}, f32[16,2560]{1,0:T(8,128)}, f32[64,51...) custom-call(bf16[3,560,512]{2,1,0:T(8,128)(2,1)} %get-tuple-element.70.refs_0_,, ...), custom_call_target="tpu_custom_call" | custom-call | tf_op jit(solution)/shard_map/back/pallas_call | solution.py:1152
  165.8 4.3 %outputs.1 = (bf16[3,77,512]{2,1,0:T(8,128)(2,1)}, bf16[3,512,512]{2,1,0:T(8,128)(2,1)}, bf16[3,77,512]{2,1,0:T(8,128)(2,1)}, f32[16]{0:T(128)}, f32[16]{0:T(128...) custom-call(bf16[3,96,512]{2,1,0:T(8,128)(2,1)} %get-tuple-element.8, ...), custom_call_target="tpu_custom_call" | custom-call | tf_op jit(solution)/shard_map/outputs/pallas_call | solution.py:1261

commit v7 on v6

--- a/solution.py
+++ b/solution.py
@@ -411,23 +411,27 @@
         del refs[:number]
         return taken
 
-    (shard_ref,), vec_refs = take(1), take(8)
-    up_ref, up_bias_ref, out_w_ref, down_ref, x_any, slot_ref, length_ref = take(7)
+    given, x_any, length_ref = take(14), *take(2)
     w_out, w2_out, vecs, bias_ref, full_a, full_b, xtext_ref, first_out, q_out, out_out, rest_out, log_out = take(12)
     k_outs, v_outs = take(seq_size), take(seq_size)
     shard, shard2, shard_a, shard_b, w_full, w2_full, into_a, into_b, x_s, n_s, first_s, q_s, k_s, v_s = take(14)
     keys, values, text_keys, text_values, out_s, rest_s, log_s = take(7)
     sems, sems2, sems_a, sems_b = take(3), take(3), take(4), take(4)
     x_sem, w_sem, out_sem, kv_sem, kv_in_sem, kv_out_sem, turn_sem = take(7)
+    held, given_sem = take(14), *take(1)
+    fetches = [pltpu.make_async_copy(src, dst, given_sem.at[n]) for n, (src, dst) in enumerate(zip(given, held))]
+    (shard_ref,), vec_refs, (up_ref, up_bias_ref, out_w_ref, down_ref, slot_ref) = held[:1], held[1:9], held[9:]
     items, patch, model = x_s.shape
     units, wide = up_ref.shape[1], shard2.shape[1]
     pairs = model // width
     place = Place(w_full.shape[0], seq_size)
     seq = lax.axis_index("seq")
     x_copies = [pltpu.make_async_copy(x_any.at[i], x_s.at[i], x_sem.at[i]) for i in range(items)]
-    for copy in x_copies:
+    place.greet()
+    for copy in fetches + x_copies:
         copy.start()
-    place.greet()
+    for copy in fetches[:9]:
+        copy.wait()
     for half, to in enumerate((shard, shard2)):
         for n in range(3):
             at = (n + 1) % 3 * model + half * (model // 2)
@@ -437,6 +441,8 @@
     halves = [Spread(place, shard, w_full, *sems), Spread(place, shard2, w2_full, *sems2)]
     for move in halves:
         move.start()
+    for copy in fetches[9:]:
+        copy.wait()
     shard_a[:, :units] = up_ref[...]
     shard_a[:, units:] = out_w_ref[...]
     shard_b[:, :model] = down_ref[...]
@@ -545,19 +551,19 @@
             copy.start()
 
     agenda = (
-        (3, move_a.forward_first),
-        (3, functools.partial(move_a.forward_second, 0)),
-        (5, move_b.forward_first),
-        (5, functools.partial(move_b.forward_second, 0)),
-        (7, functools.partial(move_a.land, 0)),
-        (7, functools.partial(move_a.land, 1)),
-        (8, functools.partial(move_a.forward_second, 1)),
-        (9, functools.partial(move_a.land, 2)),
-        (9, functools.partial(move_b.land, 0)),
-        (9, functools.partial(move_b.land, 1)),
-        (10, functools.partial(move_b.forward_second, 1)),
-        (10, functools.partial(move_b.land, 2)),
-        (11, functools.partial(move_a.land, 3)),
+        (4, move_a.forward_first),
+        (4, functools.partial(move_a.forward_second, 0)),
+        (6, move_b.forward_first),
+        (6, functools.partial(move_b.forward_second, 0)),
+        (8, functools.partial(move_a.land, 0)),
+        (8, functools.partial(move_a.land, 1)),
+        (9, functools.partial(move_a.forward_second, 1)),
+        (10, functools.partial(move_a.land, 2)),
+        (10, functools.partial(move_b.land, 0)),
+        (10, functools.partial(move_b.land, 1)),
+        (11, functools.partial(move_b.forward_second, 1)),
+        (11, functools.partial(move_b.land, 2)),
+        (13, functools.partial(move_a.land, 3)),
         (13, functools.partial(move_b.land, 3)),
     )
 
@@ -651,9 +657,10 @@
     span = seq_size * patch + tail
     tokens = jax.ShapeDtypeStruct(shape_x, bf16)
     sems = pltpu.SemaphoreType.DMA
+    given = (in_weight, *vectors, up_weight, up_bias, out_weight, down_weight, text_rows)
     outs = pl.pallas_call(
         functools.partial(forward_kernel, seq_size, text, width, head),
-        in_specs=[WHOLE] * 13 + [ANY, WHOLE, pl.BlockSpec(memory_space=pltpu.SMEM)],
+        in_specs=[ANY] * 15 + [pl.BlockSpec(memory_space=pltpu.SMEM)],
         out_specs=[ANY, ANY, WHOLE, WHOLE, ANY, ANY, WHOLE] + [ANY] * (5 + 2 * seq_size),
         out_shape=[
             jax.ShapeDtypeStruct(shape_w, bf16),
@@ -697,17 +704,19 @@
         + gather_sems(depth) * 2
         + [sems((items,)), sems((2,)), sems((4, items))]
         + [sems((4 * items * seq_size,))] * 2
-        + [sems((2 * items * seq_size,)), sems((2, 3))],
+        + [sems((2 * items * seq_size,)), sems((2, 3))]
+        + [pltpu.VMEM(array.shape, array.dtype) for array in given]
+        + [sems((len(given),))],
         compiler_params=compiler_params(collective_id=0, has_side_effects=True),
         name="forward",
-    )(in_weight, *vectors, up_weight, up_bias, out_weight, down_weight, patches, text_rows, lengths)
+    )(*given, patches, lengths)
     w_in, weights = ([full.reshape(-1, full.shape[-1]) for full in pair] for pair in (outs[:2], outs[4:6]))
     return w_in, *outs[2:4], weights, *outs[6:12], outs[12 : 12 + seq_size], outs[12 + seq_size :]
 
 
 def ffn_kernel(steps, chunk, part, seq_ref, x_ref, xtext_ref, at_ref, dy_ref, dy_slot_ref, w_any, wd_any, vec_ref,
                res_ref, restext_ref, gb_ref, ga_ref, part_out, down_out,
-               w_ref, wd_ref, part_ref, down_ref, second_s, hidden_s, pre_s, dy_s, sums_s, bias_s, out_s,
+               w_ref, wd_ref, part_ref, down_ref, second_s, hidden_s, pre_s, dy_s, sums_s, bias_s, at_s, gb_s,
                w_sem, wd_sem, part_sem, down_sem):
     step = pl.program_id(0)
     patch, model = x_ref.shape[1:]
@@ -779,16 +788,8 @@
     grad_branch = (dy.astype(f32) + norm_back(grad_second, scaled, inverse, gain)).astype(bf16)
     gb_ref[0] = grad_branch
     ga_ref[0] = mm_t(grad_branch, w_out[...]).astype(bf16)
-    out_grad = t_mm(at_ref[0], grad_branch)
-
-    @pl.when(step == 0)
-    def _():
-        out_s[...] = out_grad
-
-    @pl.when(step > 0)
-    def _():
-        out_s[...] += out_grad
-
+    at_s[rows, :] = at_ref[0]
+    gb_s[rows, :] = grad_branch
     for at, grad in ((BRANCH, grad_branch), (GAIN2, grad_second * scaled), (SHIFT2, grad_second), (DOWNB, dy)):
         sums_s[at : at + 1, :] += column_sum(grad)
 
@@ -796,7 +797,7 @@
     def _():
         groups = units // model
         copies = []
-        part_ref[:, units : units + model] = out_s[...].astype(bf16)
+        part_ref[:, units : units + model] = t_mm(at_s[...], gb_s[...]).astype(bf16)
         part_ref[:, units + model :] = to_columns(sums_s[...])
         copies.append(pltpu.make_async_copy(part_ref.at[:, units:], part_out.at[:, units:], part_sem.at[groups]))
         copies[-1].start()
@@ -848,7 +849,8 @@
             pltpu.VMEM((items * rows, model), bf16),
             pltpu.VMEM((8, model), f32),
             pltpu.VMEM((8, units), f32),
-            pltpu.VMEM((model, model), f32),
+            pltpu.VMEM((items * rows, model), bf16),
+            pltpu.VMEM((items * rows, model), bf16),
         ]
         + [pltpu.SemaphoreType.DMA((units // 1024 + 1,))] * 2
         + [pltpu.SemaphoreType.DMA((units // model + 1,))] * 2,
@@ -875,8 +877,7 @@
     first_grad_s, scaled_s, inverse_s = take(3)
     fetch_sem, dkv_sem, dkv_in_sem, text_sem, text_in_sem, patch_sem = take(6)
     scratch_a, scratch_b = take(10), take(10)
-    scratch_in = [take(11) for _ in range(2)]
-    scratch_last, scratch_vec = take(6), take(6)
+    scratch_in, scratch_last, scratch_vec = take(11), [take(6), take(6)], take(6)
 
     width, rows = q_ref.shape[2], q_ref.shape[1]
     text, model = rows - patch, pairs * width
@@ -886,8 +887,8 @@
     turn, last = p * items + i, pairs * items - 1
     sums_a, sums_b = Reduce(place, part_a, *scratch_a), Reduce(place, part_b, *scratch_b)
     chunks = ((0, pairs - 2), (pairs - 2, pairs - 1), (pairs - 1, pairs))
-    sums_in = [Reduce(place, each[0], *each[1:]) for each in scratch_in]
-    sums_in.append(ShortReduce(place, *scratch_last))
+    sums_in = [Reduce(place, *scratch_in)]
+    sums_in += [ShortReduce(place, *each) for each in scratch_last]
     sums_vec = ShortReduce(place, *scratch_vec)
     fetches = [
         pltpu.make_async_copy(src, dst, fetch_sem.at[n])
@@ -919,7 +920,7 @@
 
     def settle(of):
         slot, pair, item = lax.rem(of, 2), of // items, lax.rem(of, items)
-        total = own_s[slot]
+        total = own_s[slot].astype(f32)
         for r in range(1, seq_size):
             dkv_copy(slot, r).wait_recv()
             total = total + dkv_in[slot, r - 1].astype(f32)
@@ -938,7 +939,7 @@
             part.shape[:-1] + (3 * width,)
         )
         if pair == end - 1:
-            (sums_in[chunk].start if end == pairs else sums_in[chunk].to_core)()
+            (sums_in[chunk].start if chunk else sums_in[chunk].to_core)()
         cols = slice(pair * width, (pair + 1) * width)
         sums_s[QBIAS : QBIAS + 1, cols] = column_sum(mixed[:, :width])
         sums_s[VBIAS : VBIAS + 1, cols] = column_sum(mixed[:, 2 * width :])
@@ -964,11 +965,9 @@
     tail_at = last + 1
     agenda = [(2, sums_a.to_second), (3, sums_b.to_second), (6, sums_a.to_first), (7, sums_b.to_first),
               (9, sums_a.to_line), (10, sums_b.to_line), (tail_at, finish_a), (tail_at + 2, finish_b)]
-    turns_in = ((9, 11, tail_at, tail_at + 1), (11, tail_at, tail_at + 1, tail_at + 2))
-    for chunk, turns in enumerate(turns_in):
-        steps = (sums_in[chunk].to_second, sums_in[chunk].to_first, sums_in[chunk].to_line)
-        steps += (functools.partial(finish_in, chunk),)
-        agenda += [(max(at, items * chunks[chunk][1] + 2), step) for at, step in zip(turns, steps)]
+    steps = (sums_in[0].to_second, sums_in[0].to_first, sums_in[0].to_line, functools.partial(finish_in, 0))
+    agenda += [(max(at, items * chunks[0][1] + 2), step) for at, step in zip((9, 11, tail_at, tail_at + 1), steps)]
+    agenda += [(tail_at, sums_in[1].to_line), (tail_at + 2, functools.partial(finish_in, 1))]
     agenda += [(tail_at + 1, sums_in[2].to_line), (tail_at + 3, functools.partial(finish_in, 2))]
     agenda.sort(key=lambda entry: entry[0])
 
@@ -1016,16 +1015,16 @@
         scores, grad_probs = following
     text_probs, text_grads = jnp.concatenate(text_probs, axis=1), jnp.concatenate(text_grads, axis=1)
     dq = dq + mm(text_grads, text_keys[...])
-    dv = jnp.transpose(t_mm(jnp.concatenate(grad_heads, axis=0), probs_s[...]))
-    dk = jnp.transpose(t_mm(jnp.concatenate(q_heads, axis=0), scores_s[...])) * LN2
+    dv = jnp.transpose(t_mm(jnp.concatenate(grad_heads, axis=0), probs_s[...]).astype(bf16))
+    dk = jnp.transpose((t_mm(jnp.concatenate(q_heads, axis=0), scores_s[...]) * LN2).astype(bf16))
 
     def of_heads(wide):
         own = wide[:, :span]
         for h in range(1, heads):
             own = jnp.where(row == h, wide[:, h * span : (h + 1) * span], own)
-        return jnp.transpose(own)
-
-    text_dv, text_dk = of_heads(t_mm(grad, text_probs)), of_heads(t_mm(q, text_grads)) * LN2
+        return jnp.transpose(own.astype(bf16))
+
+    text_dv, text_dk = of_heads(t_mm(grad, text_probs)), of_heads(t_mm(q, text_grads) * LN2)
     slot = lax.rem(turn, 2)
 
     @pl.when(turn == 0)
@@ -1059,8 +1058,8 @@
     for r in range(1, seq_size):
         for n, (part, text_part) in enumerate(((dk, text_dk), (dv, text_dv))):
             cols = slice(n * width, (n + 1) * width)
-            dkv_out[slot, r - 1, :patch, cols] = part[r * patch : (r + 1) * patch].astype(bf16)
-            dkv_out[slot, r - 1, patch:, cols] = text_part[r * text : (r + 1) * text].astype(bf16)
+            dkv_out[slot, r - 1, :patch, cols] = part[r * patch : (r + 1) * patch]
+            dkv_out[slot, r - 1, patch:, cols] = text_part[r * text : (r + 1) * text]
         dkv_copy(slot, r).start()
 
     for pair in range(pairs - 1):
@@ -1145,10 +1144,9 @@
     sems = pltpu.SemaphoreType.DMA
     others = seq_size - 1
     slots = jax.ShapeDtypeStruct((items, seq_size * text, model), bf16)
-    scratch_in = []
-    for cols in (3 * (pairs - 2) * width, 3 * width):
-        scratch_in += [pltpu.VMEM((depth, 2, 2, 2, rows_a, cols), bf16)] + reduce_scratch(depth, rows_a, cols)
-    scratch_in += short_reduce_scratch(depth, rows_a, 3 * width)
+    cols = 3 * (pairs - 2) * width
+    scratch_in = [pltpu.VMEM((depth, 2, 2, 2, rows_a, cols), bf16)] + reduce_scratch(depth, rows_a, cols)
+    scratch_in += short_reduce_scratch(depth, rows_a, 3 * width) * 2
     return pl.pallas_call(
         functools.partial(back_kernel, count, patch, head, seq_size, pairs, items),
         grid=(pairs, items),
@@ -1178,7 +1176,7 @@
             pltpu.VMEM((width // head * rows, count * patch), bf16),
             pltpu.VMEM((width // head * rows, count * patch), bf16),
             pltpu.VMEM((pairs, items * rows, 3 * width), bf16),
-            pltpu.VMEM((2, rows, 2 * width), f32),
+            pltpu.VMEM((2, rows, 2 * width), bf16),
             pltpu.VMEM((2, others, rows, 2 * width), bf16),
             pltpu.VMEM((2, others, rows, 2 * width), bf16),
             pltpu.VMEM((8, model), f32),

time: 171 us -> 168 us (0.982)
  Pallas kernels: 169 us -> 167 us
    pallas_call x1, Pallas kernels: 72.7 us -> 70.9 us  [back(): pl.pallas_call(functools.partial(back_kernel, count, patch, head, seq_siz...]
where the time goes in v7:
time: 168 us; the launch traced here: 167 us
  Pallas kernels  167 us (99%)
    pallas_call x1, Pallas kernels, back(): pl.pallas_call(functools.partial(back_kernel, count, patch, head, seq_siz...  70.9 us
    pallas_call x1, Pallas kernels, forward(): pl.pallas_call(functools.partial(forward_kernel, seq_size, text, width, h...  55 us
    pallas_call x1, Pallas kernels, ffn(): pl.pallas_call(functools.partial(ffn_kernel, items, 1024, 256), grid=(ite...  36.5 us
    pallas_call x1, Pallas kernels, outputs(): pl.pallas_call(outputs_kernel, in_specs=[ANY] * 3 + [WHOLE] * 6, out_spec...  4.26 us

profile of v7, /device:TPU:0, one launch (start us, length us, event | category | flops | bytes accessed | tf_op | source)
XLA Modules:
  0.0 167.5 jit_solution(151828960489198354)
XLA Ops:
  0.7 55.0 %forward.1 = (bf16[4,2,2,2,16,896]{5,4,3,2,1,0:T(8,128)(2,1)}, bf16[4,2,2,2,16,768]{5,4,3,2,1,0:T(8,128)(2,1)}, f32[128,512]{1,0:T(8,128)}, f32[3,1,128]{2,1,0:T...) custom-call(bf16[16,1536]{1,0:T(8,128)(2,1)} %refs_0_.1, ...), custom_call_target="tpu_custom_call" | custom-call | tf_op jit(solution)/shard_map/forward/pallas_call | solution.py:661
  55.6 36.5 %ffn.1 = (bf16[3,512,512]{2,1,0:T(8,128)(2,1)}, bf16[3,48,512]{2,1,0:T(8,128)(2,1)}, bf16[3,560,512]{2,1,0:T(8,128)(2,1)}, bf16[3,560,512]{2,1,0:T(8,128)(2,1)},...) custom-call(s32[1]{0:T(128)} %bitcast.seq_ref, bf16[3,512,512]{2,1,0:T(8,128)(2,1)} %refs_16_.1, ...), custom_call_target="tpu_custom_call" | custom-call | tf_op jit(solution)/shard_map/ffn/pallas_call | solution.py:829
  92.1 70.9 %back.1 = (bf16[3,512,512]{2,1,0:T(8,128)(2,1)}, bf16[3,96,512]{2,1,0:T(8,128)(2,1)}, bf16[3,96,512]{2,1,0:T(8,128)(2,1)}, f32[16,2560]{1,0:T(8,128)}, f32[64,51...) custom-call(bf16[3,560,512]{2,1,0:T(8,128)(2,1)} %get-tuple-element.70.refs_0_,, ...), custom_call_target="tpu_custom_call" | custom-call | tf_op jit(solution)/shard_map/back/pallas_call | solution.py:1150
  163.0 4.3 %outputs.1 = (bf16[3,77,512]{2,1,0:T(8,128)(2,1)}, bf16[3,512,512]{2,1,0:T(8,128)(2,1)}, bf16[3,77,512]{2,1,0:T(8,128)(2,1)}, f32[16]{0:T(128)}, f32[16]{0:T(128...) custom-call(bf16[3,96,512]{2,1,0:T(8,128)(2,1)} %get-tuple-element.8, ...), custom_call_target="tpu_custom_call" | custom-call | tf_op jit(solution)/shard_map/outputs/pallas_call | solution.py:1259
